TPU v7x, 128 devices: a whole 4x4x4 slice. The times are simulated.
128 devices in a mesh: pipe: 2 (over x_lo), tensor: 4 (over z), dp: 16 (over y, x_hi, core).
Axes of the slice: x: 4 (x_hi: 2, x_lo: 2; x = x_hi * 2 + x_lo), y: 4, z: 4, core: 2. Of those that a mesh axis runs over, the one named last changes fastest.
Arguments:
- tokens: bfloat16 [2, 6304, 768], P(None, 'dp'), may hold values from -6 to 6
- cotangent: bfloat16 [2, 6304, 768], P(None, 'dp'), may hold values from -6 to 6
- image_counts: int32 [2, 16], replicated, may hold values from 1 to 2, 20 in all within a row
- routes: int32 [2, 6304, 2], P(None, 'dp'), may hold values from 0 to 31, all different within a row; in each aligned block of 394 rows (0 to 393, 394 to 787, ..., all dimensions but the last counted through in order) at most 30 rows name the same one
- attn_norm_gain: float32 [2, 768], P('pipe'), may hold values from 0.5 to 1.5
- query_key_value: bfloat16 [2, 768, 3, 768], P('pipe', None, None, 'tensor'), may hold values from -0.21875 to 0.21875
- attn_output: bfloat16 [2, 768, 768], P('pipe', 'tensor'), may hold values from -1.75 to 1.75
- moe_norm_gain: float32 [2, 768], P('pipe'), may hold values from 0.5 to 1.5
- router_weight: bfloat16 [2, 768, 32], P('pipe'), may hold values from -0.15917969 to 0.15917969
- expert_in: bfloat16 [2, 32, 768, 3072], P('pipe', 'dp', None, 'tensor'), may hold values from -0.21875 to 0.21875
- expert_down: bfloat16 [2, 32, 3072, 768], P('pipe', 'dp', 'tensor'), may hold values from -3 to 3
Outputs:
- section_out: bfloat16 [2, 2, 6304, 768], P('pipe', None, 'dp')
- input_grad: bfloat16 [2, 2, 6304, 768], P('pipe', None, 'dp')
- grad_attn_norm: float32 [2, 768], P('pipe')
- grad_query_key_value: float32 [2, 768, 3, 768], P('pipe', None, None, 'tensor')
- grad_attn_output: float32 [2, 768, 768], P('pipe', 'tensor')
- grad_moe_norm: float32 [2, 768], P('pipe')
- grad_router: float32 [2, 768, 32], P('pipe')
- grad_expert_in: float32 [2, 32, 768, 3072], P('pipe', 'dp', None, 'tensor')
- grad_expert_down: float32 [2, 32, 3072, 768], P('pipe', 'dp', 'tensor')
Inputs may be any that keep to these rules, and one draw needn't show every extreme that they name: `image_counts`: in each micro-batch the counts sum to 20, and some dp index holds 2 images. `routes`: each row names two different experts; in the rows of one dp index of one micro-batch no expert is named by more than 30 rows, a bound that some expert reaches in some of these blocks.
All inputs are finite; a program needn't handle non-finite values.
Results may differ from a plain program's by a relative error of at most 0.03.
Values may be sent and summed in bfloat16 or wider, within the bound.
A program may use at most 256 MiB of HBM per device.

v0:
```python
import jax
import jax.numpy as jnp
from jax import lax
from jax.sharding import PartitionSpec as P

HD = 64
IMG_LEN = 197


EPSILON = 1e-06
HIGHEST_PRECISION = lax.Precision.HIGHEST


def shifted(block, axis, distance):
    devices = range(lax.axis_size(axis))
    route = [(i - distance, i) for i in devices if i - distance in devices]
    return lax.ppermute(block, axis, route)


def layer_norm(values, gain_vector):
    average = jnp.mean(values, axis=-1, keepdims=True)
    centred = values - average
    spread = jnp.mean(centred * centred, axis=-1, keepdims=True)
    return centred * lax.rsqrt(spread + EPSILON) * gain_vector


def slot_numbers(route_ids, live_int, experts):
    matches = (route_ids[:, :, None] == jnp.arange(experts, dtype=jnp.int32)).astype(jnp.int32)
    matches = matches * live_int[:, None, None]
    matches_flat = matches.reshape(-1, experts)
    before = jnp.cumsum(matches_flat, axis=0) - matches_flat
    return jnp.sum(before * matches_flat, axis=1).reshape(route_ids.shape)


def capacity_of(row_count, experts):
    return max(2, row_count * 10 // (4 * experts))


def to_experts(outbox):
    return lax.all_to_all(outbox, "dp", split_axis=0, concat_axis=1, tiled=True)


def to_tokens(partial_value):
    summed = lax.psum(partial_value.astype(jnp.bfloat16), "tensor").astype(jnp.float32)
    return lax.all_to_all(
        summed.astype(jnp.bfloat16), "dp", split_axis=1, concat_axis=0, tiled=True
    ).astype(summed.dtype)


def attention_forward(state, gain_vector, project_shard, output_shard):
    row_count = state.shape[0]
    model_width = project_shard.shape[0]
    group_width = project_shard.shape[2]
    score_scale = HD ** (-0.5)
    normed = layer_norm(state, gain_vector).astype(jnp.bfloat16)
    projected = jnp.dot(
        normed,
        project_shard.reshape(model_width, 3 * group_width),
        preferred_element_type=jnp.float32,
    )
    projected = projected.astype(jnp.bfloat16).reshape(
        row_count // IMG_LEN, IMG_LEN, 3, group_width // HD, HD
    )
    scores = (
        jnp.einsum(
            "sihd,sjhd->shij",
            projected[:, :, 0],
            projected[:, :, 1],
            preferred_element_type=jnp.float32,
        )
        * score_scale
    )
    highest = jnp.max(scores, axis=-1, keepdims=True)
    exponent = jnp.exp(scores - highest)
    denominator = jnp.sum(exponent, axis=-1, keepdims=True)
    weights_low = (exponent / denominator).astype(jnp.bfloat16)
    log_total = highest + jnp.log(denominator)
    context = jnp.einsum(
        "shij,sjhd->sihd", weights_low, projected[:, :, 2], preferred_element_type=jnp.float32
    )
    context = context.astype(jnp.bfloat16).reshape(row_count, group_width)
    partial_value = jnp.dot(context, output_shard, preferred_element_type=jnp.float32)
    attended = lax.psum(partial_value.astype(jnp.bfloat16), "tensor").astype(jnp.float32)
    return (state + attended, (normed, projected, log_total, context))


def attention_backward(delta_one, stored, state, gain_vector, project_shard, output_shard):
    normed, projected, log_total, context = stored
    row_count = state.shape[0]
    model_width = project_shard.shape[0]
    group_width = project_shard.shape[2]
    score_scale = HD ** (-0.5)
    delta_attn = delta_one.astype(jnp.bfloat16)
    grad_output = jnp.einsum("tc,td->cd", context, delta_attn, preferred_element_type=jnp.float32)
    delta_context = jnp.einsum(
        "td,cd->tc", delta_attn, output_shard, preferred_element_type=jnp.float32
    )
    delta_context = delta_context.astype(jnp.bfloat16).reshape(
        row_count // IMG_LEN, IMG_LEN, group_width // HD, HD
    )
    queries = projected[:, :, 0]
    keys_block = projected[:, :, 1]
    values_block = projected[:, :, 2]
    scores = (
        jnp.einsum("sihd,sjhd->shij", queries, keys_block, preferred_element_type=jnp.float32)
        * score_scale
    )
    weights_full = jnp.exp(scores - log_total)
    delta_weights = jnp.einsum(
        "sihd,sjhd->shij", delta_context, values_block, preferred_element_type=jnp.float32
    )
    delta_values = jnp.einsum(
        "shij,sihd->sjhd",
        weights_full.astype(jnp.bfloat16),
        delta_context,
        preferred_element_type=jnp.float32,
    )
    delta_scores = weights_full * (
        delta_weights - jnp.sum(weights_full * delta_weights, axis=-1, keepdims=True)
    )
    delta_scores = delta_scores.astype(jnp.bfloat16)
    delta_queries = (
        jnp.einsum("shij,sjhd->sihd", delta_scores, keys_block, preferred_element_type=jnp.float32)
        * score_scale
    )
    delta_keys = (
        jnp.einsum("shij,sihd->sjhd", delta_scores, queries, preferred_element_type=jnp.float32)
        * score_scale
    )
    delta_projected = jnp.stack([delta_queries, delta_keys, delta_values], axis=2).astype(
        jnp.bfloat16
    )
    delta_projected = delta_projected.reshape(row_count, 3 * group_width)
    grad_project = jnp.einsum(
        "tm,tc->mc", normed, delta_projected, preferred_element_type=jnp.float32
    )
    grad_project = grad_project.reshape(model_width, 3, group_width)
    delta_normed = jnp.einsum(
        "tc,mc->tm",
        delta_projected,
        project_shard.reshape(model_width, 3 * group_width),
        preferred_element_type=jnp.float32,
    )
    delta_normed = lax.psum(delta_normed.astype(jnp.bfloat16), "tensor").astype(jnp.float32)
    unused, norm_back = jax.vjp(layer_norm, state, gain_vector)
    delta_state, grad_gain = norm_back(delta_normed)
    return (delta_one + delta_state, grad_gain, grad_project, grad_output)


def experts_forward(state, gain_vector, router, first_shard, second_shard, route_ids, live_int):
    row_count = state.shape[0]
    model_width = state.shape[1]
    experts = router.shape[1]
    capacity = capacity_of(row_count, experts)
    live_rows = live_int.astype(jnp.float32)
    normed = layer_norm(state, gain_vector).astype(jnp.bfloat16)
    logits = jnp.dot(normed, router, preferred_element_type=jnp.float32)
    gate_probs = jax.nn.softmax(logits, axis=-1)
    chosen = (route_ids[:, :, None] == jnp.arange(experts, dtype=jnp.int32)).astype(jnp.float32)
    gate_picks = jnp.sum(chosen * gate_probs[:, None, :], axis=-1) * live_rows[:, None]
    slot_ids = slot_numbers(route_ids, live_int, experts)
    position = jnp.where(live_int[:, None] > 0, route_ids * capacity + slot_ids, experts * capacity)
    copies = jnp.broadcast_to(normed[:, None, :], (row_count, 2, model_width)).reshape(
        row_count * 2, model_width
    )
    outbox = (
        jnp.zeros((experts * capacity, model_width), jnp.bfloat16)
        .at[position.reshape(-1)]
        .set(copies, mode="drop")
    )
    received = to_experts(outbox.reshape(experts, capacity, model_width))
    preact = jnp.einsum("erd,edf->erf", received, first_shard, preferred_element_type=jnp.float32)
    hidden = jax.nn.gelu(preact).astype(jnp.bfloat16)
    partial_value = jnp.einsum(
        "erf,efd->erd", hidden, second_shard, preferred_element_type=jnp.float32
    )
    partial_value = partial_value.astype(jnp.bfloat16).astype(jnp.float32)
    slot_index = jnp.minimum(position, experts * capacity - 1)
    returned = to_tokens(partial_value)
    pieces = returned.reshape(experts * capacity, model_width)[slot_index]
    mixed = jnp.sum(pieces * gate_picks[:, :, None], axis=1)
    stored = (
        normed,
        gate_probs,
        chosen,
        gate_picks,
        position,
        slot_index,
        received,
        preact,
        hidden,
        pieces,
    )
    return (state + mixed, stored)


def experts_backward(
    delta_out, stored, state, gain_vector, router, first_shard, second_shard, live_rows
):
    (
        normed,
        gate_probs,
        chosen,
        gate_picks,
        position,
        slot_index,
        received,
        preact,
        hidden,
        pieces,
    ) = stored
    row_count = state.shape[0]
    model_width = state.shape[1]
    experts = router.shape[1]
    capacity = capacity_of(row_count, experts)
    delta_picks = jnp.sum(pieces * delta_out[:, None, :], axis=-1) * live_rows[:, None]
    delta_probs = jnp.sum(delta_picks[:, :, None] * chosen, axis=1)
    delta_logits = gate_probs * (
        delta_probs - jnp.sum(gate_probs * delta_probs, axis=-1, keepdims=True)
    )
    grad_router = jnp.dot(normed.astype(jnp.float32).T, delta_logits, precision=HIGHEST_PRECISION)
    delta_normed = jnp.dot(delta_logits, router.astype(jnp.float32).T, precision=HIGHEST_PRECISION)
    slot_grads = (
        (gate_picks[:, :, None] * delta_out[:, None, :])
        .astype(jnp.bfloat16)
        .reshape(row_count * 2, model_width)
    )
    grad_outbox = (
        jnp.zeros((experts * capacity, model_width), jnp.bfloat16)
        .at[position.reshape(-1)]
        .set(slot_grads, mode="drop")
    )
    grad_received = to_experts(grad_outbox.reshape(experts, capacity, model_width))
    grad_second = jnp.einsum(
        "erf,erd->efd", hidden, grad_received, preferred_element_type=jnp.float32
    )
    delta_hidden = jnp.einsum(
        "erd,efd->erf", grad_received, second_shard, preferred_element_type=jnp.float32
    )
    delta_hidden = delta_hidden.astype(jnp.bfloat16)
    unused, gelu_back = jax.vjp(jax.nn.gelu, preact)
    delta_preact = gelu_back(delta_hidden.astype(jnp.float32))[0].astype(jnp.bfloat16)
    grad_first = jnp.einsum(
        "erd,erf->edf", received, delta_preact, preferred_element_type=jnp.float32
    )
    delta_arrived = jnp.einsum(
        "erf,edf->erd", delta_preact, first_shard, preferred_element_type=jnp.float32
    )
    delta_returned = to_tokens(delta_arrived)
    token_grads = (
        jnp.sum(delta_returned.reshape(experts * capacity, model_width)[slot_index], axis=1)
        * live_rows[:, None]
    )
    delta_normed = delta_normed + token_grads
    unused_value, norm_back = jax.vjp(layer_norm, state, gain_vector)
    delta_state, grad_gain = norm_back(delta_normed)
    return (delta_state, grad_gain, grad_router, grad_first, grad_second)


def layer_forward(state, weights_all, route_ids, live_int):
    gain_one, project_shard, output_shard, gain_two, router, first_shard, second_shard = weights_all
    after_attn, stored_attn = attention_forward(state, gain_one, project_shard, output_shard)
    after_moe, stored_moe = experts_forward(
        after_attn, gain_two, router, first_shard, second_shard, route_ids, live_int
    )
    result = live_int.astype(jnp.float32)[:, None] * after_moe
    return (result, (state, after_attn, live_int, stored_attn, stored_moe))


def layer_backward(delta_result, stored, weights_all):
    gain_one, project_shard, output_shard, gain_two, router, first_shard, second_shard = weights_all
    state, after_attn, live_int, stored_attn, stored_moe = stored
    live_rows = live_int.astype(jnp.float32)
    delta_two = delta_result * live_rows[:, None]
    delta_moe, grad_gain_two, grad_router, grad_first, grad_second = experts_backward(
        delta_two, stored_moe, after_attn, gain_two, router, first_shard, second_shard, live_rows
    )
    delta_one = delta_two + delta_moe
    delta_state, grad_gain_one, grad_project, grad_output = attention_backward(
        delta_one, stored_attn, state, gain_one, project_shard, output_shard
    )
    return (
        delta_state,
        (
            grad_gain_one,
            grad_project,
            grad_output,
            grad_gain_two,
            grad_router,
            grad_first,
            grad_second,
        ),
    )


def body(
    tokens,
    cotangent,
    image_counts,
    routes,
    attn_norm_gain,
    query_key_value,
    attn_output,
    moe_norm_gain,
    router_weight,
    expert_in,
    expert_down,
):
    weights_all = (
        attn_norm_gain[0],
        query_key_value[0],
        attn_output[0],
        moe_norm_gain[0],
        router_weight[0],
        expert_in[0],
        expert_down[0],
    )
    micro_count = tokens.shape[0]
    row_count = tokens.shape[1]
    sections = lax.axis_size("pipe")
    section_index = lax.axis_index("pipe")
    data_index = lax.axis_index("dp")
    moments = micro_count + sections - 1
    image_of_row = jnp.arange(row_count, dtype=jnp.int32) // IMG_LEN
    arriving = jnp.zeros(tokens.shape[1:], jnp.bfloat16)
    outputs = jnp.zeros(tokens.shape, jnp.bfloat16)
    stored_list = []
    for moment in range(moments):
        wanted = moment - section_index
        active = (wanted >= 0) & (wanted < micro_count)
        batch_index = jnp.clip(wanted, 0, micro_count - 1)
        live_int = (image_of_row < image_counts[batch_index, data_index]).astype(jnp.int32)
        start = jnp.where(section_index == 0, tokens[batch_index], arriving).astype(jnp.float32)
        result, stored = layer_forward(start, weights_all, routes[batch_index], live_int)
        outgoing = result.astype(jnp.bfloat16)
        outputs = jnp.where(active, outputs.at[batch_index].set(outgoing), outputs)
        stored_list.append(stored)
        if moment + 1 < moments:
            arriving = shifted(outgoing, "pipe", 1)
    stored_all = jax.tree.map(lambda *members: jnp.stack(members), *stored_list)
    arriving = jnp.zeros(tokens.shape[1:], jnp.bfloat16)
    input_grads = jnp.zeros(tokens.shape, jnp.bfloat16)
    grads_all = tuple((jnp.zeros(weight.shape, jnp.float32) for weight in weights_all))
    for moment in range(moments):
        wanted = moment - (sections - 1 - section_index)
        active = (wanted >= 0) & (wanted < micro_count)
        batch_index = jnp.clip(wanted, 0, micro_count - 1)
        forward_moment = jnp.clip(batch_index + section_index, 0, moments - 1)
        stored = jax.tree.map(lambda member: member[forward_moment], stored_all)
        start = jnp.where(section_index == sections - 1, cotangent[batch_index], arriving).astype(
            jnp.float32
        )
        delta_state, grad_terms = layer_backward(start, stored, weights_all)
        outgoing = delta_state.astype(jnp.bfloat16)
        input_grads = jnp.where(active, input_grads.at[batch_index].set(outgoing), input_grads)
        grads_all = jax.tree.map(
            lambda running, addend: jnp.where(active, running + addend, running),
            grads_all,
            grad_terms,
        )
        if moment + 1 < moments:
            arriving = shifted(outgoing, "pipe", -1)
    summed = (
        lax.psum(grads_all[0].astype(jnp.bfloat16), "dp").astype(jnp.float32),
        lax.psum(grads_all[1].astype(jnp.bfloat16), "dp").astype(jnp.float32),
        lax.psum(grads_all[2].astype(jnp.bfloat16), "dp").astype(jnp.float32),
        lax.psum(grads_all[3].astype(jnp.bfloat16), "dp").astype(jnp.float32),
        lax.psum(grads_all[4].astype(jnp.bfloat16), "dp").astype(jnp.float32),
    )
    return (
        outputs[None],
        input_grads[None],
        summed[0][None],
        summed[1][None],
        summed[2][None],
        summed[3][None],
        summed[4][None],
        grads_all[5][None],
        grads_all[6][None],
    )


def solution(mesh):
    placed = (
        P(None, "dp", None),
        P(None, "dp", None),
        P(),
        P(None, "dp", None),
        P("pipe", None),
        P("pipe", None, None, "tensor"),
        P("pipe", "tensor", None),
        P("pipe", None),
        P("pipe", None, None),
        P("pipe", "dp", None, "tensor"),
        P("pipe", "dp", "tensor", None),
    )
    return jax.shard_map(
        body,
        mesh=mesh,
        in_specs=placed,
        out_specs=(
            P("pipe", None, "dp", None),
            P("pipe", None, "dp", None),
            P("pipe", None),
            P("pipe", None, None, "tensor"),
            P("pipe", "tensor", None),
            P("pipe", None),
            P("pipe", None, None),
            P("pipe", "dp", None, "tensor"),
            P("pipe", "dp", "tensor", None),
        ),
        check_vma=False,
    )
```

profile of v0, /device:TPU:7, one launch (start us, length us, event | category | flops | bytes accessed | tf_op | source)
XLA Modules:
  0.0 1542.5 jit_solution(1393584530388204251)
XLA Ops:
  59.3 14.1 all-reduce.19.cloned.1.call-done
  93.4 30.8 %all_to_all.162 = bf16[32,30,768]{2,1,0:T(8,128)(2,1)S(1)} all-to-all(bf16[32,30,768]{2,1,0:T(8,128)(2,1)} %reshape.1757), channel_id=1, replica_groups=mesh['pipe'=2,'tensor'=4,'dp'=16] {'dp'}, dimensions={0} | all-to-all | bytes 2949120 | tf_op jit(solution)/shard_map/all_to_all | solution.py:40
  136.2 42.7 %all-reduce.21.cloned.1.call-done = bf16[2,480,768]{2,1,0:T(8,128)(2,1)} async-done(((bf16[2,480,768]{2,1,0:T(8,128)(2,1)}), bf16[2,480,768]{2,1,0:T(8,128)(2,1)}) %all-reduce.21.cloned.1.call-update) | async-done | bytes 1474576 | tf_op jit(solution)/shard_map/psum | solution.py:44
  182.9 7.9 all-to-all-start.1
  197.6 13.3 all-to-all-done.1
  238.4 15.5 %collective-permute-done = bf16[394,768]{1,0:T(8,128)(2,1)S(1)} collective-permute-done((bf16[394,768]{1,0:T(8,128)(2,1)S(1)}, bf16[394,768]{1,0:T(8,128)(2,1)S(1)}, u32[]{:S(2)}, u32[]{:S(2)}) %collective-permute-start) | collective-permute-done | bytes 605216 | tf_op jit(solution)/shard_map/ppermute | solution.py:17
  268.5 40.4 %all-reduce.23.cloned.1.call-done = bf16[394,768]{1,0:T(8,128)(2,1)} async-done(((bf16[394,768]{1,0:T(8,128)(2,1)}), bf16[394,768]{1,0:T(8,128)(2,1)}) %all-reduce.23.cloned.1.call-update) | async-done | bytes 605200 | tf_op jit(solution)/shard_map/psum | solution.py:83
  330.2 30.8 %all_to_all.163 = bf16[32,30,768]{2,1,0:T(8,128)(2,1)S(1)} all-to-all(bf16[32,30,768]{2,1,0:T(8,128)(2,1)} %reshape.1764), channel_id=1, replica_groups=mesh['pipe'=2,'tensor'=4,'dp'=16] {'dp'}, dimensions={0} | all-to-all | bytes 2949120 | tf_op jit(solution)/shard_map/all_to_all | solution.py:40
  382.9 32.9 %all-reduce.25.cloned.1.call-done = bf16[2,480,768]{2,1,0:T(8,128)(2,1)} async-done(((bf16[2,480,768]{2,1,0:T(8,128)(2,1)}), bf16[2,480,768]{2,1,0:T(8,128)(2,1)}) %all-reduce.25.cloned.1.call-update) | async-done | bytes 1474576 | tf_op jit(solution)/shard_map/psum | solution.py:44
  419.8 7.7 all-to-all-start.3
  434.4 13.2 all-to-all-done.3
  518.9 29.2 %all-reduce.27.cloned.1.call-done = bf16[394,768]{1,0:T(8,128)(2,1)} async-done(((bf16[394,768]{1,0:T(8,128)(2,1)}), bf16[394,768]{1,0:T(8,128)(2,1)}) %all-reduce.27.cloned.1.call-update) | async-done | bytes 605200 | tf_op jit(solution)/shard_map/psum | solution.py:83
  568.9 9.7 all-to-all-start.4
  583.3 10.7 scatter_custom_fusion.3
  615.6 12.3 all-to-all-done.6
  682.8 31.1 %all-reduce.41.cloned.1.call-done = (bf16[2,480,768]{2,1,0:T(8,128)(2,1)}, bf16[2,480,768]{2,1,0:T(8,128)(2,1)}) async-done(((bf16[2,480,768]{2,1,0:T(8,128)(2,1)}, bf16[2,480,768]{2,1,0:T(8,128)(2,1)}), (bf16[2,480,768]{2,1,0:T(8,128)(2,1)}, bf16[2,480,768]{2,1,0:T(8,128)(2,1)})) %all-reduce.41.cloned.1.call-update) | async-done | bytes 2949136 | tf_op jit(solution)/shard_map/psum | solution.py:44
  717.9 7.9 all-to-all-start.5
  851.1 30.1 %all-reduce.29.cloned.1.call-done = bf16[394,768]{1,0:T(8,128)(2,1)} async-done(((bf16[394,768]{1,0:T(8,128)(2,1)}), bf16[394,768]{1,0:T(8,128)(2,1)}) %all-reduce.29.cloned.1.call-update) | async-done | bytes 605200 | tf_op jit(solution)/shard_map/psum | solution.py:144
  912.9 10.7 scatter_custom_fusion.4
  927.3 10.6 all-to-all-start.8
  971.2 9.1 pad_maximum_fusion.1
  984.9 37.8 %all-reduce.31.cloned.1.call-done = bf16[2,480,768]{2,1,0:T(8,128)(2,1)} async-done(((bf16[2,480,768]{2,1,0:T(8,128)(2,1)}), bf16[2,480,768]{2,1,0:T(8,128)(2,1)}) %all-reduce.31.cloned.1.call-update) | async-done | bytes 1474576 | tf_op jit(solution)/shard_map/psum | solution.py:44
  1026.7 7.7 all-to-all-start.9
  1045.7 8.8 all-to-all-done.9
  1112.0 27.5 %all-reduce.33.cloned.1.call-done = bf16[394,768]{1,0:T(8,128)(2,1)} async-done(((bf16[394,768]{1,0:T(8,128)(2,1)}), bf16[394,768]{1,0:T(8,128)(2,1)}) %all-reduce.33.cloned.1.call-update) | async-done | bytes 605200 | tf_op jit(solution)/shard_map/psum | solution.py:144
  1169.1 10.7 scatter_custom_fusion.5
  1183.1 10.8 all-to-all-start.10
  1244.0 32.2 %all-reduce.35.cloned.1.call-done = bf16[2,480,768]{2,1,0:T(8,128)(2,1)} async-done(((bf16[2,480,768]{2,1,0:T(8,128)(2,1)}), bf16[2,480,768]{2,1,0:T(8,128)(2,1)}) %all-reduce.35.cloned.1.call-update) | async-done | bytes 1474576 | tf_op jit(solution)/shard_map/psum | solution.py:44
  1288.3 8.5 fusion.1
  1353.9 35.2 %all-reduce.37.cloned.1.call-done = bf16[394,768]{1,0:T(8,128)(2,1)} async-done(((bf16[394,768]{1,0:T(8,128)(2,1)}), bf16[394,768]{1,0:T(8,128)(2,1)}) %all-reduce.37.cloned.1.call-update) | async-done | bytes 605200 | tf_op jit(solution)/shard_map/psum | solution.py:144
  1393.1 59.0 %all-reduce.3 = (bf16[1,768]{1,0:T(2,128)(2,1)S(1)}, bf16[1,768]{1,0:T(2,128)(2,1)S(1)}, bf16[1,768,32]{1,2,0:T(8,128)(2,1)S(1)}) all-reduce(bf16[1,768]{1,0:T(2,128)(2,1)S(1)} %broadcast_in_dim.291, bf16[1,768]{1,0:T(2,128)(2,1)S(1)} %broadcast_in_dim.299, ...), channel_id=1, replica_groups=mesh['pipe'=2,'tensor'=4,'dp'=16] {'dp'}, use_global_device_ids=true, to_apply=%region_105.106 | all-reduce | flops 26112 | bytes 104448 | tf_op jit(solution)/shard_map/psum | solution.py:364
  1461.6 70.3 %all-reduce.39.cloned.1.call-done = (bf16[1,768,3,192]{1,3,2,0:T(8,128)(2,1)}, bf16[1,192,768]{2,1,0:T(8,128)(2,1)}) async-done(((bf16[1,768,3,192]{1,3,2,0:T(8,128)(2,1)}, bf16[1,192,768]{2,1,0:T(8,128)(2,1)}), (bf16[1,768,3,192]{1,3,2,0:T(8,128)(2,1)}, bf16[1,192,768]{2,1,0:T(8,128)(2,1)})) %all-reduce.39.cloned.1.call-update) | async-done | bytes 1179664 | tf_op jit(solution)/shard_map/psum | solution.py:365
  (898 shorter events, 805.7 us)
Async XLA Ops:
  7.2 121.7 %copy-start = (bf16[1,2,768,768]{3,2,1,0:T(8,128)(2,1)S(1)}, bf16[1,2,768,768]{3,2,1,0:T(8,128)(2,1)}, u32[]{:S(2)}) copy-start(bf16[1,2,768,768]{3,2,1,0:T(8,128)(2,1)} %param.33) | copy-start | bytes 7077892
  7.2 66.2 %all-reduce.19.cloned.1.call-start = ((), (), s32[]{:S(2)}) async-start(), calls=%async_computation.12 | async-start | bytes 1228800 | tf_op jit(solution)/shard_map/psum | solution.py:83
  29.3 149.6 %all-reduce.21.cloned.1.call-start = ((), (), s32[]{:S(2)}) async-start(), calls=%async_computation.13 | async-start | bytes 2949120 | tf_op jit(solution)/shard_map/psum | solution.py:44
  58.0 74.4 %copy-start.111 = (s32[788]{0:T(1024)}, s32[788]{0:T(1024)S(1)}, u32[]{:S(2)}) copy-start(s32[788]{0:T(1024)S(1)} %fusion.276) | copy-start | bytes 9460
  182.9 27.9 %all-to-all-start.1 = ((bf16[2,480,768]{2,0,1:T(2,128)(2,1)}), bf16[2,480,768]{2,0,1:T(2,128)(2,1)}, u32[]{:S(2)}, u32[]{:S(2)}) async-start(bf16[2,480,768]{2,0,1:T(2,128)(2,1)} %copy.574), calls=%async_computation.1 | async-start | bytes 2949120 | tf_op jit(solution)/shard_map/all_to_all | solution.py:45
  190.8 118.1 %all-reduce.23.cloned.1.call-start = ((), (), s32[]{:S(2)}) async-start(), calls=%async_computation.14 | async-start | bytes 1228800 | tf_op jit(solution)/shard_map/psum | solution.py:83
  193.9 40.9 %copy-start.137 = (f32[394]{0:T(512)}, f32[394]{0:T(512)S(1)}, u32[]{:S(2)}) copy-start(f32[394]{0:T(512)S(1)} %fusion.361) | copy-start | bytes 4732
  236.9 16.9 %collective-permute-start = (bf16[394,768]{1,0:T(8,128)(2,1)S(1)}, bf16[394,768]{1,0:T(8,128)(2,1)S(1)}, u32[]{:S(2)}, u32[]{:S(2)}) collective-permute-start(bf16[394,768]{1,0:T(8,128)(2,1)S(1)} %get-tuple-element.203), channel_id=1, source_target_pairs={{0,64},{1,65},{2,66},{3,67},{4,68},{5,69},{6,70},{7,71},{8,72},{9,... | collective-permute-start | bytes 1815560 | tf_op jit(solution)/shard_map/ppermute | solution.py:17
  265.5 44.8 %copy-start.82 = (bf16[2,197,3,64]{1,0,3,2:T(2,128)(2,1)}, bf16[2,197,3,64]{1,0,3,2:T(2,128)(2,1)S(1)}, u32[]{:S(2)}) copy-start(bf16[2,197,3,64]{1,0,3,2:T(2,128)(2,1)S(1)} %copy.585) | copy-start | bytes 453892
  268.5 147.3 %all-reduce.25.cloned.1.call-start = ((), (), s32[]{:S(2)}) async-start(), calls=%async_computation.15 | async-start | bytes 2949120 | tf_op jit(solution)/shard_map/psum | solution.py:44
  419.8 27.8 %all-to-all-start.3 = ((bf16[2,480,768]{2,0,1:T(2,128)(2,1)}), bf16[2,480,768]{2,0,1:T(2,128)(2,1)}, u32[]{:S(2)}, u32[]{:S(2)}) async-start(bf16[2,480,768]{2,0,1:T(2,128)(2,1)} %copy.593), calls=%async_computation.3 | async-start | bytes 2949120 | tf_op jit(solution)/shard_map/all_to_all | solution.py:45
  427.5 120.6 %all-reduce.27.cloned.1.call-start = ((), (), s32[]{:S(2)}) async-start(), calls=%async_computation.16 | async-start | bytes 1228800 | tf_op jit(solution)/shard_map/psum | solution.py:83
  428.5 48.5 %copy-start.183 = (pred[394]{0:T(512)(128)(4,1)}, pred[394]{0:T(512)(128)(4,1)S(1)}, u32[]{:S(2)}) copy-start(pred[394]{0:T(512)(128)(4,1)S(1)} %broadcast_compare_fusion.3) | copy-start | bytes 1186
  474.6 17.2 %collective-permute-start.1 = (bf16[394,768]{1,0:T(8,128)(2,1)}, bf16[394,768]{1,0:T(8,128)(2,1)}, u32[]{:S(2)}, u32[]{:S(2)}) collective-permute-start(bf16[394,768]{1,0:T(8,128)(2,1)} %get-tuple-element.199), channel_id=1, source_target_pairs={{0,64},{1,65},{2,66},{3,67},{4,68},{5,69},{6,70},{7,71},{8,72},{9,... | collective-permute-start | bytes 1815560 | tf_op jit(solution)/shard_map/ppermute | solution.py:17
  518.9 61.8 %copy-start.135 = (f32[394]{0:T(512)}, f32[394]{0:T(512)S(1)}, u32[]{:S(2)}) copy-start(f32[394]{0:T(512)S(1)} %fusion.363) | copy-start | bytes 4732
  568.9 30.8 %all-to-all-start.4 = ((bf16[32,30,768]{2,1,0:T(8,128)(2,1)}), bf16[32,30,768]{2,1,0:T(8,128)(2,1)}, u32[]{:S(2)}, u32[]{:S(2)}) async-start(bf16[32,30,768]{2,1,0:T(8,128)(2,1)} %reshape.1772), calls=%async_computation.4 | async-start | bytes 3145728 | tf_op jit(solution)/shard_map/all_to_all | solution.py:40
  599.8 28.1 %all-to-all-start.6 = ((bf16[32,30,768]{2,1,0:T(8,128)(2,1)}), bf16[32,30,768]{2,1,0:T(8,128)(2,1)}, u32[]{:S(2)}, u32[]{:S(2)}) async-start(bf16[32,30,768]{2,1,0:T(8,128)(2,1)} %reshape.1778), calls=%async_computation.6 | async-start | bytes 3145728 | tf_op jit(solution)/shard_map/all_to_all | solution.py:40
  606.8 107.1 %all-reduce.41.cloned.1.call-start = ((), (), s32[]{:S(2)}) async-start(), calls=%async_computation.23 | async-start | bytes 5898240 | tf_op jit(solution)/shard_map/psum | solution.py:44
  717.9 27.8 %all-to-all-start.5 = ((bf16[2,480,768]{2,0,1:T(2,128)(2,1)}), bf16[2,480,768]{2,0,1:T(2,128)(2,1)}, u32[]{:S(2)}, u32[]{:S(2)}) async-start(bf16[2,480,768]{2,0,1:T(2,128)(2,1)} %copy.612), calls=%async_computation.5 | async-start | bytes 2949120 | tf_op jit(solution)/shard_map/all_to_all | solution.py:45
  745.7 27.3 %all-to-all-start.7 = ((bf16[2,480,768]{2,0,1:T(2,128)(2,1)}), bf16[2,480,768]{2,0,1:T(2,128)(2,1)}, u32[]{:S(2)}, u32[]{:S(2)}) async-start(bf16[2,480,768]{2,0,1:T(2,128)(2,1)} %copy.627), calls=%async_computation.7 | async-start | bytes 2949120 | tf_op jit(solution)/shard_map/all_to_all | solution.py:45
  753.0 128.2 %all-reduce.29.cloned.1.call-start = ((), (), s32[]{:S(2)}) async-start(), calls=%async_computation.17 | async-start | bytes 1228800 | tf_op jit(solution)/shard_map/psum | solution.py:144
  890.9 13.1 collective-permute-start.2
  927.3 32.7 %all-to-all-start.8 = ((bf16[32,30,768]{2,1,0:T(8,128)(2,1)}), bf16[32,30,768]{2,1,0:T(8,128)(2,1)}, u32[]{:S(2)}, u32[]{:S(2)}) async-start(bf16[32,30,768]{2,1,0:T(8,128)(2,1)} %reshape.1780), calls=%async_computation.8 | async-start | bytes 3145728 | tf_op jit(solution)/shard_map/all_to_all | solution.py:40
  938.0 84.8 %all-reduce.31.cloned.1.call-start = ((), (), s32[]{:S(2)}) async-start(), calls=%async_computation.18 | async-start | bytes 2949120 | tf_op jit(solution)/shard_map/psum | solution.py:44
  1026.7 27.8 %all-to-all-start.9 = ((bf16[2,480,768]{2,0,1:T(2,128)(2,1)}), bf16[2,480,768]{2,0,1:T(2,128)(2,1)}, u32[]{:S(2)}, u32[]{:S(2)}) async-start(bf16[2,480,768]{2,0,1:T(2,128)(2,1)} %copy.647), calls=%async_computation.9 | async-start | bytes 2949120 | tf_op jit(solution)/shard_map/all_to_all | solution.py:45
  1034.5 105.1 %all-reduce.33.cloned.1.call-start = ((), (), s32[]{:S(2)}) async-start(), calls=%async_computation.19 | async-start | bytes 1228800 | tf_op jit(solution)/shard_map/psum | solution.py:144
  1148.1 13.1 collective-permute-start.3
  1183.1 31.9 %all-to-all-start.10 = ((bf16[32,30,768]{2,1,0:T(8,128)(2,1)}), bf16[32,30,768]{2,1,0:T(8,128)(2,1)}, u32[]{:S(2)}, u32[]{:S(2)}) async-start(bf16[32,30,768]{2,1,0:T(8,128)(2,1)} %reshape.1783), calls=%async_computation.10 | async-start | bytes 3145728 | tf_op jit(solution)/shard_map/all_to_all | solution.py:40
  1193.9 82.3 %all-reduce.35.cloned.1.call-start = ((), (), s32[]{:S(2)}) async-start(), calls=%async_computation.20 | async-start | bytes 2949120 | tf_op jit(solution)/shard_map/psum | solution.py:44
  1280.2 27.8 %all-to-all-start.11 = ((bf16[2,480,768]{2,0,1:T(2,128)(2,1)}), bf16[2,480,768]{2,0,1:T(2,128)(2,1)}, u32[]{:S(2)}, u32[]{:S(2)}) async-start(bf16[2,480,768]{2,0,1:T(2,128)(2,1)} %copy.664), calls=%async_computation.11 | async-start | bytes 2949120 | tf_op jit(solution)/shard_map/all_to_all | solution.py:45
  1288.0 101.1 %all-reduce.37.cloned.1.call-start = ((), (), s32[]{:S(2)}) async-start(), calls=%async_computation.21 | async-start | bytes 1228800 | tf_op jit(solution)/shard_map/psum | solution.py:144
  1348.8 183.0 %all-reduce.39.cloned.1.call-start = ((), (), s32[]{:S(2)}) async-start(), calls=%async_computation.22 | async-start | bytes 2359296 | tf_op jit(solution)/shard_map/psum | solution.py:365
  (195 other events, 1190.7 us)
Sparse Core Ops, SparseCore 0:
  29.4 43.9 all-reduce.18
  131.6 47.2 all-reduce.20
  268.6 40.2 all-reduce.22
  368.4 47.3 all-reduce.24
  507.9 40.2 all-reduce.26
  642.2 71.6 all-reduce.40
  841.6 39.4 all-reduce.28
  971.4 51.3 all-reduce.30
  1099.5 40.0 all-reduce.32
  1226.6 49.5 all-reduce.34
  1348.9 40.0 all-reduce.36
  1392.2 139.6 all-reduce.38
where the time goes:
time: 1560 us; the launch traced here: 1540 us
  waiting for transfers between devices  515 us (33%)
  local copies, waits for them, and re-layouts  435 us (28%)
  other arithmetic  228 us (15%)
  matrix products  130 us (8%)
  blocking collectives  121 us (8%)
  starting transfers between devices  96.2 us (6%)
  between operations  17.6 us (1%)
    psum x5, waiting for transfers between devices, to_tokens(): lax.psum(partial_value.astype(jnp.bfloat16), 'tensor').astype(jnp.float32)  177 us
    psum x3, waiting for transfers between devices, attention_backward(): lax.psum(delta_normed.astype(jnp.bfloat16), 'tensor').astype(jnp.float32)  92.8 us
    psum x3, waiting for transfers between devices, attention_forward(): lax.psum(partial_value.astype(jnp.bfloat16), 'tensor').astype(jnp.float32)  83.6 us
    psum x1, waiting for transfers between devices, body(): lax.psum(grads_all[1].astype(jnp.bfloat16), 'dp').astype(jnp.float32)  70.3 us
    all_to_all x2, blocking collectives, to_experts(): return lax.all_to_all(outbox, 'dp', split_axis=0, concat_axis=1, tiled=True)  61.6 us
    psum x1, blocking collectives, body(): lax.psum(grads_all[0].astype(jnp.bfloat16), 'dp').astype(jnp.float32)  59 us
    unnamed x412, local copies, waits for them, and re-layouts  56.6 us
    another operation x25, other arithmetic, body(): stored_all = jax.tree.map(lambda *members: jnp.stack(members), *stored_list)  48.2 us
  transfers between devices with their start and end apart: 26, of which 24 were waited for; matrix products, arithmetic and copies ran while one was open for 21% of the time, Pallas kernels for 0%

commit v1 on v0

v1 whole, which is shorter than its diff:
```python
import functools

import jax
import jax.numpy as jnp
from jax import lax
from jax.experimental import pallas as pl
from jax.experimental.pallas import tpu as pltpu
from jax.sharding import PartitionSpec as P

BF = jnp.bfloat16
F32 = jnp.float32
MESH = pl.DeviceIdType.MESH
D = 768
HD = 64
NH = 3
GW = NH * HD
IMG_LEN = 197
R = 224
NR = 2 * R
CH = NR // 4
EXPERTS = 32
SL = 32
NT = 4
NDP = 16
Q = D // NT
EPSILON = 1e-06
VMEM_BYTES = 48 * 1024 * 1024
GP = 896


def dot(a, b, ca=1, cb=0):
    return lax.dot_general(a, b, (((ca,), (cb,)), ((), ())), preferred_element_type=F32)


def params(**more):
    return pltpu.CompilerParams(vmem_limit_bytes=VMEM_BYTES, **more)


def norm_parts(values):
    mean = jnp.mean(values, axis=-1, keepdims=True)
    centred = values - mean
    inverse = lax.rsqrt(jnp.mean(centred * centred, axis=-1, keepdims=True) + EPSILON)
    return centred * inverse, inverse


def norm_back(delta, gain, normal, inverse):
    scaled = delta * gain
    return inverse * (
        scaled
        - jnp.mean(scaled, axis=-1, keepdims=True)
        - normal * jnp.mean(scaled * normal, axis=-1, keepdims=True)
    )


def pick(index, options):
    result = options[0]
    for number in range(1, len(options)):
        result = jnp.where(index == number, options[number], result)
    return result


def column_quarter(values, member):
    return pick(member, [values[:, Q * q : Q * (q + 1)] for q in range(NT)])


def unpack(packed):
    images = [
        jnp.concatenate([packed[q][:, Q * i : Q * (i + 1)] for q in range(NT)], axis=1)
        for i in range(2)
    ]
    return jnp.concatenate(images, axis=0)


def head_parts(projected, image, head):
    rows = slice(image * R, (image + 1) * R)
    return [
        projected[rows, part * GW + head * HD : part * GW + (head + 1) * HD] for part in range(3)
    ]


def probabilities(queries, keys):
    scores = dot(queries, keys, 1, 1) * (HD**-0.5)
    held = lax.broadcasted_iota(jnp.int32, scores.shape, 1) < IMG_LEN
    scores = jnp.where(held, scores, -1e30)
    exponent = jnp.exp(scores - jnp.max(scores, axis=-1, keepdims=True))
    return exponent / jnp.sum(exponent, axis=-1, keepdims=True)


def attention_forward_kernel(mode, *refs):
    if mode == "plain":
        plain, gain, project, output, part, qkv, ctx = refs
        state = plain[...]
    elif mode == "packed":
        packed, gain, project, output, part, qkv, ctx, kept = refs
        state = unpack(packed)
        kept[...] = state
    else:
        plain, packed, gain, project, output, part, qkv, ctx, kept = refs
        first = lax.axis_index("pipe") == 0
        state = jnp.where(first, plain[...], unpack(packed))
        kept[...] = state
    normal, _ = norm_parts(state.astype(F32))
    normed = (normal * gain[...]).astype(BF)
    projected = dot(normed, project[...]).astype(BF)
    qkv[...] = projected
    for image in range(2):
        for head in range(NH):
            queries, keys, values = head_parts(projected, image, head)
            weights = probabilities(queries, keys).astype(BF)
            ctx[image * R : (image + 1) * R, head * HD : (head + 1) * HD] = dot(
                weights, values
            ).astype(BF)
    part[...] = dot(ctx[...], output[...]).astype(BF)


def attention_forward(mode, inputs, gain, project, output):
    shapes = [
        jax.ShapeDtypeStruct((NR, D), BF),
        jax.ShapeDtypeStruct((NR, 3 * GW), BF),
        jax.ShapeDtypeStruct((NR, GW), BF),
    ]
    if mode != "plain":
        shapes.append(jax.ShapeDtypeStruct((NR, D), BF))
    return pl.pallas_call(
        functools.partial(attention_forward_kernel, mode),
        out_shape=shapes,
        compiler_params=params(),
        name="attention_forward",
    )(*inputs, gain, project, output)


def live_rows(count):
    row = lax.broadcasted_iota(jnp.int32, (NR, 1), 0)
    image = (row >= R).astype(jnp.int32)
    return (image < count) & (row - image * R < IMG_LEN)


def dispatch_kernel(count, state, summed, gain, router, routes, outbox, x1, meta):
    values = state[...].astype(F32) + summed[...].astype(F32)
    x1[...] = values
    normal, _ = norm_parts(values)
    normed = (normal * gain[...]).astype(BF)
    logits = dot(normed, router[...])
    exponent = jnp.exp(logits - jnp.max(logits, axis=-1, keepdims=True))
    gate = exponent / jnp.sum(exponent, axis=-1, keepdims=True)
    live = live_rows(count[0, 0])
    experts = lax.broadcasted_iota(jnp.int32, (NR, EXPERTS), 1)
    route = [routes[:, k : k + 1] for k in range(2)]
    match = [jnp.where(live & (route[k] == experts), 1.0, 0.0) for k in range(2)]
    above = lax.broadcasted_iota(jnp.int32, (NR, NR), 1) < lax.broadcasted_iota(
        jnp.int32, (NR, NR), 0
    )
    before = dot(jnp.where(above, 1.0, 0.0).astype(BF), (match[0] + match[1]).astype(BF))
    meta[:, 0:EXPERTS] = gate
    hot = None
    slots = lax.broadcasted_iota(jnp.int32, (NR, EXPERTS * SL), 1)
    for k in range(2):
        slot = jnp.sum(match[k] * before, axis=1, keepdims=True).astype(jnp.int32)
        position = jnp.where(live, route[k] * SL + slot, -1)
        meta[:, 32 + k : 33 + k] = jnp.sum(match[k] * gate, axis=1, keepdims=True)
        meta[:, 34 + k : 35 + k] = position.astype(F32)
        meta[:, 36 + k : 37 + k] = route[k].astype(F32)
        same = slots == position
        hot = same if hot is None else hot | same
    meta[:, 38:39] = jnp.where(live, 1.0, 0.0)
    outbox[...] = dot(jnp.where(hot, 1.0, 0.0).astype(BF), normed, 0, 0).astype(BF)


def dispatch(count, state, summed, gain, router, routes):
    return pl.pallas_call(
        dispatch_kernel,
        in_specs=[pl.BlockSpec(memory_space=pltpu.SMEM)]
        + [pl.BlockSpec(memory_space=pltpu.VMEM)] * 5,
        out_shape=[
            jax.ShapeDtypeStruct((EXPERTS * SL, D), BF),
            jax.ShapeDtypeStruct((NR, D), F32),
            jax.ShapeDtypeStruct((NR, 128), F32),
        ],
        compiler_params=params(),
        name="dispatch",
    )(count, state, summed, gain, router, routes)


CUBE = 0.044715
ROOT = 0.7978845608028654


def gelu_parts(pre):
    squared = pre * pre
    inner = jnp.tanh(ROOT * (pre + CUBE * pre * squared))
    return 0.5 * pre * (1.0 + inner), inner, squared


def store_quarters(target, half, values):
    for q in range(NT):
        target[q, :, half * Q : (half + 1) * Q] = values[:, q * Q : (q + 1) * Q].astype(BF)


def experts_forward_kernel(arrived, first, second, part):
    rows = arrived[...].reshape(NDP * SL, D)
    hidden = gelu_parts(dot(rows, first[0]))[0].astype(BF)
    result = dot(hidden, second[0])
    for half in range(2):

        @pl.when(pl.program_id(0) == half)
        def _():
            store_quarters(part, half, result)


def experts_forward(arrived, first, second):
    return pl.pallas_call(
        experts_forward_kernel,
        grid=(2,),
        in_specs=[
            pl.BlockSpec((NDP, SL, D), lambda p: (0, p, 0)),
            pl.BlockSpec((1, D, D), lambda p: (p, 0, 0)),
            pl.BlockSpec((1, D, D), lambda p: (p, 0, 0)),
        ],
        out_specs=pl.BlockSpec((NT, NDP * SL, 2 * Q), lambda p: (0, 0, 0)),
        out_shape=jax.ShapeDtypeStruct((NT, NDP * SL, 2 * Q), BF),
        compiler_params=params(),
        name="experts_forward",
    )(arrived, first, second)


def experts_backward_kernel(arrived, delta, first, second, part, hidden_out, dpre_out):
    rows = arrived[...].reshape(NDP * SL, D)
    grads = delta[...].reshape(NDP * SL, D)
    pre = dot(rows, first[0])
    hidden, inner, squared = gelu_parts(pre)
    hidden_out[...] = hidden.astype(BF).reshape(NDP, SL, D)
    slope = 0.5 * (1.0 + inner) + (0.5 * ROOT) * pre * (1.0 - inner * inner) * (
        1.0 + 3.0 * CUBE * squared
    )
    dhidden = dot(grads, second[0], 1, 1).astype(BF).astype(F32)
    dpre = (dhidden * slope).astype(BF)
    dpre_out[...] = dpre.reshape(NDP, SL, D)
    result = dot(dpre, first[0], 1, 1)
    for half in range(2):

        @pl.when(pl.program_id(0) == half)
        def _():
            store_quarters(part, half, result)


def experts_backward(arrived, delta, first, second):
    rows = pl.BlockSpec((NDP, SL, D), lambda p: (0, p, 0))
    weights = pl.BlockSpec((1, D, D), lambda p: (p, 0, 0))
    return pl.pallas_call(
        experts_backward_kernel,
        grid=(2,),
        in_specs=[rows, rows, weights, weights],
        out_specs=[pl.BlockSpec((NT, NDP * SL, 2 * Q), lambda p: (0, 0, 0)), rows, rows],
        out_shape=[
            jax.ShapeDtypeStruct((NT, NDP * SL, 2 * Q), BF),
            jax.ShapeDtypeStruct((NDP, 2 * SL, D), BF),
            jax.ShapeDtypeStruct((NDP, 2 * SL, D), BF),
        ],
        compiler_params=params(),
        name="experts_backward",
    )(arrived, delta, first, second)


def expert_grads_kernel(a0, a1, b0, b1, c0, c1, d0, d1, grad_first, grad_second):
    def flat(ref):
        return ref[...].reshape(NDP * SL, D)

    grad_first[0] = dot(flat(a0), flat(b0), 0, 0) + dot(flat(a1), flat(b1), 0, 0)
    grad_second[0] = dot(flat(c0), flat(d0), 0, 0) + dot(flat(c1), flat(d1), 0, 0)


def expert_grads(*inputs):
    rows = pl.BlockSpec((NDP, SL, D), lambda p: (0, p, 0))
    weights = pl.BlockSpec((1, D, D), lambda p: (p, 0, 0))
    return pl.pallas_call(
        expert_grads_kernel,
        grid=(2,),
        in_specs=[rows] * 8,
        out_specs=[weights, weights],
        out_shape=[jax.ShapeDtypeStruct((2, D, D), F32)] * 2,
        compiler_params=params(),
        name="expert_grads",
    )(*inputs)


def gathered(returned, meta, k):
    position = meta[:, 34 + k : 35 + k].astype(jnp.int32)
    place = jnp.where(position >= 0, (position // 64) * SL + position % SL, -1)
    odd = (position // SL) % 2 == 1
    hot = lax.broadcasted_iota(jnp.int32, (NR, NDP * SL), 1) == place
    both = dot(jnp.where(hot, 1.0, 0.0).astype(BF), returned)
    return jnp.where(odd, both[:, Q:], both[:, :Q])


def combine_kernel(returned, x1, meta, packed, pieces):
    member = lax.axis_index("tensor")
    live = meta[:, 38:39]
    total = column_quarter(x1, member)
    for k in range(2):
        piece = gathered(returned[...], meta, k)
        pieces[k] = piece.astype(BF)
        total = total + meta[:, 32 + k : 33 + k] * piece
    total = (total * live).astype(BF)
    packed[:, :Q] = total[:R]
    packed[:, Q:] = total[R:]


def combine(returned, x1, meta):
    return pl.pallas_call(
        combine_kernel,
        out_shape=[
            jax.ShapeDtypeStruct((R, 2 * Q), BF),
            jax.ShapeDtypeStruct((2, NR, Q), BF),
        ],
        compiler_params=params(),
        name="combine",
    )(returned, x1, meta)


def spread_kernel(delta, meta, outbox):
    values = delta[...].astype(F32) * meta[:, 38:39]
    slots = lax.broadcasted_iota(jnp.int32, (NR, EXPERTS * SL), 1)
    total = None
    for k in range(2):
        position = meta[:, 34 + k : 35 + k].astype(jnp.int32)
        hot = jnp.where(slots == position, 1.0, 0.0).astype(BF)
        scaled = (values * meta[:, 32 + k : 33 + k]).astype(BF)
        term = dot(hot, scaled, 0, 0)
        total = term if total is None else total + term
    outbox[...] = total.astype(BF)


def spread(delta, meta):
    return pl.pallas_call(
        spread_kernel,
        out_shape=jax.ShapeDtypeStruct((EXPERTS * SL, D), BF),
        compiler_params=params(),
        name="spread",
    )(delta, meta)


def collect_kernel(returned, meta, pieces, delta, packed, dpicks):
    member = lax.axis_index("tensor")
    total = None
    lanes = lax.broadcasted_iota(jnp.int32, (NR, 128), 1)
    columns = jnp.zeros((NR, 128), F32)
    part = column_quarter(delta, member).astype(F32) * meta[:, 38:39]
    for k in range(2):
        piece = gathered(returned[...], meta, k)
        total = piece if total is None else total + piece
        dots = jnp.sum(pieces[k].astype(F32) * part, axis=1, keepdims=True)
        columns = jnp.where(lanes == k, dots, columns)
    total = total.astype(BF)
    packed[:, :Q] = total[:R]
    packed[:, Q:] = total[R:]
    dpicks[:, :NR] = jnp.transpose(columns)[:8]
    dpicks[:, NR:] = jnp.zeros((8, 512 - NR), F32)


def collect(returned, meta, pieces, delta):
    return pl.pallas_call(
        collect_kernel,
        out_shape=[jax.ShapeDtypeStruct((R, 2 * Q), BF), jax.ShapeDtypeStruct((8, 512), F32)],
        compiler_params=params(),
        name="collect",
    )(returned, meta, pieces, delta)


def halves(values):
    high = values.astype(BF)
    return high, (values - high.astype(F32)).astype(BF)


def layer_backward_kernel(
    packed, dpicks, delta, x1, meta, gain_two, router, state, gain_one, qkv, ctx, project, output,
    part, dx1_out, grads, grad_gain, dqkv,
):
    live = meta[:, 38:39]
    gate = meta[:, 0:EXPERTS]
    dx2 = delta[...].astype(F32) * live
    total = dpicks[0] + dpicks[1] + dpicks[2] + dpicks[3]
    total = jnp.concatenate([total, jnp.zeros((120, 512), F32)], axis=0)
    columns = jnp.transpose(total)[:NR]
    experts = lax.broadcasted_iota(jnp.int32, (NR, EXPERTS), 1)
    dgate = jnp.zeros((NR, EXPERTS), F32)
    for k in range(2):
        route = meta[:, 36 + k : 37 + k].astype(jnp.int32)
        dgate = dgate + jnp.where(route == experts, columns[:, k : k + 1] * live, 0.0)
    dlogits = gate * (dgate - jnp.sum(gate * dgate, axis=-1, keepdims=True))
    normal, inverse = norm_parts(x1[...])
    normed = (normal * gain_two[...]).astype(BF)
    high, low = halves(dlogits)
    grads[:, 768:800] = dot(normed, high, 0, 0) + dot(normed, low, 0, 0)
    grads[:, 800:] = jnp.zeros((D, GP - 800), F32)
    dz2 = unpack(packed).astype(F32) + dot(high, router[...], 1, 1) + dot(low, router[...], 1, 1)
    grad_gain[...] = jnp.broadcast_to(jnp.sum(dz2 * normal, axis=0, keepdims=True), (8, D))
    dx1 = dx2 + norm_back(dz2, gain_two[...], normal, inverse)
    dx1_out[...] = dx1
    dattn = dx1.astype(BF)
    grads[:, 576:768] = dot(dattn, ctx[...], 0, 0)
    dctx = dot(dattn, output[...], 1, 1).astype(BF)
    scale = HD**-0.5
    projected = qkv[...]
    for image in range(2):
        rows = slice(image * R, (image + 1) * R)
        for head in range(NH):
            queries, keys, values = head_parts(projected, image, head)
            dc = dctx[rows, head * HD : (head + 1) * HD]
            weights = probabilities(queries, keys)
            dweights = dot(dc, values, 1, 1)
            dvalues = dot(weights.astype(BF), dc, 0, 0)
            dscores = weights * (dweights - jnp.sum(weights * dweights, axis=-1, keepdims=True))
            dscores = dscores.astype(BF)
            dqueries = dot(dscores, keys) * scale
            dkeys = dot(dscores, queries, 0, 0) * scale
            for number, value in enumerate((dqueries, dkeys, dvalues)):
                start = number * GW + head * HD
                dqkv[rows, start : start + HD] = value.astype(BF)
    normal_one, _ = norm_parts(state[...].astype(F32))
    normed_one = (normal_one * gain_one[...]).astype(BF)
    part[...] = dot(dqkv[...], project[...], 1, 1).astype(BF)
    grads[:, 0:576] = dot(normed_one, dqkv[...], 0, 0)


def layer_backward(*inputs):
    return pl.pallas_call(
        layer_backward_kernel,
        out_shape=[
            jax.ShapeDtypeStruct((NR, D), BF),
            jax.ShapeDtypeStruct((NR, D), F32),
            jax.ShapeDtypeStruct((D, GP), F32),
            jax.ShapeDtypeStruct((8, D), F32),
        ],
        scratch_shapes=[pltpu.VMEM((NR, 3 * GW), BF)],
        compiler_params=params(),
        name="layer_backward",
    )(*inputs)


def greet(tensor=False, dp=False, pipe=False):
    barrier = pltpu.get_barrier_semaphore()
    count = 0
    for used, axis, size in ((tensor, "tensor", NT), (dp, "dp", NDP), (pipe, "pipe", 2)):
        if used:
            me = lax.axis_index(axis)
            for step in range(1, size):
                pl.semaphore_signal(
                    barrier, inc=1, device_id={axis: (me + step) % size}, device_id_type=MESH
                )
            count += size - 1
    return barrier, count


def send(source, target, send_sem, recv_sem, axis, peer):
    copy = pltpu.make_async_remote_copy(
        src_ref=source,
        dst_ref=target,
        send_sem=send_sem,
        recv_sem=recv_sem,
        device_id={axis: peer},
        device_id_type=MESH,
    )
    copy.start()
    return copy


def add_up(own, held, me, count):
    total = own.astype(F32)
    for step in range(1, count):
        total = total + held[(me + step) % count].astype(F32)
    return total


def sum_tensor_kernel(part, result, held, mine, sems):
    barrier, count = greet(tensor=True)
    pl.semaphore_wait(barrier, count)
    me = lax.axis_index("tensor")
    copies = []
    for step in range(1, NT):
        peer = (me + step) % NT
        copies.append(
            send(part.at[peer], held.at[me], sems.at[0, step], sems.at[1, step], "tensor", peer)
        )
    for copy in copies:
        copy.wait()
    mine[...] = add_up(part[me], held, me, NT).astype(BF)
    copies = []
    for step in range(1, NT):
        peer = (me + step) % NT
        copies.append(
            send(mine, result.at[me], sems.at[2, step], sems.at[3, step], "tensor", peer)
        )
    result[me] = mine[...]
    for copy in copies:
        copy.wait()


def sum_tensor(part):
    return pl.pallas_call(
        sum_tensor_kernel,
        in_specs=[pl.BlockSpec(memory_space=pltpu.VMEM)],
        out_specs=pl.BlockSpec(memory_space=pltpu.VMEM),
        out_shape=jax.ShapeDtypeStruct((NT, CH, D), BF),
        scratch_shapes=[
            pltpu.VMEM((NT, CH, D), BF),
            pltpu.VMEM((CH, D), BF),
            pltpu.SemaphoreType.DMA((4, NT)),
        ],
        compiler_params=params(collective_id=1, has_side_effects=True),
        name="sum_tensor",
    )(part.reshape(NT, CH, D)).reshape(NR, D)


def to_experts_kernel(outbox, result, sems):
    barrier, count = greet(dp=True)
    me = lax.axis_index("dp")
    result[me] = outbox[me]
    pl.semaphore_wait(barrier, count)
    copies = []
    for step in range(1, NDP):
        peer = (me + step) % NDP
        copies.append(
            send(outbox.at[peer], result.at[me], sems.at[0, step], sems.at[1, step], "dp", peer)
        )
    for copy in copies:
        copy.wait()


def to_experts(outbox):
    return pl.pallas_call(
        to_experts_kernel,
        in_specs=[pl.BlockSpec(memory_space=pltpu.VMEM)],
        out_specs=pl.BlockSpec(memory_space=pltpu.VMEM),
        out_shape=jax.ShapeDtypeStruct((NDP, 2 * SL, D), BF),
        scratch_shapes=[pltpu.SemaphoreType.DMA((2, NDP))],
        compiler_params=params(collective_id=2, has_side_effects=True),
        name="to_experts",
    )(outbox.reshape(NDP, 2 * SL, D))


def to_tokens_kernel(part, result, held, mine, sums, copies_sems):
    barrier, count = greet(tensor=True, dp=True)
    pl.semaphore_wait(barrier, count)
    me = lax.axis_index("tensor")
    home = lax.axis_index("dp")
    group = home // 4
    scattered = []
    for turn in range(4):
        block = ((group + turn + 1) % 4) * 4
        for step in range(1, NT):
            peer = (me + step) % NT
            scattered.append(
                send(
                    part.at[peer, pl.ds(block, 4)],
                    held.at[me, pl.ds(block, 4)],
                    sums.at[0, turn, step],
                    sums.at[1, turn, step],
                    "tensor",
                    peer,
                )
            )
    returned = []
    for turn in range(4):
        block = ((group + turn + 1) % 4) * 4
        for step in range(1, NT):
            scattered[turn * 3 + step - 1].wait_recv()
        total = part[me, pl.ds(block, 4)].astype(F32)
        for step in range(1, NT):
            total = total + held[(me + step) % NT, pl.ds(block, 4)].astype(F32)
        mine[pl.ds(block, 4)] = total.astype(BF)
        for number in range(4):
            if turn < 3:
                offset = (turn + 1) * 4 + number
                peer = block + (home + number) % 4
                returned.append((offset, peer))
            elif number > 0:
                offset = number
                peer = block + (home + number) % 4
                returned.append((offset, peer))
            else:
                result[home] = mine[home]
                continue
            returned[-1] = send(
                mine.at[peer],
                result.at[home],
                copies_sems.at[0, offset],
                copies_sems.at[1, offset],
                "dp",
                peer,
            )
    for copy in returned:
        copy.wait()
    for copy in scattered:
        copy.wait_send()


def to_tokens(part):
    return pl.pallas_call(
        to_tokens_kernel,
        in_specs=[pl.BlockSpec(memory_space=pltpu.VMEM)],
        out_specs=pl.BlockSpec(memory_space=pltpu.VMEM),
        out_shape=jax.ShapeDtypeStruct((NDP, SL, 2 * Q), BF),
        scratch_shapes=[
            pltpu.VMEM((NT, NDP, SL, 2 * Q), BF),
            pltpu.VMEM((NDP, SL, 2 * Q), BF),
            pltpu.SemaphoreType.DMA((2, 4, NT)),
            pltpu.SemaphoreType.DMA((2, NDP)),
        ],
        compiler_params=params(collective_id=3, has_side_effects=True),
        name="to_tokens",
    )(part.reshape(NT, NDP, SL, 2 * Q)).reshape(NDP * SL, 2 * Q)


def gather_over_tensor(source, result, sems, row):
    me = lax.axis_index("tensor")
    copies = []
    for step in range(1, NT):
        peer = (me + step) % NT
        copies.append(
            send(
                source, result.at[me], sems.at[row, step], sems.at[row + 1, step], "tensor", peer
            )
        )
    return copies


def next_stage_kernel(packed, result, near, chosen, sems):
    barrier, count = greet(tensor=True, pipe=True)
    pl.semaphore_wait(barrier, count)
    stage = lax.axis_index("pipe")
    across = send(packed, near, sems.at[0, 0], sems.at[1, 0], "pipe", 1 - stage)
    across.wait_recv()
    chosen[...] = jnp.where(stage == 0, packed[...], near[...])
    copies = gather_over_tensor(chosen, result, sems, 0)
    result[lax.axis_index("tensor")] = chosen[...]
    for copy in copies:
        copy.wait()
    across.wait_send()


def next_stage(packed):
    return pl.pallas_call(
        next_stage_kernel,
        in_specs=[pl.BlockSpec(memory_space=pltpu.VMEM)],
        out_specs=pl.BlockSpec(memory_space=pltpu.VMEM),
        out_shape=jax.ShapeDtypeStruct((NT, R, 2 * Q), BF),
        scratch_shapes=[
            pltpu.VMEM((R, 2 * Q), BF),
            pltpu.VMEM((R, 2 * Q), BF),
            pltpu.SemaphoreType.DMA((2, NT)),
        ],
        compiler_params=params(collective_id=4, has_side_effects=True),
        name="next_stage",
    )(packed)


def gather_kernel(packed, dpicks, result, dpicks_all, sems):
    barrier, count = greet(tensor=True)
    pl.semaphore_wait(barrier, count)
    me = lax.axis_index("tensor")
    copies = gather_over_tensor(packed, result, sems, 0)
    copies += gather_over_tensor(dpicks, dpicks_all, sems, 2)
    result[me] = packed[...]
    dpicks_all[me] = dpicks[...]
    for copy in copies:
        copy.wait()


def gather(packed, dpicks):
    return pl.pallas_call(
        gather_kernel,
        in_specs=[pl.BlockSpec(memory_space=pltpu.VMEM)] * 2,
        out_specs=[pl.BlockSpec(memory_space=pltpu.VMEM)] * 2,
        out_shape=[
            jax.ShapeDtypeStruct((NT, R, 2 * Q), BF),
            jax.ShapeDtypeStruct((NT, 8, 512), F32),
        ],
        scratch_shapes=[pltpu.SemaphoreType.DMA((4, NT))],
        compiler_params=params(collective_id=5, has_side_effects=True),
        name="gather",
    )(packed, dpicks)


def state_grad_kernel(
    piped, part, dx1, state, gain, result, chunk, gains, held, near, chosen, own, sems
):
    barrier, count = greet(tensor=True, pipe=piped)
    pl.semaphore_wait(barrier, count)
    me = lax.axis_index("tensor")
    stage = lax.axis_index("pipe")
    copies = []
    for step in range(1, NT):
        peer = (me + step) % NT
        copies.append(
            send(part.at[peer], held.at[me], sems.at[0, step], sems.at[1, step], "tensor", peer)
        )
    normal, inverse = norm_parts(state[me].astype(F32))
    for copy in copies:
        copy.wait()
    dz1 = add_up(part[me], held, me, NT)
    chunk[...] = (dx1[me] + norm_back(dz1, gain[...], normal, inverse)).astype(BF)
    if piped:
        across = send(chunk, near, sems.at[0, 0], sems.at[1, 0], "pipe", 1 - stage)
    own[...] = jnp.broadcast_to(jnp.sum(dz1 * normal, axis=0, keepdims=True), (8, D))
    small = gather_over_tensor(own, gains, sems, 2)
    gains[me] = own[...]
    if piped:
        across.wait_recv()
        chosen[...] = jnp.where(stage == 1, chunk[...], near[...])
    else:
        chosen[...] = chunk[...]
    copies = gather_over_tensor(chosen, result, sems, 4)
    result[me] = chosen[...]
    for copy in copies + small:
        copy.wait()
    if piped:
        across.wait_send()


def state_grad(piped, part, dx1, state, gain):
    result, chunk, gains = pl.pallas_call(
        functools.partial(state_grad_kernel, piped),
        in_specs=[pl.BlockSpec(memory_space=pltpu.VMEM)] * 4,
        out_specs=[pl.BlockSpec(memory_space=pltpu.VMEM)] * 3,
        out_shape=[
            jax.ShapeDtypeStruct((NT, CH, D), BF),
            jax.ShapeDtypeStruct((CH, D), BF),
            jax.ShapeDtypeStruct((NT, 8, D), F32),
        ],
        scratch_shapes=[
            pltpu.VMEM((NT, CH, D), BF),
            pltpu.VMEM((CH, D), BF),
            pltpu.VMEM((CH, D), BF),
            pltpu.VMEM((8, D), F32),
            pltpu.SemaphoreType.DMA((6, NT)),
        ],
        compiler_params=params(collective_id=6 if piped else 7, has_side_effects=True),
        name="state_grad",
    )(part.reshape(NT, CH, D), dx1.reshape(NT, CH, D), state.reshape(NT, CH, D), gain)
    return result.reshape(NR, D), chunk, gains


GR = D // NDP


def sum_dp_kernel(part, result, held, mine, sems):
    barrier, count = greet(dp=True)
    pl.semaphore_wait(barrier, count)
    me = lax.axis_index("dp")
    copies = []
    for step in range(1, NDP):
        peer = (me + step) % NDP
        copies.append(
            send(part.at[peer], held.at[me], sems.at[0, step], sems.at[1, step], "dp", peer)
        )
    for copy in copies:
        copy.wait()
    mine[...] = add_up(part[me], held, me, NDP).astype(BF)
    copies = []
    for step in range(1, NDP):
        peer = (me + step) % NDP
        copies.append(send(mine, result.at[me], sems.at[2, step], sems.at[3, step], "dp", peer))
    result[me] = mine[...]
    for copy in copies:
        copy.wait()


def sum_dp(part):
    return pl.pallas_call(
        sum_dp_kernel,
        in_specs=[pl.BlockSpec(memory_space=pltpu.VMEM)],
        out_specs=pl.BlockSpec(memory_space=pltpu.VMEM),
        out_shape=jax.ShapeDtypeStruct((NDP, GR, GP), BF),
        scratch_shapes=[
            pltpu.VMEM((NDP, GR, GP), BF),
            pltpu.VMEM((GR, GP), BF),
            pltpu.SemaphoreType.DMA((4, NDP)),
        ],
        compiler_params=params(collective_id=8, has_side_effects=True),
        name="sum_dp",
    )(part.reshape(NDP, GR, GP)).reshape(D, GP)


def pad_rows(values):
    micro, _, width = values.shape
    values = values.reshape(micro, 2, IMG_LEN, width)
    return jnp.pad(values, ((0, 0), (0, 0), (0, R - IMG_LEN), (0, 0))).reshape(micro, NR, width)


def unpad_rows(values):
    lead = values.shape[:-2]
    width = values.shape[-1]
    values = values.reshape(*lead, 2, R, width)[..., :IMG_LEN, :]
    return values.reshape(*lead, 2 * IMG_LEN, width)


def unpack_rows(gathered_parts):
    micro = gathered_parts.shape[1]
    values = gathered_parts[:, :, :IMG_LEN].reshape(NT, micro, IMG_LEN, 2, Q)
    return values.transpose(1, 3, 2, 0, 4).reshape(micro, 2 * IMG_LEN, D)


def body(
    tokens,
    cotangent,
    image_counts,
    routes,
    attn_norm_gain,
    query_key_value,
    attn_output,
    moe_norm_gain,
    router_weight,
    expert_in,
    expert_down,
):
    gain_one = attn_norm_gain
    gain_two = moe_norm_gain
    project = query_key_value[0].reshape(D, 3 * GW)
    output = attn_output[0]
    router = router_weight[0]
    first, second = expert_in[0], expert_down[0]
    stage = lax.axis_index("pipe")
    early = stage == 0
    counts = image_counts[:, lax.axis_index("dp")].reshape(2, 1, 1)
    plain = pad_rows(tokens)
    upstream = pad_rows(cotangent)
    paths = pad_rows(routes)

    def chosen(one, other):
        return jax.tree.map(lambda a, b: jnp.where(early, a, b), one, other)

    saved = []
    packed_list = []
    arriving = None
    for moment in range(3):
        if moment == 0:
            mode, inputs = "plain", (plain[0],)
            count, path = counts[0], paths[0]
        elif moment == 1:
            mode, inputs = "mixed", (plain[1], arriving)
            count, path = chosen((counts[1], paths[1]), (counts[0], paths[0]))
        else:
            mode, inputs = "packed", (arriving,)
            count, path = counts[1], paths[1]
        results = attention_forward(mode, inputs, gain_one, project, output)
        part, qkv, ctx = results[:3]
        state = inputs[0] if mode == "plain" else results[3]
        outbox, x1, meta = dispatch(count, state, sum_tensor(part), gain_two, router, path)
        arrived = to_experts(outbox)
        returned = to_tokens(experts_forward(arrived, first, second))
        packed, pieces = combine(returned, x1, meta)
        packed_list.append(packed)
        saved.append((state, qkv, ctx, x1, meta, arrived, pieces))
        if moment < 2:
            arriving = next_stage(packed)

    late_stored = [saved[1], chosen(saved[0], saved[2]), saved[1]]
    terms = []
    chunks = []
    gathered_grads = []
    arriving = None
    for moment in range(3):
        state, qkv, ctx, x1, meta, arrived, pieces = late_stored[moment]
        if moment == 0:
            delta = upstream[0]
        elif moment == 1:
            delta = jnp.where(early, arriving, upstream[1])
        else:
            delta = arriving
        delta_arrived = to_experts(spread(delta, meta))
        part, hidden, dpre = experts_backward(arrived, delta_arrived, first, second)
        returned = to_tokens(part)
        packed, dpicks = collect(returned, meta, pieces, delta)
        packed, dpicks = gather(packed, dpicks)
        part, dx1, grads, grad_gain_two = layer_backward(
            packed, dpicks, delta, x1, meta, gain_two, router, state, gain_one, qkv, ctx, project,
            output,
        )
        arriving, chunk, grad_gain_one = state_grad(moment < 2, part, dx1, state, gain_one)
        gathered_grads.append(arriving)
        chunks.append(chunk)
        terms.append(
            (
                (grads, grad_gain_two[0], grad_gain_one[:, 0].sum(axis=0)),
                (arrived, dpre, hidden, delta_arrived),
            )
        )
    ends = chosen(terms[2], terms[0])
    grads, grad_gain_two, grad_gain_one = jax.tree.map(jnp.add, terms[1][0], ends[0])
    pairs = [half for pair in zip(terms[1][1], ends[1]) for half in pair]
    grad_first, grad_second = expert_grads(*pairs)
    columns = jnp.stack([grad_gain_two, grad_gain_one], axis=1)
    whole = jnp.concatenate([grads[:, :800], columns, grads[:, 802:]], axis=1)
    whole = sum_dp(whole.astype(BF)).astype(F32)

    late_packed = jnp.stack([chosen(packed_list[0], packed_list[1]), chosen(packed_list[1], packed_list[2])])
    section_out = unpack_rows(lax.all_gather(late_packed, "tensor"))
    own = lax.all_gather(chunks[1], "tensor").reshape(NR, D)
    input_grad = unpad_rows(
        jnp.stack(
            [jnp.where(early, own, gathered_grads[0]), jnp.where(early, gathered_grads[2], gathered_grads[1])]
        )
    )
    return (
        section_out[None],
        input_grad[None],
        whole[:, 801][None],
        whole[:, :576].reshape(1, D, 3, GW),
        whole[:, 576:768].T[None],
        whole[:, 800][None],
        whole[:, 768:800][None],
        grad_first[None],
        grad_second[None],
    )


def solution(mesh):
    placed = (
        P(None, "dp", None),
        P(None, "dp", None),
        P(),
        P(None, "dp", None),
        P("pipe", None),
        P("pipe", None, None, "tensor"),
        P("pipe", "tensor", None),
        P("pipe", None),
        P("pipe", None, None),
        P("pipe", "dp", None, "tensor"),
        P("pipe", "dp", "tensor", None),
    )
    return jax.shard_map(
        body,
        mesh=mesh,
        in_specs=placed,
        out_specs=(
            P("pipe", None, "dp", None),
            P("pipe", None, "dp", None),
            P("pipe", None),
            P("pipe", None, None, "tensor"),
            P("pipe", "tensor", None),
            P("pipe", None),
            P("pipe", None, None),
            P("pipe", "dp", None, "tensor"),
            P("pipe", "dp", "tensor", None),
        ),
        check_vma=False,
    )
```

time: 1560 us -> 772 us (0.49)
  Pallas kernels: 0 us -> 672 us
  waiting for transfers between devices: 515 us -> 0.02 us
  local copies, waits for them, and re-layouts: 435 us -> 47.7 us
  other arithmetic: 228 us -> 14 us
  matrix products: 130 us -> 0 us
  blocking collectives: 121 us -> 12.2 us
  starting transfers between devices: 96.2 us -> 0.04 us
    pallas_call x0 -> x49, Pallas kernels: none -> 672 us  [the longest x6 166 us: to_tokens(): pl.pallas_call(to_tokens_kernel, in_specs=[pl.BlockSpec(memory_space=pltp...]
    psum x12 -> x0, waiting for transfers between devices: 423 us -> none  [the longest x5 177 us: to_tokens(): lax.psum(partial_value.astype(jnp.bfloat16), 'tensor').astype(jnp.float32)]
    dot_general x66 -> x0, matrix products: 130 us -> none  [the longest x3 19 us: experts_backward(): jnp.einsum('erf,erd->efd', hidden, grad_received, preferred_element_type=...]
    all_to_all x10 -> x0, starting transfers between devices: 84.4 us -> none  [the longest x6 46.2 us: to_tokens(): lax.all_to_all(summed.astype(jnp.bfloat16), 'dp', split_axis=1, concat_ax...]
    reduce_sum x48 -> x2, other arithmetic: 72.9 us -> 0.05 us  [body(): grad_gain_one[:, 0].sum(axis=0)]
    all_to_all x10 -> x0, waiting for transfers between devices: 64.5 us -> none  [the longest x6 45.5 us: to_tokens(): lax.all_to_all(summed.astype(jnp.bfloat16), 'dp', split_axis=1, concat_ax...]
    gather x12 -> x0, local copies, waits for them, and re-layouts: 63.7 us -> none  [the longest x6 32 us: experts_forward(): pieces = returned.reshape(experts * capacity, model_width)[slot_index]]
    all_to_all x2 -> x0, blocking collectives: 61.6 us -> none  [to_experts(): return lax.all_to_all(outbox, 'dp', split_axis=0, concat_axis=1, tiled=True)]
  transfers between devices with their start and end apart: 26 -> 1, of which waited for: 24 -> 0; matrix products, arithmetic and copies ran while one was open for 21% -> 4% of each run, Pallas kernels for 0% -> 50%
where the time goes in v1:
time: 772 us; the launch traced here: 763 us
  Pallas kernels  672 us (87%)
  local copies, waits for them, and re-layouts  47.7 us (6%)
  between operations  16.8 us (2%)
  other arithmetic  14 us (2%)
  blocking collectives  12.2 us (2%)
    pallas_call x6, Pallas kernels, to_tokens(): pl.pallas_call(to_tokens_kernel, in_specs=[pl.BlockSpec(memory_space=pltp...  166 us
    pallas_call x6, Pallas kernels, to_experts(): pl.pallas_call(to_experts_kernel, in_specs=[pl.BlockSpec(memory_space=plt...  146 us
    pallas_call x3, Pallas kernels, state_grad(): pl.pallas_call(functools.partial(state_grad_kernel, piped), in_specs=[pl....  71.4 us
    pallas_call x3, Pallas kernels, sum_tensor(): pl.pallas_call(sum_tensor_kernel, in_specs=[pl.BlockSpec(memory_space=plt...  64.4 us
    pallas_call x1, Pallas kernels, sum_dp(): pl.pallas_call(sum_dp_kernel, in_specs=[pl.BlockSpec(memory_space=pltpu.V...  42 us
    pallas_call x3, Pallas kernels, gather(): pl.pallas_call(gather_kernel, in_specs=[pl.BlockSpec(memory_space=pltpu.V...  35.1 us
    pallas_call x3, Pallas kernels, layer_backward(): pl.pallas_call(layer_backward_kernel, out_shape=[jax.ShapeDtypeStruct((NR...  33.7 us
    pallas_call x2, Pallas kernels, next_stage(): pl.pallas_call(next_stage_kernel, in_specs=[pl.BlockSpec(memory_space=plt...  30.4 us
  transfers between devices with their start and end apart: 1, of which 0 were waited for; matrix products, arithmetic and copies ran while one was open for 4% of the time, Pallas kernels for 50%

profile of v1, /device:TPU:7, one launch (start us, length us, event | category | flops | bytes accessed | tf_op | source)
XLA Modules:
  0.0 762.8 jit_solution(18259820758820590555)
XLA Ops:
  17.1 21.5 %sum_tensor.3 = bf16[4,112,768]{2,1,0:T(8,128)(2,1)S(1)} custom-call(bf16[4,112,768]{2,1,0:T(8,128)(2,1)S(1)} %bitcast.143), custom_call_target="tpu_custom_call" | custom-call | tf_op jit(solution)/shard_map/sum_tensor/pallas_call | solution.py:499
  41.6 27.1 %to_experts.6.arrived = bf16[16,64,768]{2,1,0:T(8,128)(2,1)S(1)} custom-call(bf16[16,64,768]{2,1,0:T(8,128)(2,1)S(1)} %bitcast.125), custom_call_target="tpu_custom_call" | custom-call | tf_op jit(solution)/shard_map/to_experts/pallas_call | solution.py:530
  74.3 27.4 %to_tokens.6 = bf16[16,32,384]{2,1,0:T(8,128)(2,1)S(1)} custom-call(bf16[4,16,32,384]{3,2,1,0:T(8,128)(2,1)S(1)} %bitcast.113), custom_call_target="tpu_custom_call" | custom-call | tf_op jit(solution)/shard_map/to_tokens/pallas_call | solution.py:598
  103.9 15.0 %next_stage.2.refs_1_ = bf16[4,224,384]{2,1,0:T(8,128)(2,1)S(1)} custom-call(bf16[224,384]{1,0:T(8,128)(2,1)S(1)} %get-tuple-element.81.packed), custom_call_target="tpu_custom_call" | custom-call | tf_op jit(solution)/shard_map/next_stage/pallas_call | solution.py:642
  122.0 21.5 %sum_tensor.4 = bf16[4,112,768]{2,1,0:T(8,128)(2,1)S(1)} custom-call(bf16[4,112,768]{2,1,0:T(8,128)(2,1)S(1)} %bitcast.141), custom_call_target="tpu_custom_call" | custom-call | tf_op jit(solution)/shard_map/sum_tensor/pallas_call | solution.py:499
  147.1 23.8 %to_experts.7.arrived.a1 = bf16[16,64,768]{2,1,0:T(8,128)(2,1)S(1)} custom-call(bf16[16,64,768]{2,1,0:T(8,128)(2,1)S(1)} %bitcast.123), custom_call_target="tpu_custom_call" | custom-call | tf_op jit(solution)/shard_map/to_experts/pallas_call | solution.py:530
  176.6 27.4 %to_tokens.7 = bf16[16,32,384]{2,1,0:T(8,128)(2,1)S(1)} custom-call(bf16[4,16,32,384]{3,2,1,0:T(8,128)(2,1)S(1)} %bitcast.114), custom_call_target="tpu_custom_call" | custom-call | tf_op jit(solution)/shard_map/to_tokens/pallas_call | solution.py:598
  207.0 15.3 %next_stage.3.refs_0_ = bf16[4,224,384]{2,1,0:T(8,128)(2,1)S(1)} custom-call(bf16[224,384]{1,0:T(8,128)(2,1)S(1)} %get-tuple-element.87.packed), custom_call_target="tpu_custom_call" | custom-call | tf_op jit(solution)/shard_map/next_stage/pallas_call | solution.py:642
  225.4 21.5 %sum_tensor.5 = bf16[4,112,768]{2,1,0:T(8,128)(2,1)S(1)} custom-call(bf16[4,112,768]{2,1,0:T(8,128)(2,1)S(1)} %bitcast.142), custom_call_target="tpu_custom_call" | custom-call | tf_op jit(solution)/shard_map/sum_tensor/pallas_call | solution.py:499
  249.8 23.9 %to_experts.8.arrived = bf16[16,64,768]{2,1,0:T(8,128)(2,1)S(1)} custom-call(bf16[16,64,768]{2,1,0:T(8,128)(2,1)S(1)} %bitcast.124), custom_call_target="tpu_custom_call" | custom-call | tf_op jit(solution)/shard_map/to_experts/pallas_call | solution.py:530
  279.6 27.4 %to_tokens.8 = bf16[16,32,384]{2,1,0:T(8,128)(2,1)S(1)} custom-call(bf16[4,16,32,384]{3,2,1,0:T(8,128)(2,1)S(1)} %bitcast.115), custom_call_target="tpu_custom_call" | custom-call | tf_op jit(solution)/shard_map/to_tokens/pallas_call | solution.py:598
  319.6 23.5 %to_experts.9.delta = bf16[16,64,768]{2,1,0:T(8,128)(2,1)S(1)} custom-call(bf16[16,64,768]{2,1,0:T(8,128)(2,1)S(1)} %bitcast.110), custom_call_target="tpu_custom_call" | custom-call | tf_op jit(solution)/shard_map/to_experts/pallas_call | solution.py:530
  344.3 7.3 experts_backward.3
  352.8 27.9 %to_tokens.9 = bf16[16,32,384]{2,1,0:T(8,128)(2,1)S(1)} custom-call(bf16[4,16,32,384]{3,2,1,0:T(8,128)(2,1)S(1)} %bitcast.126), custom_call_target="tpu_custom_call" | custom-call | tf_op jit(solution)/shard_map/to_tokens/pallas_call | solution.py:598
  382.6 11.7 %gather.3 = (bf16[4,224,384]{2,1,0:T(8,128)(2,1)S(1)}, f32[4,8,512]{2,1,0:T(8,128)S(1)}) custom-call(bf16[224,384]{1,0:T(8,128)(2,1)S(1)} %get-tuple-element.96.packed, f32[8,512]{1,0:T(8,128)S(1)} %get-tuple-element.97.dpicks), custom_call_target="tpu_custom_call" | custom-call | tf_op jit(solution)/shard_map/gather/pallas_call | solution.py:670
  394.3 11.2 %layer_backward.3 = (bf16[448,768]{1,0:T(8,128)(2,1)S(1)}, f32[448,768]{1,0:T(8,128)}, f32[768,896]{1,0:T(8,128)}, f32[8,768]{1,0:T(8,128)S(1)}) custom-call(bf16[4,224,384]{2,1,0:T(8,128)(2,1)S(1)} %get-tuple-element.98.packed, f32[4,8,512]{2,1,0:T(8,128)S(1)} %get-tuple-element.99.dpicks, bf16[448,768]{1,0:T(8,128)(2,1)S(1)} %bitcast.95, ...), custom_call_target="tpu_custom_call" | custom-call | tf_op jit(solution)/shard_map/layer_backward/pallas_call | solution.py:426
  406.9 25.5 %state_grad.3 = (bf16[4,112,768]{2,1,0:T(8,128)(2,1)S(1)}, bf16[112,768]{1,0:T(8,128)(2,1)}, f32[4,8,768]{2,1,0:T(8,128)S(1)}) custom-call(bf16[4,112,768]{2,1,0:T(8,128)(2,1)S(1)} %bitcast.140, f32[4,112,768]{2,1,0:T(8,128)S(1)} %bitcast.137, bf16[4,112,768]{2,1,0:T(8,128)(2,1)S(1)} %bitcast.88, f32[1,768]{1,0:T(1,128)S(1)} %copy-done.63), custom_call_target="tpu_custom_call" | custom-call | tf_op jit(solution)/shard_map/state_grad/pallas_call | solution.py:721
  435.2 23.8 %to_experts.10.delta.d0 = bf16[16,64,768]{2,1,0:T(8,128)(2,1)S(1)} custom-call(bf16[16,64,768]{2,1,0:T(8,128)(2,1)S(1)} %bitcast.111), custom_call_target="tpu_custom_call" | custom-call | tf_op jit(solution)/shard_map/to_experts/pallas_call | solution.py:530
  460.2 7.1 experts_backward.4
  468.5 28.0 %to_tokens.10 = bf16[16,32,384]{2,1,0:T(8,128)(2,1)S(1)} custom-call(bf16[4,16,32,384]{3,2,1,0:T(8,128)(2,1)S(1)} %bitcast.127), custom_call_target="tpu_custom_call" | custom-call | tf_op jit(solution)/shard_map/to_tokens/pallas_call | solution.py:598
  499.6 11.7 %gather.4 = (bf16[4,224,384]{2,1,0:T(8,128)(2,1)S(1)}, f32[4,8,512]{2,1,0:T(8,128)S(1)}) custom-call(bf16[224,384]{1,0:T(8,128)(2,1)S(1)} %get-tuple-element.108.packed, f32[8,512]{1,0:T(8,128)S(1)} %get-tuple-element.109.dpicks), custom_call_target="tpu_custom_call" | custom-call | tf_op jit(solution)/shard_map/gather/pallas_call | solution.py:670
  511.3 11.2 %layer_backward.4 = (bf16[448,768]{1,0:T(8,128)(2,1)S(1)}, f32[448,768]{1,0:T(8,128)}, f32[768,896]{1,0:T(8,128)}, f32[8,768]{1,0:T(8,128)S(1)}) custom-call(bf16[4,224,384]{2,1,0:T(8,128)(2,1)S(1)} %get-tuple-element.110.packed, f32[4,8,512]{2,1,0:T(8,128)S(1)} %get-tuple-element.111.dpicks, bf16[448,768]{1,0:T(8,128)(2,1)S(1)} %bitcast_select_fusion.delta, ...), custom_call_target="tpu_custom_call" | custom-call | tf_op jit(solution)/shard_map/layer_backward/pallas_call | solution.py:426
  523.9 25.9 %state_grad.4 = (bf16[4,112,768]{2,1,0:T(8,128)(2,1)S(1)}, bf16[112,768]{1,0:T(8,128)(2,1)S(1)}, f32[4,8,768]{2,1,0:T(8,128)S(1)}) custom-call(bf16[4,112,768]{2,1,0:T(8,128)(2,1)S(1)} %bitcast.139, f32[4,112,768]{2,1,0:T(8,128)S(1)} %bitcast.136, bf16[4,112,768]{2,1,0:T(8,128)(2,1)S(1)} %bitcast.116, f32[1,768]{1,0:T(1,128)S(1)} %copy-done.63), custom_call_target="tpu_custom_call" | custom-call | tf_op jit(solution)/shard_map/state_grad/pallas_call | solution.py:721
  552.2 23.6 %to_experts.11.delta = bf16[16,64,768]{2,1,0:T(8,128)(2,1)S(1)} custom-call(bf16[16,64,768]{2,1,0:T(8,128)(2,1)S(1)} %bitcast.112), custom_call_target="tpu_custom_call" | custom-call | tf_op jit(solution)/shard_map/to_experts/pallas_call | solution.py:530
  577.0 7.1 experts_backward.5
  585.3 28.1 %to_tokens.11 = bf16[16,32,384]{2,1,0:T(8,128)(2,1)S(1)} custom-call(bf16[4,16,32,384]{3,2,1,0:T(8,128)(2,1)S(1)} %bitcast.128), custom_call_target="tpu_custom_call" | custom-call | tf_op jit(solution)/shard_map/to_tokens/pallas_call | solution.py:598
  615.3 11.7 %gather.5 = (bf16[4,224,384]{2,1,0:T(8,128)(2,1)S(1)}, f32[4,8,512]{2,1,0:T(8,128)S(1)}) custom-call(bf16[224,384]{1,0:T(8,128)(2,1)S(1)} %get-tuple-element.121.packed, f32[8,512]{1,0:T(8,128)S(1)} %get-tuple-element.122.dpicks), custom_call_target="tpu_custom_call" | custom-call | tf_op jit(solution)/shard_map/gather/pallas_call | solution.py:670
  627.0 11.2 %layer_backward.5 = (bf16[448,768]{1,0:T(8,128)(2,1)S(1)}, f32[448,768]{1,0:T(8,128)}, f32[768,896]{1,0:T(8,128)}, f32[8,768]{1,0:T(8,128)S(1)}) custom-call(bf16[4,224,384]{2,1,0:T(8,128)(2,1)S(1)} %get-tuple-element.123.packed, f32[4,8,512]{2,1,0:T(8,128)S(1)} %get-tuple-element.124.dpicks, bf16[448,768]{1,0:T(8,128)(2,1)S(1)} %bitcast.92, ...), custom_call_target="tpu_custom_call" | custom-call | tf_op jit(solution)/shard_map/layer_backward/pallas_call | solution.py:426
  639.5 19.9 %state_grad.5 = (bf16[4,112,768]{2,1,0:T(8,128)(2,1)S(1)}, bf16[112,768]{1,0:T(8,128)(2,1)}, f32[4,8,768]{2,1,0:T(8,128)S(1)}) custom-call(bf16[4,112,768]{2,1,0:T(8,128)(2,1)S(1)} %bitcast.138, f32[4,112,768]{2,1,0:T(8,128)S(1)} %bitcast.135, bf16[4,112,768]{2,1,0:T(8,128)(2,1)S(1)} %bitcast.89, f32[1,768]{1,0:T(1,128)S(1)} %copy-done.63), custom_call_target="tpu_custom_call" | custom-call | tf_op jit(solution)/shard_map/state_grad/pallas_call | solution.py:721
  663.6 42.0 %sum_dp.1 = bf16[16,48,896]{2,1,0:T(8,128)(2,1)S(1)} custom-call(bf16[16,48,896]{2,1,0:T(8,128)(2,1)S(1)} %pad_maximum_fusion.part), custom_call_target="tpu_custom_call" | custom-call | tf_op jit(solution)/shard_map/sum_dp/pallas_call | solution.py:769
  708.8 12.2 %all-gather.1 = bf16[448,768]{1,0:T(8,128)(2,1)S(1)} all-gather(bf16[112,768]{1,0:T(8,128)(2,1)S(1)} %copy-done.69), channel_id=3, replica_groups=mesh['pipe'=2,'tensor'=4,'dp'=16] {'tensor'}, dimensions={0}, use_global_device_ids=true | all-gather | bytes 860160 | tf_op jit(solution)/shard_map/all_gather | solution.py:898
  740.2 9.0 %expert_grads.1 = (f32[2,768,768]{2,1,0:T(8,128)}, f32[2,768,768]{2,1,0:T(8,128)}) custom-call(bf16[16,64,768]{2,1,0:T(8,128)(2,1)S(1)} %copy-done.7, bf16[16,64,768]{2,1,0:T(8,128)(2,1)S(1)} %copy-done.4, bf16[16,64,768]{2,1,0:T(8,128)(2,1)S(1)} %copy-done.42, bf16[16,64,768]{2,1,0:T(8,128)(2,1)} %broadcast_select_fusion.2.b1, ...), custom_call_target="tpu_custom_call" | custom-call | tf_op jit(solution)/shard_map/expert_grads/pallas_call | solution.py:275
  (221 shorter events, 114.5 us)
Async XLA Ops:
  7.2 742.0 %all-gather.4.cloned.1.call-start = ((), (), s32[]{:S(2)}) async-start(), calls=%async_computation | async-start | bytes 1720320 | tf_op jit(solution)/shard_map/all_gather | solution.py:897
  10.2 236.7 %copy-start.21 = (bf16[1,768,32]{2,1,0:T(8,128)(2,1)}, bf16[1,768,32]{2,1,0:T(8,128)(2,1)S(1)}, u32[]{:S(2)}) copy-start(bf16[1,768,32]{2,1,0:T(8,128)(2,1)S(1)} %copy.52) | copy-start | bytes 147460
  10.5 133.0 %copy-start.32 = (s32[1,2,224,2]{3,2,1,0:T(8,128)}, s32[1,2,224,2]{3,2,1,0:T(8,128)S(1)}, u32[]{:S(2)}) copy-start(s32[1,2,224,2]{3,2,1,0:T(8,128)S(1)} %get-tuple-element.169) | copy-start | bytes 10756
  13.6 25.0 %copy-start.17 = (bf16[1,2,224,768]{3,2,1,0:T(8,128)(2,1)}, bf16[1,2,224,768]{3,2,1,0:T(8,128)(2,1)S(1)}, u32[]{:S(2)}) copy-start(bf16[1,2,224,768]{3,2,1,0:T(8,128)(2,1)S(1)} %get-tuple-element.167) | copy-start | bytes 2064388
  17.1 24.4 %copy-start.55 = (bf16[448,576]{1,0:T(8,128)(2,1)}, bf16[448,576]{1,0:T(8,128)(2,1)S(1)}, u32[]{:S(2)}) copy-start(bf16[448,576]{1,0:T(8,128)(2,1)S(1)} %get-tuple-element.112) | copy-start | bytes 1548292
  17.1 24.4 %copy-start.64 = (bf16[448,192]{1,0:T(8,128)(2,1)}, bf16[448,192]{1,0:T(8,128)(2,1)S(1)}, u32[]{:S(2)}) copy-start(bf16[448,192]{1,0:T(8,128)(2,1)S(1)} %get-tuple-element.114) | copy-start | bytes 516100
  41.6 60.2 %copy-start.23 = (f32[448,768]{1,0:T(8,128)}, f32[448,768]{1,0:T(8,128)S(1)}, u32[]{:S(2)}) copy-start(f32[448,768]{1,0:T(8,128)S(1)} %get-tuple-element.79.x1) | copy-start | bytes 4128772
  41.6 60.2 %copy-start.49 = (f32[448,128]{1,0:T(8,128)}, f32[448,128]{1,0:T(8,128)S(1)}, u32[]{:S(2)}) copy-start(f32[448,128]{1,0:T(8,128)S(1)} %get-tuple-element.80.meta) | copy-start | bytes 688132
  41.6 27.1 %copy-start.2 = (bf16[1,2,768,768]{3,2,1,0:T(8,128)(2,1)S(1)}, bf16[1,2,768,768]{3,2,1,0:T(8,128)(2,1)}, u32[]{:S(2)}) copy-start(bf16[1,2,768,768]{3,2,1,0:T(8,128)(2,1)} %param.20) | copy-start | bytes 7077892
  122.0 25.1 %copy-start.5 = (bf16[448,768]{1,0:T(8,128)(2,1)}, bf16[448,768]{1,0:T(8,128)(2,1)S(1)}, u32[]{:S(2)}) copy-start(bf16[448,768]{1,0:T(8,128)(2,1)S(1)} %get-tuple-element.82.state) | copy-start | bytes 2064388
  122.0 25.1 %copy-start.30 = (bf16[448,576]{1,0:T(8,128)(2,1)}, bf16[448,576]{1,0:T(8,128)(2,1)S(1)}, u32[]{:S(2)}) copy-start(bf16[448,576]{1,0:T(8,128)(2,1)S(1)} %get-tuple-element.100.qkv) | copy-start | bytes 1548292
  147.1 56.9 %copy-start.16 = (f32[448,768]{1,0:T(8,128)}, f32[448,768]{1,0:T(8,128)S(1)}, u32[]{:S(2)}) copy-start(f32[448,768]{1,0:T(8,128)S(1)} %get-tuple-element.85.x1) | copy-start | bytes 4128772
  222.3 24.6 %copy-start.33 = (s32[1,2,224,2]{3,2,1,0:T(8,128)S(1)}, s32[1,2,224,2]{3,2,1,0:T(8,128)}, u32[]{:S(2)}) copy-start(s32[1,2,224,2]{3,2,1,0:T(8,128)} %copy-done.32) | copy-start | bytes 10756
  225.4 24.4 %copy-start.57 = (bf16[448,576]{1,0:T(8,128)(2,1)}, bf16[448,576]{1,0:T(8,128)(2,1)S(1)}, u32[]{:S(2)}) copy-start(bf16[448,576]{1,0:T(8,128)(2,1)S(1)} %get-tuple-element.113) | copy-start | bytes 1548292
  225.4 24.4 %copy-start.66 = (bf16[448,192]{1,0:T(8,128)(2,1)}, bf16[448,192]{1,0:T(8,128)(2,1)S(1)}, u32[]{:S(2)}) copy-start(bf16[448,192]{1,0:T(8,128)(2,1)S(1)} %get-tuple-element.115) | copy-start | bytes 516100
  225.4 54.1 %copy-start.29 = (bf16[448,768]{1,0:T(8,128)(2,1)}, bf16[448,768]{1,0:T(8,128)(2,1)S(1)}, u32[]{:S(2)}) copy-start(bf16[448,768]{1,0:T(8,128)(2,1)S(1)} %get-tuple-element.88.state) | copy-start | bytes 2064388
  249.8 57.2 %copy-start.25 = (f32[448,768]{1,0:T(8,128)}, f32[448,768]{1,0:T(8,128)S(1)}, u32[]{:S(2)}) copy-start(f32[448,768]{1,0:T(8,128)S(1)} %get-tuple-element.91.x1) | copy-start | bytes 4128772
  249.8 57.2 %copy-start.51 = (f32[448,128]{1,0:T(8,128)}, f32[448,128]{1,0:T(8,128)S(1)}, u32[]{:S(2)}) copy-start(f32[448,128]{1,0:T(8,128)S(1)} %get-tuple-element.92.meta) | copy-start | bytes 688132
  352.8 29.8 %copy-start.38 = (bf16[16,64,768]{2,1,0:T(8,128)(2,1)}, bf16[16,64,768]{2,1,0:T(8,128)(2,1)S(1)}, u32[]{:S(2)}) copy-start(bf16[16,64,768]{2,1,0:T(8,128)(2,1)S(1)} %get-tuple-element.139) | copy-start | bytes 4718596
  352.8 27.9 %copy-start.35 = (bf16[2,448,192]{2,1,0:T(8,128)(2,1)S(1)}, bf16[2,448,192]{2,1,0:T(8,128)(2,1)}, u32[]{:S(2)}) copy-start(bf16[2,448,192]{2,1,0:T(8,128)(2,1)} %copy-done.34) | copy-start | bytes 1032196
  352.8 41.5 %copy-start.6 = (bf16[448,768]{1,0:T(8,128)(2,1)S(1)}, bf16[448,768]{1,0:T(8,128)(2,1)}, u32[]{:S(2)}) copy-start(bf16[448,768]{1,0:T(8,128)(2,1)} %copy-done.5) | copy-start | bytes 2064388
  352.8 41.5 %copy-start.20 = (bf16[1,192,768]{2,1,0:T(8,128)(2,1)S(1)}, bf16[1,192,768]{2,1,0:T(8,128)(2,1)}, u32[]{:S(2)}) copy-start(bf16[1,192,768]{2,1,0:T(8,128)(2,1)} %param.17) | copy-start | bytes 884740
  352.8 41.5 %copy-start.22 = (bf16[1,768,32]{2,1,0:T(8,128)(2,1)S(1)}, bf16[1,768,32]{2,1,0:T(8,128)(2,1)}, u32[]{:S(2)}) copy-start(bf16[1,768,32]{2,1,0:T(8,128)(2,1)} %copy-done.21) | copy-start | bytes 147460
  352.8 41.5 %copy-start.31 = (bf16[448,576]{1,0:T(8,128)(2,1)S(1)}, bf16[448,576]{1,0:T(8,128)(2,1)}, u32[]{:S(2)}) copy-start(bf16[448,576]{1,0:T(8,128)(2,1)} %copy-done.30) | copy-start | bytes 1548292
  352.8 41.5 %copy-start.54 = (bf16[448,192]{1,0:T(8,128)(2,1)S(1)}, bf16[448,192]{1,0:T(8,128)(2,1)}, u32[]{:S(2)}) copy-start(bf16[448,192]{1,0:T(8,128)(2,1)} %copy-done.53) | copy-start | bytes 516100
  468.5 28.1 %copy-start.41 = (bf16[16,64,768]{2,1,0:T(8,128)(2,1)}, bf16[16,64,768]{2,1,0:T(8,128)(2,1)S(1)}, u32[]{:S(2)}) copy-start(bf16[16,64,768]{2,1,0:T(8,128)(2,1)S(1)} %get-tuple-element.137.b0) | copy-start | bytes 4718596
  468.5 28.0 %copy-start.65 = (bf16[448,192]{1,0:T(8,128)(2,1)S(1)}, bf16[448,192]{1,0:T(8,128)(2,1)}, u32[]{:S(2)}) copy-start(bf16[448,192]{1,0:T(8,128)(2,1)} %copy-done.64) | copy-start | bytes 516100
  468.5 28.0 %copy-start.67 = (bf16[448,192]{1,0:T(8,128)(2,1)S(1)}, bf16[448,192]{1,0:T(8,128)(2,1)}, u32[]{:S(2)}) copy-start(bf16[448,192]{1,0:T(8,128)(2,1)} %copy-done.66) | copy-start | bytes 516100
  468.5 28.1 %copy-start.56 = (bf16[448,576]{1,0:T(8,128)(2,1)S(1)}, bf16[448,576]{1,0:T(8,128)(2,1)}, u32[]{:S(2)}) copy-start(bf16[448,576]{1,0:T(8,128)(2,1)} %copy-done.55) | copy-start | bytes 1548292
  468.5 28.1 %copy-start.58 = (bf16[448,576]{1,0:T(8,128)(2,1)S(1)}, bf16[448,576]{1,0:T(8,128)(2,1)}, u32[]{:S(2)}) copy-start(bf16[448,576]{1,0:T(8,128)(2,1)} %copy-done.57) | copy-start | bytes 1548292
  549.8 26.0 %copy-start.68 = (bf16[112,768]{1,0:T(8,128)(2,1)}, bf16[112,768]{1,0:T(8,128)(2,1)S(1)}, u32[]{:S(2)}) copy-start(bf16[112,768]{1,0:T(8,128)(2,1)S(1)} %get-tuple-element.118) | copy-start | bytes 516100
  585.3 30.0 %copy-start.45 = (bf16[16,64,768]{2,1,0:T(8,128)(2,1)}, bf16[16,64,768]{2,1,0:T(8,128)(2,1)S(1)}, u32[]{:S(2)}) copy-start(bf16[16,64,768]{2,1,0:T(8,128)(2,1)S(1)} %get-tuple-element.138) | copy-start | bytes 4718596
  (44 other events, 183.7 us)
Sparse Core Ops, SparseCore 0:
  310.9 23.1 all-gather.3

commit v2 on v0

v2 whole, which is shorter than its diff:
```python
import functools

import jax
import jax.numpy as jnp
from jax import lax
from jax.experimental import pallas as pl
from jax.experimental.pallas import tpu as pltpu
from jax.sharding import PartitionSpec as P

BF = jnp.bfloat16
F32 = jnp.float32
MESH = pl.DeviceIdType.MESH
D = 768
HD = 64
NH = 3
GW = NH * HD
IMG_LEN = 197
R = 224
NR = 2 * R
CH = NR // 4
EXPERTS = 32
SL = 32
NT = 4
NDP = 16
Q = D // NT
EPSILON = 1e-06
VMEM_BYTES = 48 * 1024 * 1024
GP = 896


def dot(a, b, ca=1, cb=0):
    return lax.dot_general(a, b, (((ca,), (cb,)), ((), ())), preferred_element_type=F32)


def params(**more):
    return pltpu.CompilerParams(vmem_limit_bytes=VMEM_BYTES, **more)


def norm_parts(values):
    mean = jnp.mean(values, axis=-1, keepdims=True)
    centred = values - mean
    inverse = lax.rsqrt(jnp.mean(centred * centred, axis=-1, keepdims=True) + EPSILON)
    return centred * inverse, inverse


def norm_back(delta, gain, normal, inverse):
    scaled = delta * gain
    return inverse * (
        scaled
        - jnp.mean(scaled, axis=-1, keepdims=True)
        - normal * jnp.mean(scaled * normal, axis=-1, keepdims=True)
    )


def pick(index, options):
    result = options[0]
    for number in range(1, len(options)):
        result = jnp.where(index == number, options[number], result)
    return result


def column_quarter(values, member):
    return pick(member, [values[:, Q * q : Q * (q + 1)] for q in range(NT)])


def unpack(packed):
    images = [
        jnp.concatenate([packed[q][:, Q * i : Q * (i + 1)] for q in range(NT)], axis=1)
        for i in range(2)
    ]
    return jnp.concatenate(images, axis=0)


def head_parts(projected, image, head):
    rows = slice(image * R, (image + 1) * R)
    return [
        projected[rows, part * GW + head * HD : part * GW + (head + 1) * HD] for part in range(3)
    ]


def probabilities(queries, keys):
    scores = dot(queries, keys, 1, 1) * (HD**-0.5)
    held = lax.broadcasted_iota(jnp.int32, scores.shape, 1) < IMG_LEN
    scores = jnp.where(held, scores, -1e30)
    exponent = jnp.exp(scores - jnp.max(scores, axis=-1, keepdims=True))
    return exponent / jnp.sum(exponent, axis=-1, keepdims=True)


VMEM = pl.BlockSpec(memory_space=pltpu.VMEM)
SMEM = pl.BlockSpec(memory_space=pltpu.SMEM)
ANYWHERE = pl.BlockSpec(memory_space=pl.ANY)


class Part:
    def __init__(self, steps, inputs, outs, scratch, specs=None):
        self.steps = steps
        self.inputs = inputs
        self.outs = outs
        self.scratch = scratch
        self.specs = specs or [VMEM] * len(inputs)


def drive(running):
    running = list(running)
    while running:
        for steps in list(running):
            if next(steps, StopIteration) is StopIteration:
                running.remove(steps)


def greet(axes):
    barrier = pltpu.get_barrier_semaphore()
    count = 0
    for axis in axes:
        size = lax.axis_size(axis)
        me = lax.axis_index(axis)
        for step in range(1, size):
            pl.semaphore_signal(
                barrier, inc=1, device_id={axis: (me + step) % size}, device_id_type=MESH
            )
        count += size - 1
    return barrier, count


def run(name, number, axes, parts):
    def kernel(*refs):
        barrier, count = greet(axes)
        ins = sum(len(part.inputs) for part in parts)
        outs = sum(len(part.outs) for part in parts)
        place = [0, ins, ins + outs]
        running = []
        for part in parts:
            pieces = []
            for which, items in enumerate((part.inputs, part.outs, part.scratch)):
                pieces.append(refs[place[which] : place[which] + len(items)])
                place[which] += len(items)
            running.append(part.steps(*pieces))
        running = [steps for steps in running if next(steps, StopIteration) is not StopIteration]
        pl.semaphore_wait(barrier, count)
        drive(running)

    flat = [item for part in parts for item in part.inputs]
    results = pl.pallas_call(
        kernel,
        in_specs=[spec for part in parts for spec in part.specs],
        out_specs=[VMEM for part in parts for _ in part.outs],
        out_shape=[jax.ShapeDtypeStruct(*out) for part in parts for out in part.outs],
        scratch_shapes=[item for part in parts for item in part.scratch],
        compiler_params=params(collective_id=number, has_side_effects=True),
        name=name,
    )(*flat)
    split = []
    for part in parts:
        split.append(results[: len(part.outs)])
        results = results[len(part.outs) :]
    return split


def send(source, target, send_sem, recv_sem, axis, peer):
    copy = pltpu.make_async_remote_copy(
        src_ref=source,
        dst_ref=target,
        send_sem=send_sem,
        recv_sem=recv_sem,
        device_id={axis: peer},
        device_id_type=MESH,
    )
    copy.start()
    return copy


def sems(*shape):
    return pltpu.SemaphoreType.DMA(shape)


def spread_over_tensor(source, target_of, pairs, row):
    me = lax.axis_index("tensor")
    return [
        send(
            source, target_of(me), pairs.at[row, step], pairs.at[row + 1, step], "tensor",
            (me + step) % NT,
        )
        for step in range(1, NT)
    ]


def attention_part(mode, inputs, gain, project, output):
    def steps(ins, outs, scratch):
        part, held, mine, pairs = scratch
        if mode == "plain":
            plain, gain, project, output = ins
            summed, qkv, ctx = outs
            state = plain[...]
        else:
            summed, qkv, ctx, kept = outs
            if mode == "packed":
                packed, gain, project, output = ins
                state = unpack(packed)
            else:
                plain, packed, gain, project, output = ins
                state = jnp.where(lax.axis_index("pipe") == 0, plain[...], unpack(packed))
            kept[...] = state
        normal, _ = norm_parts(state.astype(F32))
        normed = (normal * gain[...]).astype(BF)
        projected = dot(normed, project[...]).astype(BF)
        qkv[...] = projected
        for image in range(2):
            for head in range(NH):
                queries, keys, values = head_parts(projected, image, head)
                weights = probabilities(queries, keys).astype(BF)
                ctx[image * R : (image + 1) * R, head * HD : (head + 1) * HD] = dot(
                    weights, values
                ).astype(BF)
        part[...] = dot(ctx[...], output[...]).astype(BF).reshape(NT, CH, D)
        yield
        me = lax.axis_index("tensor")
        copies = [
            send(
                part.at[(me + step) % NT], held.at[me], pairs.at[0, step], pairs.at[1, step],
                "tensor", (me + step) % NT,
            )
            for step in range(1, NT)
        ]
        yield
        for copy in copies:
            copy.wait()
        total = part[me].astype(F32)
        for step in range(1, NT):
            total = total + held[(me + step) % NT].astype(F32)
        mine[...] = total.astype(BF)
        copies = spread_over_tensor(mine, lambda me: summed.at[me], pairs, 2)
        summed[me] = mine[...]
        yield
        for copy in copies:
            copy.wait()

    outs = [((NT, CH, D), BF), ((NR, 3 * GW), BF), ((NR, GW), BF)]
    if mode != "plain":
        outs.append(((NR, D), BF))
    return Part(
        steps,
        [*inputs, gain, project, output],
        outs,
        [
            pltpu.VMEM((NT, CH, D), BF),
            pltpu.VMEM((NT, CH, D), BF),
            pltpu.VMEM((CH, D), BF),
            sems(4, NT),
        ],
    )


RELATIVE = [(dy, dx, dc) for dy in (2, 1, 3, 0) for dx in (1, 0) for dc in (0, 1)]
RELATIVE.remove((0, 0, 0))


def peer_at(relative, sign):
    dy, dx, dc = relative
    me = lax.axis_index("dp")
    row = (me // 4 + sign * dy + 4) % 4
    return row * 4 + ((me // 2 + dx) % 2) * 2 + (me + dc) % 2


def quartered(relative):
    return relative[0] != 0 and relative[1] == 1


SHORT = [relative for relative in RELATIVE if quartered(relative)]


def to_experts(outbox, arrived, pairs, relayed, hybrid):
    me = lax.axis_index("dp")
    member = lax.axis_index("tensor")
    rows = pl.ds(pl.multiple_of(member * 16, 16), 16)
    direct, relays, order = [], [], []
    for number, relative in enumerate(RELATIVE):
        peer = peer_at(relative, 1)
        short = hybrid and quartered(relative)
        copy = send(
            outbox.at[peer, rows] if short else outbox.at[peer],
            arrived.at[me, rows] if short else arrived.at[me],
            pairs.at[0, number],
            pairs.at[1, number],
            "dp",
            peer,
        )
        if short:
            order.append((number, relative, copy))
        else:
            direct.append(copy)
    arrived[me] = outbox[me]
    yield
    order.sort(key=lambda item: item[1][0] == 2)
    for _, relative, copy in order:
        number = SHORT.index(relative)
        copy.wait_recv()
        source = peer_at(relative, -1)
        for step in range(1, NT):
            relays.append(
                send(
                    arrived.at[source, rows],
                    arrived.at[source, rows],
                    relayed.at[0, number, step],
                    relayed.at[1, number, step],
                    "tensor",
                    (member + step) % NT,
                )
            )
    for _ in range(6):
        yield
    for copy in direct:
        copy.wait()
    for _, _, copy in order:
        copy.wait_send()
    for copy in relays:
        copy.wait()


def to_experts_scratch(hybrid):
    return [
        pltpu.VMEM((NDP, 2 * SL, D), BF),
        sems(2, NDP),
        sems(2, len(SHORT), NT) if hybrid else sems(2, 1, 1),
    ]


def live_rows(count):
    row = lax.broadcasted_iota(jnp.int32, (NR, 1), 0)
    image = (row >= R).astype(jnp.int32)
    return (image < count) & (row - image * R < IMG_LEN)


def dispatch_part(hybrid, count, state, summed, gain, router, routes):
    def steps(ins, outs, scratch):
        count, state, summed, gain, router, routes = ins
        arrived, x1, meta = outs
        outbox, pairs, relayed = scratch
        values = state[...].astype(F32) + summed[...].reshape(NR, D).astype(F32)
        x1[...] = values
        normal, _ = norm_parts(values)
        normed = (normal * gain[...]).astype(BF)
        logits = dot(normed, router[...])
        exponent = jnp.exp(logits - jnp.max(logits, axis=-1, keepdims=True))
        gate = exponent / jnp.sum(exponent, axis=-1, keepdims=True)
        live = live_rows(count[0, 0])
        experts = lax.broadcasted_iota(jnp.int32, (NR, EXPERTS), 1)
        route = [routes[:, k : k + 1] for k in range(2)]
        match = [jnp.where(live & (route[k] == experts), 1.0, 0.0) for k in range(2)]
        above = lax.broadcasted_iota(jnp.int32, (NR, NR), 1) < lax.broadcasted_iota(
            jnp.int32, (NR, NR), 0
        )
        before = dot(jnp.where(above, 1.0, 0.0).astype(BF), (match[0] + match[1]).astype(BF))
        meta[:, 0:EXPERTS] = gate
        hot = None
        slots = lax.broadcasted_iota(jnp.int32, (NR, EXPERTS * SL), 1)
        for k in range(2):
            slot = jnp.sum(match[k] * before, axis=1, keepdims=True).astype(jnp.int32)
            position = jnp.where(live, route[k] * SL + slot, -1)
            meta[:, 32 + k : 33 + k] = jnp.sum(match[k] * gate, axis=1, keepdims=True)
            meta[:, 34 + k : 35 + k] = position.astype(F32)
            meta[:, 36 + k : 37 + k] = route[k].astype(F32)
            same = slots == position
            hot = same if hot is None else hot | same
        meta[:, 38:39] = jnp.where(live, 1.0, 0.0)
        result = dot(jnp.where(hot, 1.0, 0.0).astype(BF), normed, 0, 0).astype(BF)
        outbox[...] = result.reshape(NDP, 2 * SL, D)
        yield
        yield from to_experts(outbox, arrived, pairs, relayed, hybrid)

    return Part(
        steps,
        [count, state, summed, gain, router, routes],
        [((NDP, 2 * SL, D), BF), ((NR, D), F32), ((NR, 128), F32)],
        to_experts_scratch(hybrid),
        [SMEM] + [VMEM] * 5,
    )


def spread_part(hybrid, delta, meta):
    def steps(ins, outs, scratch):
        delta, meta = ins
        (arrived,) = outs
        outbox, pairs, relayed = scratch
        values = delta[...].astype(F32) * meta[:, 38:39]
        slots = lax.broadcasted_iota(jnp.int32, (NR, EXPERTS * SL), 1)
        total = None
        for k in range(2):
            position = meta[:, 34 + k : 35 + k].astype(jnp.int32)
            hot = jnp.where(slots == position, 1.0, 0.0).astype(BF)
            scaled = (values * meta[:, 32 + k : 33 + k]).astype(BF)
            term = dot(hot, scaled, 0, 0)
            total = term if total is None else total + term
        outbox[...] = total.astype(BF).reshape(NDP, 2 * SL, D)
        yield
        yield from to_experts(outbox, arrived, pairs, relayed, hybrid)

    return Part(steps, [delta, meta], [((NDP, 2 * SL, D), BF)], to_experts_scratch(hybrid))


CUBE = 0.044715
ROOT = 0.7978845608028654


def gelu_parts(pre):
    squared = pre * pre
    inner = jnp.tanh(ROOT * (pre + CUBE * pre * squared))
    return 0.5 * pre * (1.0 + inner), inner, squared


def store_quarters(target, expert, values):
    values = values.astype(BF).reshape(NDP, 2, 16, D)
    for q in range(NT):
        for half in range(2):
            target[q, expert, :, :, half * Q : (half + 1) * Q] = values[
                :, half, :, q * Q : (q + 1) * Q
            ]


def expert_steps(first, second, compute, result, scratch):
    w1, w2, loads, part, held, mine, sums, pairs = scratch
    loading = []
    for expert in range(2):
        for number, (source, target) in enumerate(((first, w1), (second, w2))):
            copy = pltpu.make_async_copy(
                source.at[expert], target.at[expert], loads.at[number, expert]
            )
            copy.start()
            loading.append(copy)
    loading[0].wait()
    store_quarters(part, 0, compute(0, w1, w2, loading[1]))
    yield
    me = lax.axis_index("tensor")
    home = lax.axis_index("dp")
    whole = [
        send(
            part.at[(me + step) % NT, 0], held.at[me, 0], sums.at[0, 4, step], sums.at[1, 4, step],
            "tensor", (me + step) % NT,
        )
        for step in range(1, NT)
    ]
    loading[2].wait()
    store_quarters(part, 1, compute(1, w1, w2, loading[3]))
    group = home // 4
    scattered = []
    for turn in range(4):
        block = ((group + turn + 1) % 4) * 4
        for step in range(1, NT):
            peer = (me + step) % NT
            scattered.append(
                send(
                    part.at[peer, 1, pl.ds(block, 4)],
                    held.at[me, 1, pl.ds(block, 4)],
                    sums.at[0, turn, step],
                    sums.at[1, turn, step],
                    "tensor",
                    peer,
                )
            )
    yield
    for copy in whole:
        copy.wait()
    total = part[me, 0].astype(F32)
    for step in range(1, NT):
        total = total + held[(me + step) % NT, 0].astype(F32)
    mine[:, 0] = total.astype(BF)
    returned = []
    for turn in range(4):
        block = ((group + turn + 1) % 4) * 4
        for step in range(1, NT):
            scattered[turn * 3 + step - 1].wait_recv()
        total = part[me, 1, pl.ds(block, 4)].astype(F32)
        for step in range(1, NT):
            total = total + held[(me + step) % NT, 1, pl.ds(block, 4)].astype(F32)
        mine[pl.ds(block, 4), 1] = total.astype(BF)
        for number in range(4):
            if turn == 3 and number == 0:
                result[home] = mine[home]
                continue
            offset = (turn + 1) % 4 * 4 + number
            peer = block + (home + number) % 4
            returned.append(
                send(
                    mine.at[peer], result.at[home], pairs.at[0, offset], pairs.at[1, offset], "dp",
                    peer,
                )
            )
        yield
    for copy in returned:
        copy.wait()
    for copy in scattered:
        copy.wait_send()


EXPERT_SCRATCH = [
    pltpu.VMEM((2, D, D), BF),
    pltpu.VMEM((2, D, D), BF),
    sems(2, 2),
    pltpu.VMEM((NT, 2, NDP, 16, 2 * Q), BF),
    pltpu.VMEM((NT, 2, NDP, 16, 2 * Q), BF),
    pltpu.VMEM((NDP, 2, 16, 2 * Q), BF),
    sems(2, 5, NT),
    sems(2, NDP),
]
RETURNED = ((NDP, 2, 16, 2 * Q), BF)


def expert_rows(ref, expert):
    return ref[:, expert * SL : (expert + 1) * SL].reshape(NDP * SL, D)


def experts_forward_part(arrived, first, second):
    def steps(ins, outs, scratch):
        arrived, first, second = ins

        def compute(expert, w1, w2, loading):
            hidden = gelu_parts(dot(expert_rows(arrived, expert), w1[expert]))[0].astype(BF)
            loading.wait()
            return dot(hidden, w2[expert])

        yield from expert_steps(first, second, compute, outs[0], scratch)

    return Part(
        steps, [arrived, first, second], [RETURNED], EXPERT_SCRATCH, [VMEM, ANYWHERE, ANYWHERE]
    )


def experts_backward_part(arrived, delta, first, second):
    def steps(ins, outs, scratch):
        arrived, delta, first, second = ins
        result, hidden_out, dpre_out = outs

        def compute(expert, w1, w2, loading):
            place = slice(expert * SL, (expert + 1) * SL)
            pre = dot(expert_rows(arrived, expert), w1[expert])
            hidden, inner, squared = gelu_parts(pre)
            hidden_out[:, place] = hidden.astype(BF).reshape(NDP, SL, D)
            slope = 0.5 * (1.0 + inner) + (0.5 * ROOT) * pre * (1.0 - inner * inner) * (
                1.0 + 3.0 * CUBE * squared
            )
            loading.wait()
            dhidden = dot(expert_rows(delta, expert), w2[expert], 1, 1).astype(BF).astype(F32)
            dpre = (dhidden * slope).astype(BF)
            dpre_out[:, place] = dpre.reshape(NDP, SL, D)
            return dot(dpre, w1[expert], 1, 1)

        yield from expert_steps(first, second, compute, result, scratch)

    rows = ((NDP, 2 * SL, D), BF)
    return Part(
        steps,
        [arrived, delta, first, second],
        [RETURNED, rows, rows],
        EXPERT_SCRATCH,
        [VMEM, VMEM, ANYWHERE, ANYWHERE],
    )


def expert_grads_kernel(stage, *refs):
    grad_first, grad_second = refs[12:]

    def flat(ref):
        return ref[...].reshape(NDP * SL, D)

    def pairs(a, b):
        grad_first[0] = dot(flat(a[0]), flat(a[1]), 0, 0) + dot(flat(b[0]), flat(b[1]), 0, 0)
        grad_second[0] = dot(flat(a[2]), flat(a[3]), 0, 0) + dot(flat(b[2]), flat(b[3]), 0, 0)

    @pl.when(stage[0] == 0)
    def _():
        pairs(refs[0:4], refs[4:8])

    @pl.when(stage[0] != 0)
    def _():
        pairs(refs[0:4], refs[8:12])


def expert_grads(stage, both, first_only, last_only):
    shape = (NDP, SL, D)
    weights = pl.BlockSpec((1, D, D), lambda p, s: (p, 0, 0))
    return pl.pallas_call(
        expert_grads_kernel,
        grid_spec=pltpu.PrefetchScalarGridSpec(
            num_scalar_prefetch=1,
            grid=(2,),
            in_specs=[pl.BlockSpec(shape, lambda p, s: (0, p, 0))] * 4
            + [pl.BlockSpec(shape, lambda p, s: (0, p * (1 - s[0]), 0))] * 4
            + [pl.BlockSpec(shape, lambda p, s: (0, p * s[0], 0))] * 4,
            out_specs=[weights, weights],
        ),
        out_shape=[jax.ShapeDtypeStruct((2, D, D), F32)] * 2,
        compiler_params=params(),
        name="expert_grads",
    )(stage, *both, *first_only, *last_only)


def gathered(returned, meta, k):
    position = meta[:, 34 + k : 35 + k].astype(jnp.int32)
    place = jnp.where(position >= 0, (position // SL) * 16 + position % 16, -1)
    odd = (position // 16) % 2 == 1
    hot = lax.broadcasted_iota(jnp.int32, (NR, NDP * SL), 1) == place
    both = dot(jnp.where(hot, 1.0, 0.0).astype(BF), returned)
    return jnp.where(odd, both[:, Q:], both[:, :Q])


HALVES = (slice(0, CH), slice(CH, R))


def combine_part(onward, returned, x1, meta):
    def steps(ins, outs, scratch):
        returned, x1, meta = ins
        packed, pieces = outs[:2]
        member = lax.axis_index("tensor")
        live = meta[:, 38:39]
        total = column_quarter(x1, member)
        rows = returned[...].reshape(NDP * SL, 2 * Q)
        for k in range(2):
            piece = gathered(rows, meta, k)
            pieces[k] = piece.astype(BF)
            total = total + meta[:, 32 + k : 33 + k] * piece
        total = (total * live).astype(BF)
        packed[:, :Q] = total[:R]
        packed[:, Q:] = total[R:]
        if not onward:
            return
        yield
        result = outs[2]
        near, chosen, across_sems, pairs = scratch
        stage = lax.axis_index("pipe")
        across = [
            send(
                packed.at[half], near.at[half], across_sems.at[0, i], across_sems.at[1, i], "pipe",
                1 - stage,
            )
            for i, half in enumerate(HALVES)
        ]
        copies = []
        for i, half in enumerate(HALVES):
            across[i].wait_recv()
            chosen[half] = jnp.where(stage == 0, packed[half], near[half])
            copies += spread_over_tensor(
                chosen.at[half], lambda me: result.at[me, half], pairs, 2 * i
            )
        result[member] = chosen[...]
        yield
        for copy in copies:
            copy.wait()
        for copy in across:
            copy.wait_send()

    outs = [((R, 2 * Q), BF), ((2, NR, Q), BF)]
    scratch = []
    if onward:
        outs.append(((NT, R, 2 * Q), BF))
        scratch = [pltpu.VMEM((R, 2 * Q), BF), pltpu.VMEM((R, 2 * Q), BF), sems(2, 2), sems(4, NT)]
    return Part(steps, [returned, x1, meta], outs, scratch)


def collect_part(returned, meta, pieces, delta):
    def steps(ins, outs, scratch):
        returned, meta, pieces, delta = ins
        result, dpicks_all = outs
        packed, dpicks, pairs = scratch
        member = lax.axis_index("tensor")
        total = None
        rows = returned[...].reshape(NDP * SL, 2 * Q)
        lanes = lax.broadcasted_iota(jnp.int32, (NR, 128), 1)
        columns = jnp.zeros((NR, 128), F32)
        part = column_quarter(delta, member).astype(F32) * meta[:, 38:39]
        for k in range(2):
            piece = gathered(rows, meta, k)
            total = piece if total is None else total + piece
            dots = jnp.sum(pieces[k].astype(F32) * part, axis=1, keepdims=True)
            columns = jnp.where(lanes == k, dots, columns)
        total = total.astype(BF)
        packed[:, :Q] = total[:R]
        packed[:, Q:] = total[R:]
        dpicks[:, :NR] = jnp.transpose(columns)[:8]
        dpicks[:, NR:] = jnp.zeros((8, 512 - NR), F32)
        yield
        copies = spread_over_tensor(packed, lambda me: result.at[me], pairs, 0)
        copies += spread_over_tensor(dpicks, lambda me: dpicks_all.at[me], pairs, 2)
        result[member] = packed[...]
        dpicks_all[member] = dpicks[...]
        for _ in range(6):
            yield
        for copy in copies:
            copy.wait()

    return Part(
        steps,
        [returned, meta, pieces, delta],
        [((NT, R, 2 * Q), BF), ((NT, 8, 512), F32)],
        [pltpu.VMEM((R, 2 * Q), BF), pltpu.VMEM((8, 512), F32), sems(4, NT)],
    )


def halves(values):
    high = values.astype(BF)
    return high, (values - high.astype(F32)).astype(BF)


RS_ROWS = ((0, 64), (64, 48))
GR = D // NDP


def sum_dp(pack, result, near, half, held, mine, tile, tiles, core_sems, chip_sems, tile_sems):
    home = lax.axis_index("dp")
    core = home % 2
    chip = home // 2
    partner = home + 1 - 2 * core
    copy = send(pack.at[1 - core], near, core_sems.at[0, 0], core_sems.at[1, 0], "dp", partner)
    yield
    copy.wait()
    half[...] = (pack[core].astype(F32) + near[...].astype(F32)).astype(BF)
    chips = [(dy, dx) for dy in (2, 1, 3, 0) for dx in (1, 0) if (dy, dx) != (0, 0)]

    def chip_at(dy, dx):
        return ((chip // 2 + dy) % 4) * 2 + (chip + dx) % 2

    copies = []
    for number, (dy, dx) in enumerate(chips):
        other = chip_at(dy, dx)
        copies.append(
            send(
                half.at[other], held.at[chip], chip_sems.at[0, number], chip_sems.at[1, number],
                "dp", other * 2 + core,
            )
        )
    yield
    for copy in copies:
        copy.wait()
    total = half[chip].astype(F32)
    for step in range(1, 8):
        total = total + held[(chip + step) % 8].astype(F32)
    mine[...] = total[:, :768].astype(BF)
    tile[...] = total[:, 768:]
    small = spread_over_tensor(tile, lambda me: tiles.at[me], tile_sems, 0)
    copies = []
    for number, (dy, dx) in enumerate(chips):
        other = chip_at(dy, dx)
        copies.append(
            send(
                mine, result.at[core, chip, :, pl.ds(0, 768)], chip_sems.at[2, number],
                chip_sems.at[3, number], "dp", other * 2 + core,
            )
        )
    result[core, chip, :, 0:768] = mine[...]
    yield
    for copy in small:
        copy.wait()
    me = lax.axis_index("tensor")
    others = tile[...]
    for step in range(1, NT):
        others = others + tiles[(me + step) % NT]
    lanes = lax.broadcasted_iota(jnp.int32, (GR, 128), 1)
    result[core, chip, :, 768:] = jnp.where(lanes == 33, others, tile[...]).astype(BF)
    for number, (dy, dx) in enumerate(chips):
        other = chip_at(dy, dx)
        place = result.at[core, chip, :, pl.ds(768, 128)]
        copies.append(
            send(
                place, place, chip_sems.at[4, number], chip_sems.at[5, number], "dp",
                other * 2 + core,
            )
        )
    yield
    for copy in copies:
        copy.wait()
    copy = send(
        result.at[core], result.at[core], core_sems.at[0, 1], core_sems.at[1, 1], "dp", partner
    )
    yield
    copy.wait()


SUM_SCRATCH = [
    pltpu.VMEM((8, GR, GP), BF),
    pltpu.VMEM((8, GR, GP), BF),
    pltpu.VMEM((8, GR, GP), BF),
    pltpu.VMEM((GR, D), BF),
    pltpu.VMEM((GR, 128), F32),
    pltpu.VMEM((NT, GR, 128), F32),
    sems(2, 2),
    sems(6, 8),
    sems(2, NT),
]


def gathers(sources, targets, pairs, begin):
    def handle(chosen):
        me = lax.axis_index("tensor")
        for number in chosen:
            for step in range(1, NT):
                copy = pltpu.make_async_remote_copy(
                    src_ref=sources[number],
                    dst_ref=targets[number].at[me],
                    send_sem=pairs.at[2 * number, step],
                    recv_sem=pairs.at[2 * number + 1, step],
                    device_id={"tensor": (me + step) % NT},
                    device_id_type=MESH,
                )
                if begin:
                    copy.start()
                else:
                    copy.wait()

    @pl.when(lax.axis_index("pipe") == 0)
    def _():
        handle((0,))

    @pl.when(lax.axis_index("pipe") == 1)
    def _():
        handle((1, 2))


def layer_part(last, inputs, finals=()):
    def steps(ins, outs, scratch):
        (
            packed, dpicks, delta, x1, meta, gain_two, router, state, gain_one, qkv, ctx, project,
            output,
        ) = ins[:13]
        dqkv, part, dx1_kept, held, near, chosen, pairs, across_sems = scratch[:8]
        live = meta[:, 38:39]
        gate = meta[:, 0:EXPERTS]
        dx2 = delta[...].astype(F32) * live
        total = dpicks[0] + dpicks[1] + dpicks[2] + dpicks[3]
        total = jnp.concatenate([total, jnp.zeros((120, 512), F32)], axis=0)
        columns = jnp.transpose(total)[:NR]
        experts = lax.broadcasted_iota(jnp.int32, (NR, EXPERTS), 1)
        dgate = jnp.zeros((NR, EXPERTS), F32)
        for k in range(2):
            route = meta[:, 36 + k : 37 + k].astype(jnp.int32)
            dgate = dgate + jnp.where(route == experts, columns[:, k : k + 1] * live, 0.0)
        dlogits = gate * (dgate - jnp.sum(gate * dgate, axis=-1, keepdims=True))
        normal, inverse = norm_parts(x1[...])
        high, low = halves(dlogits)
        dz2 = (
            unpack(packed).astype(F32) + dot(high, router[...], 1, 1) + dot(low, router[...], 1, 1)
        )
        dx1 = dx2 + norm_back(dz2, gain_two[...], normal, inverse)
        dx1_kept[...] = dx1.reshape(NT, CH, D)
        dattn = dx1.astype(BF)
        if last:
            yield
            gathers(ins[15:18], outs[2:5], scratch[8], True)
            for source, target in zip(ins[15:18], outs[2:5]):
                target[lax.axis_index("tensor")] = source[...]
        dctx = dot(dattn, output[...], 1, 1).astype(BF)
        scale = HD**-0.5
        projected = qkv[...]
        for image in range(2):
            rows = slice(image * R, (image + 1) * R)
            for head in range(NH):
                queries, keys, values = head_parts(projected, image, head)
                dc = dctx[rows, head * HD : (head + 1) * HD]
                weights = probabilities(queries, keys)
                dweights = dot(dc, values, 1, 1)
                dvalues = dot(weights.astype(BF), dc, 0, 0)
                dscores = weights * (dweights - jnp.sum(weights * dweights, axis=-1, keepdims=True))
                dscores = dscores.astype(BF)
                dqueries = dot(dscores, keys) * scale
                dkeys = dot(dscores, queries, 0, 0) * scale
                for number, value in enumerate((dqueries, dkeys, dvalues)):
                    start = number * GW + head * HD
                    dqkv[rows, start : start + HD] = value.astype(BF)
        own_part = dot(dqkv[...], project[...], 1, 1).astype(BF)
        part[...] = own_part.reshape(NT, CH, D)
        if not last:
            yield
        me = lax.axis_index("tensor")
        stage = lax.axis_index("pipe")
        scattered = [
            [
                send(
                    part.at[(me + step) % NT, pl.ds(start, size)],
                    held.at[me, pl.ds(start, size)],
                    pairs.at[2 * i, step],
                    pairs.at[2 * i + 1, step],
                    "tensor",
                    (me + step) % NT,
                )
                for step in range(1, NT)
            ]
            for i, (start, size) in enumerate(RS_ROWS)
        ]
        normal_one, _ = norm_parts(state[...].astype(F32))
        normed_one = (normal_one * gain_one[...]).astype(BF)
        normed = (normal * gain_two[...]).astype(BF)
        gain_rows = [
            jnp.sum(dz2 * normal, axis=0, keepdims=True),
            jnp.sum(own_part.astype(F32) * normal_one, axis=0, keepdims=True),
        ]
        places = lax.broadcasted_iota(jnp.int32, (128, D), 0)
        tall = jnp.where(places == 32, gain_rows[0], 0.0)
        tall = jnp.where(places == 33, gain_rows[1], tall)
        terms = [
            (0, 576, dot(normed_one, dqkv[...], 0, 0)),
            (576, 768, dot(dattn, ctx[...], 0, 0)),
        ]
        side = jnp.transpose(tall)
        router_term = dot(normed, high, 0, 0) + dot(normed, low, 0, 0)
        side = side + jnp.concatenate([router_term, jnp.zeros((D, 96), F32)], axis=1)
        terms.append((768, GP, side))
        if last:
            one, first = ins[13:15]
            pack = scratch[9]
            for low_end, high_end, term in terms:
                term = jnp.where(stage == 0, term, first[:, low_end:high_end])
                term = term + one[:, low_end:high_end]
                pack[:, :, :, low_end:high_end] = term.astype(BF).reshape(
                    2, 8, GR, high_end - low_end
                )
            summing = sum_dp(pack, outs[1], *scratch[10:])
            next(summing)
            next(summing)
        else:
            for low_end, high_end, term in terms:
                outs[2][:, low_end:high_end] = term
            summing = iter(())
        waiting = []
        result = outs[0]
        chunk = chosen if last else outs[1]
        across = []
        for i, (start, size) in enumerate(RS_ROWS):
            rows = pl.ds(start, size)
            for copy in scattered[i]:
                copy.wait_recv()
            dz1 = part[me, rows].astype(F32)
            for step in range(1, NT):
                dz1 = dz1 + held[(me + step) % NT, rows].astype(F32)
            here = pl.ds(pl.multiple_of(me * CH + start, 16), size)
            normal_here, inverse_here = norm_parts(state[here].astype(F32))
            delta_here = norm_back(dz1, gain_one[...], normal_here, inverse_here)
            chunk[rows] = (dx1_kept[me, rows] + delta_here).astype(BF)
            if not last:
                across.append(
                    send(
                        chunk.at[rows], near.at[rows], across_sems.at[0, i], across_sems.at[1, i],
                        "pipe", 1 - stage,
                    )
                )
        for i, (start, size) in enumerate(RS_ROWS):
            rows = pl.ds(start, size)
            if not last:
                across[i].wait_recv()
                chosen[rows] = jnp.where(stage == 1, chunk[rows], near[rows])
            waiting += spread_over_tensor(
                chosen.at[rows], lambda me: result.at[me, rows], pairs, 4 + 2 * i
            )
        result[me] = chosen[...]
        yield
        for _ in summing:
            yield
        if last:
            gathers(ins[15:18], outs[2:5], scratch[8], False)
        for copy in waiting:
            copy.wait()
        for group in scattered:
            for copy in group:
                copy.wait_send()
        for copy in across:
            copy.wait_send()

    outs = [((NT, CH, D), BF)]
    scratch = [
        pltpu.VMEM((NR, 3 * GW), BF),
        pltpu.VMEM((NT, CH, D), BF),
        pltpu.VMEM((NT, CH, D), F32),
        pltpu.VMEM((NT, CH, D), BF),
        pltpu.VMEM((CH, D), BF),
        pltpu.VMEM((CH, D), BF),
        sems(8, NT),
        sems(2, 2),
    ]
    if last:
        wide = ((NT, R, 2 * Q), BF)
        outs += [((2, 8, GR, GP), BF), ((NT, CH, D), BF), wide, wide]
        scratch += [sems(6, NT), pltpu.VMEM((2, 8, GR, GP), BF)] + SUM_SCRATCH
    else:
        outs += [((CH, D), BF), ((D, GP), F32)]
    return Part(steps, [*inputs, *finals], outs, scratch)


def finish_kernel(stage, *refs):
    states, grads, whole = refs[:4], refs[4:8], refs[8]
    section_out, input_grad, project_grad, output_grad, router_grad, gains = refs[9:]

    def rows(values):
        values = values.astype(F32)
        return jnp.concatenate([values[:IMG_LEN], values[R : R + IMG_LEN]], axis=0).astype(BF)

    def place(base):
        for micro in range(2):
            section_out[micro] = rows(unpack(states[base + micro]))
            input_grad[micro] = rows(grads[base + micro][...])

    @pl.when(stage[0, 0] == 0)
    def _():
        place(0)

    @pl.when(stage[0, 0] != 0)
    def _():
        place(2)

    project_grad[...] = whole[:, :576].astype(F32)
    output_grad[...] = jnp.transpose(whole[:, 576:768].astype(F32))
    side = whole[:, 768:].astype(F32)
    router_grad[...] = side[:, :EXPERTS]
    gains[...] = jnp.transpose(side)[32:40]


def finish(stage, states, grads, whole):
    return pl.pallas_call(
        finish_kernel,
        in_specs=[SMEM] + [VMEM] * 9,
        out_shape=[
            jax.ShapeDtypeStruct((2, 2 * IMG_LEN, D), BF),
            jax.ShapeDtypeStruct((2, 2 * IMG_LEN, D), BF),
            jax.ShapeDtypeStruct((D, 3 * GW), F32),
            jax.ShapeDtypeStruct((GW, D), F32),
            jax.ShapeDtypeStruct((D, EXPERTS), F32),
            jax.ShapeDtypeStruct((8, D), F32),
        ],
        compiler_params=params(),
        name="finish",
    )(stage, *states, *grads, whole)


def pad_rows(values):
    micro, _, width = values.shape
    values = values.reshape(micro, 2, IMG_LEN, width)
    return jnp.pad(values, ((0, 0), (0, 0), (0, R - IMG_LEN), (0, 0))).reshape(micro, NR, width)


def body(
    tokens,
    cotangent,
    image_counts,
    routes,
    attn_norm_gain,
    query_key_value,
    attn_output,
    moe_norm_gain,
    router_weight,
    expert_in,
    expert_down,
):
    gain_one = attn_norm_gain
    gain_two = moe_norm_gain
    project = query_key_value[0].reshape(D, 3 * GW)
    output = attn_output[0]
    router = router_weight[0]
    first, second = expert_in[0], expert_down[0]
    stage = lax.axis_index("pipe")
    early = stage == 0
    counts = image_counts[:, lax.axis_index("dp")].reshape(2, 1, 1)
    plain = pad_rows(tokens)
    upstream = pad_rows(cotangent)
    paths = pad_rows(routes)

    def chosen(one, other):
        return jax.tree.map(lambda a, b: jnp.where(early, a, b), one, other)

    def attend(mode, inputs):
        return attention_part(mode, inputs, gain_one, project, output)

    def layer_inputs(packed, dpicks, delta, saved):
        state, qkv, ctx, x1, meta, arrived, pieces = saved
        return [
            packed, dpicks, delta, x1, meta, gain_two, router, state, gain_one, qkv, ctx, project,
            output,
        ]

    saved = []
    packed_list = []
    states = []
    arriving = None
    for moment in range(2):
        if moment == 0:
            mode, inputs = "plain", (plain[0],)
            count, path = counts[0], paths[0]
        else:
            mode, inputs = "mixed", (plain[1], arriving)
            count, path = chosen((counts[1], paths[1]), (counts[0], paths[0]))
        (results,) = run(
            "attention_" + mode, 1 + moment, ("tensor",), [attend(mode, inputs)]
        )
        summed, qkv, ctx = results[:3]
        state = inputs[0] if mode == "plain" else results[3]
        ((arrived, x1, meta),) = run(
            "dispatch", 3, ("tensor", "dp"),
            [dispatch_part(True, count, state, summed, gain_two, router, path)],
        )
        ((returned,),) = run(
            "experts_forward", 4, ("tensor", "dp"), [experts_forward_part(arrived, first, second)]
        )
        ((packed, pieces, arriving),) = run(
            "combine", 5, ("tensor", "pipe"), [combine_part(True, returned, x1, meta)]
        )
        packed_list.append(packed)
        states.append(arriving)
        saved.append((state, qkv, ctx, x1, meta, arrived, pieces))

    late = saved[1]
    delta = upstream[0]
    (summed, qkv, ctx, state), (delta_arrived,) = run(
        "attention_and_spread", 6, ("tensor", "dp"),
        [attend("packed", (arriving,)), spread_part(False, delta, late[4])],
    )
    (arrived, x1, meta), (returned, hidden, dpre) = run(
        "dispatch_and_experts_backward", 7, ("tensor", "dp"),
        [
            dispatch_part(False, counts[1], state, summed, gain_two, router, paths[1]),
            experts_backward_part(late[5], delta_arrived, first, second),
        ],
    )
    terms = [(late[5], dpre, hidden, delta_arrived)]
    (returned_forward,), (packed, dpicks) = run(
        "experts_forward_and_collect", 8, ("tensor", "dp"),
        [
            experts_forward_part(arrived, first, second),
            collect_part(returned, late[4], late[6], delta),
        ],
    )
    (packed_last, pieces), (grad_state, chunk, grads) = run(
        "combine_and_layer_backward", 9, ("tensor", "pipe"),
        [
            combine_part(False, returned_forward, x1, meta),
            layer_part(False, layer_inputs(packed, dpicks, delta, late)),
        ],
    )
    packed_list.append(packed_last)
    saved.append((state, qkv, ctx, x1, meta, arrived, pieces))
    grad_list = [grads]
    grad_states = [grad_state.reshape(NR, D)]

    for moment in range(1, 3):
        if moment == 1:
            late = chosen(saved[0], saved[2])
            delta = jnp.where(early, grad_states[0], upstream[1])
        else:
            late = saved[1]
            delta = grad_states[1]
        meta, arrived, pieces = late[4:]
        ((delta_arrived,),) = run("spread", 10, ("tensor", "dp"), [spread_part(True, delta, meta)])
        ((returned, hidden, dpre),) = run(
            "experts_backward", 11, ("tensor", "dp"),
            [experts_backward_part(arrived, delta_arrived, first, second)],
        )
        terms.append((arrived, dpre, hidden, delta_arrived))
        ((packed, dpicks),) = run(
            "collect", 12, ("tensor",), [collect_part(returned, meta, pieces, delta)]
        )
        inputs = layer_inputs(packed, dpicks, delta, late)
        if moment == 1:
            ((grad_state, chunk, grads),) = run(
                "layer_backward", 13, ("tensor", "pipe"), [layer_part(False, inputs)]
            )
            grad_list.append(grads)
            grad_states.append(grad_state.reshape(NR, D))
        else:
            finals = [grad_list[1], grad_list[0], chunk, packed_list[1], packed_list[2]]
            ((grad_state, whole, own, wide_one, wide_two),) = run(
                "layer_backward_last", 14, ("tensor", "dp"), [layer_part(True, inputs, finals)]
            )
            grad_states.append(grad_state.reshape(NR, D))

    grad_first, grad_second = expert_grads(
        stage.reshape(1).astype(jnp.int32), terms[1], terms[2], terms[0]
    )
    section_out, input_grad, project_grad, output_grad, router_grad, gains = finish(
        stage.reshape(1, 1).astype(jnp.int32),
        [states[0], states[1], wide_one, wide_two],
        [own.reshape(NR, D), grad_states[2], grad_states[0], grad_states[1]],
        whole.reshape(D, GP),
    )
    return (
        section_out[None],
        input_grad[None],
        gains[1:2],
        project_grad.reshape(1, D, 3, GW),
        output_grad[None],
        gains[0:1],
        router_grad[None],
        grad_first[None],
        grad_second[None],
    )


def solution(mesh):
    placed = (
        P(None, "dp", None),
        P(None, "dp", None),
        P(),
        P(None, "dp", None),
        P("pipe", None),
        P("pipe", None, None, "tensor"),
        P("pipe", "tensor", None),
        P("pipe", None),
        P("pipe", None, None),
        P("pipe", "dp", None, "tensor"),
        P("pipe", "dp", "tensor", None),
    )
    return jax.shard_map(
        body,
        mesh=mesh,
        in_specs=placed,
        out_specs=(
            P("pipe", None, "dp", None),
            P("pipe", None, "dp", None),
            P("pipe", None),
            P("pipe", None, None, "tensor"),
            P("pipe", "tensor", None),
            P("pipe", None),
            P("pipe", None, None),
            P("pipe", "dp", None, "tensor"),
            P("pipe", "dp", "tensor", None),
        ),
        check_vma=False,
    )
```

time: 1560 us -> 569 us (0.36)
  Pallas kernels: 0 us -> 517 us
  waiting for transfers between devices: 515 us -> 0 us
  local copies, waits for them, and re-layouts: 435 us -> 41.3 us
  other arithmetic: 228 us -> 1.88 us
  matrix products: 130 us -> 0 us
  blocking collectives: 121 us -> 0 us
  starting transfers between devices: 96.2 us -> 0 us
    pallas_call x0 -> x22, Pallas kernels: none -> 517 us  [the longest x20 502 us: run(): pl.pallas_call(kernel, in_specs=[spec for part in parts for spec in part....]
    psum x12 -> x0, waiting for transfers between devices: 423 us -> none  [the longest x5 177 us: to_tokens(): lax.psum(partial_value.astype(jnp.bfloat16), 'tensor').astype(jnp.float32)]
    dot_general x66 -> x0, matrix products: 130 us -> none  [the longest x3 19 us: experts_backward(): jnp.einsum('erf,erd->efd', hidden, grad_received, preferred_element_type=...]
    all_to_all x10 -> x0, starting transfers between devices: 84.4 us -> none  [the longest x6 46.2 us: to_tokens(): lax.all_to_all(summed.astype(jnp.bfloat16), 'dp', split_axis=1, concat_ax...]
    reduce_sum x48 -> x0, other arithmetic: 72.9 us -> none  [the longest x3 16.8 us: experts_backward(): jnp.sum(delta_returned.reshape(experts * capacity, model_width)[slot_inde...]
    all_to_all x10 -> x0, waiting for transfers between devices: 64.5 us -> none  [the longest x6 45.5 us: to_tokens(): lax.all_to_all(summed.astype(jnp.bfloat16), 'dp', split_axis=1, concat_ax...]
    gather x12 -> x0, local copies, waits for them, and re-layouts: 63.7 us -> none  [the longest x6 32 us: experts_forward(): pieces = returned.reshape(experts * capacity, model_width)[slot_index]]
    all_to_all x2 -> x0, blocking collectives: 61.6 us -> none  [to_experts(): return lax.all_to_all(outbox, 'dp', split_axis=0, concat_axis=1, tiled=True)]
  transfers between devices with their start and end apart: 26 -> 0, of which waited for: 24 -> 0; matrix products, arithmetic and copies ran while one was open for 21% -> 0% of each run, Pallas kernels for 0% -> 0%
where the time goes in v2:
time: 569 us; the launch traced here: 563 us
  Pallas kernels  517 us (91%)
  local copies, waits for them, and re-layouts  41.3 us (7%)
    pallas_call x20, Pallas kernels, run(): pl.pallas_call(kernel, in_specs=[spec for part in parts for spec in part....  502 us
    unnamed x144, local copies, waits for them, and re-layouts  30.4 us

profile of v2, /device:TPU:7, one launch (start us, length us, event | category | flops | bytes accessed | tf_op | source)
XLA Modules:
  0.0 563.1 jit_solution(8497852185158605691)
XLA Ops:
  1.9 1.4 copy.29
  5.5 22.8 %attention_plain.1 = (bf16[4,112,768]{2,1,0:T(8,128)(2,1)S(1)}, bf16[448,576]{1,0:T(8,128)(2,1)S(1)}, bf16[448,192]{1,0:T(8,128)(2,1)S(1)}) custom-call(bf16[448,768]{1,0:T(8,128)(2,1)S(1)} %bitcast.41, f32[1,768]{1,0:T(1,128)S(1)} %copy-done.64, bf16[768,576]{1,0:T(8,128)(2,1)S(1)} %copy.30.refs_2_.refs_3_.refs_14_.refs_11_, bf16[192,768]{1,0:T(8,128)(2,1)S(1)} %bitcast.50), custom_call_target="tpu_custom_call" | custom-call | tf_op jit(solution)/shard_map/attention_plain/pallas_call | solution.py:143
  32.8 1.7 pad_slice_fusion.4
  34.6 1.2 copy-done.11
  36.8 20.7 %dispatch.2 = (bf16[16,64,768]{2,1,0:T(8,128)(2,1)S(1)}, f32[448,768]{1,0:T(8,128)S(1)}, f32[448,128]{1,0:T(8,128)S(1)}) custom-call(s32[1,1]{1,0:T(1,128)} %get-tuple-element.160.refs_0_, bf16[448,768]{1,0:T(8,128)(2,1)S(1)} %bitcast.42, bf16[4,112,768]{2,1,0:T(8,128)(2,1)S(1)} %copy-done.51, f32[1,768]{1,0:T(1,128)S(1)} %copy-done.65, ...), custom_call_target="tpu_custom_call" | custom-call | tf_op jit(solution)/shard_map/dispatch/pallas_call | solution.py:143
  57.6 28.3 %experts_forward.2.refs_0_ = bf16[16,2,16,384]{3,2,1,0:T(8,128)(2,1)S(1)} custom-call(bf16[16,64,768]{2,1,0:T(8,128)(2,1)S(1)} %get-tuple-element.72.refs_0_, bf16[2,768,768]{2,1,0:T(8,128)(2,1)S(1)} %bitcast.39, bf16[2,768,768]{2,1,0:T(8,128)(2,1)} %bitcast.69), custom_call_target="tpu_custom_call" | custom-call | tf_op jit(solution)/shard_map/experts_forward/pallas_call | solution.py:143
  85.9 14.6 %combine.2 = (bf16[224,384]{1,0:T(8,128)(2,1)}, bf16[2,448,192]{2,1,0:T(8,128)(2,1)S(1)}, bf16[4,224,384]{2,1,0:T(8,128)(2,1)S(1)}) custom-call(bf16[16,2,16,384]{3,2,1,0:T(8,128)(2,1)S(1)} %experts_forward.2.refs_0_, f32[448,768]{1,0:T(8,128)S(1)} %get-tuple-element.73.refs_1_, f32[448,128]{1,0:T(8,128)S(1)} %get-tuple-element.74.refs_2_), custom_call_target="tpu_custom_call" | custom-call | tf_op jit(solution)/shard_map/combine/pallas_call | solution.py:143
  106.6 19.4 %attention_mixed.1 = (bf16[4,112,768]{2,1,0:T(8,128)(2,1)S(1)}, bf16[448,576]{1,0:T(8,128)(2,1)S(1)}, bf16[448,192]{1,0:T(8,128)(2,1)S(1)}, bf16[448,768]{1,0:T(8,128)(2,1)S(1)}) custom-call(bf16[448,768]{1,0:T(8,128)(2,1)S(1)} %bitcast.62, bf16[4,224,384]{2,1,0:T(8,128)(2,1)S(1)} %copy-done.28, f32[1,768]{1,0:T(1,128)S(1)} %copy-done.64, ...), custom_call_target="tpu_custom_call" | custom-call | tf_op jit(solution)/shard_map/attention_mixed/pallas_call | solution.py:143
  127.5 19.1 %dispatch.3 = (bf16[16,64,768]{2,1,0:T(8,128)(2,1)S(1)}, f32[448,768]{1,0:T(8,128)S(1)}, f32[448,128]{1,0:T(8,128)S(1)}) custom-call(s32[1,1]{1,0:T(1,128)S(6)} %select_n.79.refs_0_, bf16[448,768]{1,0:T(8,128)(2,1)S(1)} %get-tuple-element.76.refs_1_.refs_10_.refs_7_, bf16[4,112,768]{2,1,0:T(8,128)(2,1)S(1)} %get-tuple-element.77.refs_2_, ...), custom_call_target="tpu_custom_call" | custom-call | tf_op jit(solution)/shard_map/dispatch/pallas_call | solution.py:143
  146.6 29.2 %experts_forward.3.refs_0_ = bf16[16,2,16,384]{3,2,1,0:T(8,128)(2,1)S(1)} custom-call(bf16[16,64,768]{2,1,0:T(8,128)(2,1)S(1)} %get-tuple-element.78.refs_0_.refs_6_.refs_4_.refs_8_, bf16[2,768,768]{2,1,0:T(8,128)(2,1)S(1)} %bitcast.40, bf16[2,768,768]{2,1,0:T(8,128)(2,1)} %bitcast.70), custom_call_target="tpu_custom_call" | custom-call | tf_op jit(solution)/shard_map/experts_forward/pallas_call | solution.py:143
  175.9 13.1 %combine.3 = (bf16[224,384]{1,0:T(8,128)(2,1)S(1)}, bf16[2,448,192]{2,1,0:T(8,128)(2,1)S(1)}, bf16[4,224,384]{2,1,0:T(8,128)(2,1)S(1)}) custom-call(bf16[16,2,16,384]{3,2,1,0:T(8,128)(2,1)S(1)} %experts_forward.3.refs_0_, f32[448,768]{1,0:T(8,128)S(1)} %get-tuple-element.79.refs_1_.refs_6_.refs_3_, ...), custom_call_target="tpu_custom_call" | custom-call | tf_op jit(solution)/shard_map/combine/pallas_call | solution.py:143
  191.0 26.8 %attention_and_spread.1 = (bf16[4,112,768]{2,1,0:T(8,128)(2,1)S(1)}, bf16[448,576]{1,0:T(8,128)(2,1)S(1)}, bf16[448,192]{1,0:T(8,128)(2,1)S(1)}, bf16[448,768]{1,0:T(8,128)(2,1)S(1)}, bf16[16,64,768]{2,1,0:T(8,128)(2,1)}) custom-call(bf16[4,224,384]{2,1,0:T(8,128)(2,1)S(1)} %get-tuple-element.81.refs_0_.refs_1_, f32[1,768]{1,0:T(1,128)S(1)} %copy-done.64, ...), custom_call_target="tpu_custom_call" | custom-call | tf_op jit(solution)/shard_map/attention_and_spread/pallas_call | solution.py:143
  217.8 36.8 %dispatch_and_experts_backward.1 = (bf16[16,64,768]{2,1,0:T(8,128)(2,1)S(1)}, f32[448,768]{1,0:T(8,128)S(1)}, f32[448,128]{1,0:T(8,128)S(1)}, bf16[16,2,16,384]{...) custom-call(s32[1,1]{1,0:T(1,128)} %get-tuple-element.159.refs_0_, ...), custom_call_target="tpu_custom_call" | custom-call | tf_op jit(solution)/shard_map/dispatch_and_experts_backward/pallas_call | solution.py:143
  255.7 33.8 %experts_forward_and_collect.1 = (bf16[16,2,16,384]{3,2,1,0:T(8,128)(2,1)S(1)}, bf16[4,224,384]{2,1,0:T(8,128)(2,1)S(1)}, f32[4,8,512]{2,1,0:T(8,128)S(1)}) custom-call(bf16[16,64,768]{2,1,0:T(8,128)(2,1)S(1)} %get-tuple-element.85.refs_0_, bf16[2,768,768]{2,1,0:T(8,128)(2,1)} %bitcast.36, bf16[2,768,768]{2,1,0:T(8,128)(2,1)} %bitcast.72, ...), custom_call_target="tpu_custom_call" | custom-call | tf_op jit(solution)/shard_map/experts_forward_and_collect/pallas_call | solution.py:143
  289.6 29.7 %combine_and_layer_backward.1 = (bf16[224,384]{1,0:T(8,128)(2,1)S(1)}, bf16[2,448,192]{2,1,0:T(8,128)(2,1)S(1)}, bf16[4,112,768]{2,1,0:T(8,128)(2,1)S(1)}, bf16[112,768]{1,0:T(8,128)(2,1)}, f32[768,896]{1,0:T(8,128)}) custom-call(bf16[16,2,16,384]{3,2,1,0:T(8,128)(2,1)S(1)} %get-tuple-element.88.refs_0_, f32[448,768]{1,0:T(8,128)} %copy-done.24, ...), custom_call_target="tpu_custom_call" | custom-call | tf_op jit(solution)/shard_map/combine_and_layer_backward/pallas_call | solution.py:143
  320.3 20.3 %spread.2.refs_1_.refs_3_ = bf16[16,64,768]{2,1,0:T(8,128)(2,1)S(1)} custom-call(bf16[448,768]{1,0:T(8,128)(2,1)S(1)} %get-tuple-element.161.refs_0_.refs_3_.refs_2_, f32[448,128]{1,0:T(8,128)S(1)} %broadcast_select_fusion.6.refs_1_.refs_4_), custom_call_target="tpu_custom_call" | custom-call | tf_op jit(solution)/shard_map/spread/pallas_call | solution.py:143
  340.6 1.2 copy-done.7
  341.8 30.8 %experts_backward.2 = (bf16[16,2,16,384]{3,2,1,0:T(8,128)(2,1)S(1)}, bf16[16,64,768]{2,1,0:T(8,128)(2,1)S(1)}, bf16[16,64,768]{2,1,0:T(8,128)(2,1)S(1)}) custom-call(bf16[16,64,768]{2,1,0:T(8,128)(2,1)S(1)} %broadcast_select_fusion.refs_0_, bf16[16,64,768]{2,1,0:T(8,128)(2,1)} %copy-done.7, bf16[2,768,768]{2,1,0:T(8,128)(2,1)} %bitcast.37, ...), custom_call_target="tpu_custom_call" | custom-call | tf_op jit(solution)/shard_map/experts_backward/pallas_call | solution.py:143
  374.9 11.7 %collect.2 = (bf16[4,224,384]{2,1,0:T(8,128)(2,1)S(1)}, f32[4,8,512]{2,1,0:T(8,128)S(1)}) custom-call(bf16[16,2,16,384]{3,2,1,0:T(8,128)(2,1)S(1)} %get-tuple-element.96.refs_0_, f32[448,128]{1,0:T(8,128)S(1)} %broadcast_select_fusion.6.refs_1_.refs_4_, bf16[2,448,192]{2,1,0:T(8,128)(2,1)S(1)} %broadcast_select_fusion.4.refs_2_, ...), custom_call_target="tpu_custom_call" | custom-call | tf_op jit(solution)/shard_map/collect/pallas_call | solution.py:143
  386.7 1.2 broadcast_select_fusion.2.refs_3_
  389.4 28.8 %layer_backward.1 = (bf16[4,112,768]{2,1,0:T(8,128)(2,1)S(1)}, bf16[112,768]{1,0:T(8,128)(2,1)S(1)}, f32[768,896]{1,0:T(8,128)}) custom-call(bf16[4,224,384]{2,1,0:T(8,128)(2,1)S(1)} %get-tuple-element.99.refs_0_, f32[4,8,512]{2,1,0:T(8,128)S(1)} %get-tuple-element.100.refs_1_, bf16[448,768]{1,0:T(8,128)(2,1)S(1)} %get-tuple-element.161.refs_0_.refs_3_.refs_2_, ...), custom_call_target="tpu_custom_call" | custom-call | tf_op jit(solution)/shard_map/layer_backward/pallas_call | solution.py:143
  418.2 20.6 %spread.3.refs_1_.refs_7_ = bf16[16,64,768]{2,1,0:T(8,128)(2,1)S(1)} custom-call(bf16[448,768]{1,0:T(8,128)(2,1)S(1)} %bitcast.46, f32[448,128]{1,0:T(8,128)S(1)} %get-tuple-element.80.refs_2_.refs_5_.refs_4_.refs_7_.refs_1_), custom_call_target="tpu_custom_call" | custom-call | tf_op jit(solution)/shard_map/spread/pallas_call | solution.py:143
  438.8 1.2 copy-done.8
  440.0 30.1 %experts_backward.3 = (bf16[16,2,16,384]{3,2,1,0:T(8,128)(2,1)S(1)}, bf16[16,64,768]{2,1,0:T(8,128)(2,1)S(1)}, bf16[16,64,768]{2,1,0:T(8,128)(2,1)S(1)}) custom-call(bf16[16,64,768]{2,1,0:T(8,128)(2,1)S(1)} %copy-done.6, bf16[16,64,768]{2,1,0:T(8,128)(2,1)} %copy-done.8, bf16[2,768,768]{2,1,0:T(8,128)(2,1)} %bitcast.38, bf16[2,768,768]{2,1,0:T(8,128)(2,1)} %bitcast.74), custom_call_target="tpu_custom_call" | custom-call | tf_op jit(solution)/shard_map/experts_backward/pallas_call | solution.py:143
  471.2 12.6 %collect.3 = (bf16[4,224,384]{2,1,0:T(8,128)(2,1)S(1)}, f32[4,8,512]{2,1,0:T(8,128)S(1)}) custom-call(bf16[16,2,16,384]{3,2,1,0:T(8,128)(2,1)S(1)} %get-tuple-element.106.refs_0_, f32[448,128]{1,0:T(8,128)S(1)} %get-tuple-element.80.refs_2_.refs_5_.refs_4_.refs_7_.refs_1_, bf16[2,448,192]{2,1,0:T(8,128)(2,1)S(1)} %copy-done.38, bf16[448,768]{1,0:T(8,128)(2,1)S(1)} %bitcast.47), custom_call_target="tpu_custom_call" | custom-call | tf_op jit(solution)/shard_map/collect/pallas_call | solution.py:143
  483.9 52.7 %layer_backward_last.1 = (bf16[4,112,768]{2,1,0:T(8,128)(2,1)S(1)}, bf16[2,8,48,896]{3,2,1,0:T(8,128)(2,1)}, bf16[4,112,768]{2,1,0:T(8,128)(2,1)S(1)}, bf16[4,22...) custom-call(bf16[4,224,384]{2,1,0:T(8,128)(2,1)S(1)} %get-tuple-element.107.refs_0_, ...), custom_call_target="tpu_custom_call" | custom-call | tf_op jit(solution)/shard_map/layer_backward_last/pallas_call | solution.py:143
  536.6 4.1 finish.1
  540.8 3.3 copy.40
  544.1 2.0 copy.41
  546.7 2.9 copy.39
  550.3 1.4 copy-done.42
  551.7 10.9 %expert_grads.1 = (f32[2,768,768]{2,1,0:T(8,128)}, f32[2,768,768]{2,1,0:T(8,128)}) custom-call(s32[1]{0:T(128)} %bitcast.25.stage, bf16[16,64,768]{2,1,0:T(8,128)(2,1)S(1)} %broadcast_select_fusion.refs_0_, bf16[16,64,768]{2,1,0:T(8,128)(2,1)S(1)} %copy-done.42, bf16[16,64,768]{2,1,0:T(8,128)(2,1)S(1)} %copy-done.40, bf16[16,64,768]{2,1,0:T(8,128)(2,1)} %copy-done.7, ...), custom_call_target="tpu_custom_call" | custom-call | tf_op jit(solution)/shard_map/expert_grads/pallas_call | solution.py:580
  (154 shorter events, 25.7 us)
Async XLA Ops:
  4.3 24.1 %copy-start.10 = (bf16[1,2,224,768]{3,2,1,0:T(8,128)(2,1)}, bf16[1,2,224,768]{3,2,1,0:T(8,128)(2,1)S(1)}, u32[]{:S(2)}) copy-start(bf16[1,2,224,768]{3,2,1,0:T(8,128)(2,1)S(1)} %get-tuple-element.154) | copy-start | bytes 2064388
  4.8 26.0 %copy-start.69 = (bf16[1,768,32]{1,2,0:T(8,128)(2,1)S(1)}, bf16[1,768,32]{1,2,0:T(8,128)(2,1)}, u32[]{:S(2)}) copy-start(bf16[1,768,32]{1,2,0:T(8,128)(2,1)} %param.19) | copy-start | bytes 147460
  5.4 184.5 %copy-start.3 = (bf16[768,576]{1,0:T(8,128)(2,1)}, bf16[768,576]{1,0:T(8,128)(2,1)S(1)}, u32[]{:S(2)}) copy-start(bf16[768,576]{1,0:T(8,128)(2,1)S(1)} %copy.30.refs_2_.refs_3_.refs_14_.refs_11_) | copy-start | bytes 2654212
  5.5 29.0 %copy-start.65 = (f32[1,768]{1,0:T(1,128)S(1)}, f32[1,768]{1,0:T(1,128)}, u32[]{:S(2)}) copy-start(f32[1,768]{1,0:T(1,128)} %refs_5_.3) | copy-start | bytes 9220
  30.9 26.7 %copy-start.2 = (bf16[1,2,768,768]{3,2,1,0:T(8,128)(2,1)S(1)}, bf16[1,2,768,768]{3,2,1,0:T(8,128)(2,1)}, u32[]{:S(2)}) copy-start(bf16[1,2,768,768]{3,2,1,0:T(8,128)(2,1)} %param.20) | copy-start | bytes 7077892
  34.5 51.3 %copy-start.35 = (s32[1,2,224,2]{3,2,1,0:T(8,128)}, s32[1,2,224,2]{3,2,1,0:T(8,128)S(1)}, u32[]{:S(2)}) copy-start(s32[1,2,224,2]{3,2,1,0:T(8,128)S(1)} %get-tuple-element.156) | copy-start | bytes 10756
  57.5 28.3 %copy-start.18 = (bf16[16,64,768]{2,1,0:T(8,128)(2,1)}, bf16[16,64,768]{2,1,0:T(8,128)(2,1)S(1)}, u32[]{:S(2)}) copy-start(bf16[16,64,768]{2,1,0:T(8,128)(2,1)S(1)} %get-tuple-element.72.refs_0_) | copy-start | bytes 4718596
  57.5 28.3 %copy-start.22 = (f32[448,768]{1,0:T(8,128)}, f32[448,768]{1,0:T(8,128)S(1)}, u32[]{:S(2)}) copy-start(f32[448,768]{1,0:T(8,128)S(1)} %get-tuple-element.73.refs_1_) | copy-start | bytes 4128772
  57.6 28.3 %copy-start.45 = (f32[448,128]{1,0:T(8,128)}, f32[448,128]{1,0:T(8,128)S(1)}, u32[]{:S(2)}) copy-start(f32[448,128]{1,0:T(8,128)S(1)} %get-tuple-element.74.refs_2_) | copy-start | bytes 688132
  106.6 20.1 %copy-start.34 = (s32[1,2,224,2]{3,2,1,0:T(8,128)S(1)}, s32[1,2,224,2]{3,2,1,0:T(8,128)}, u32[]{:S(2)}) copy-start(s32[1,2,224,2]{3,2,1,0:T(8,128)} %get-tuple-element.155) | copy-start | bytes 10756
  106.6 20.1 %copy-start.36 = (s32[1,2,224,2]{3,2,1,0:T(8,128)S(1)}, s32[1,2,224,2]{3,2,1,0:T(8,128)}, u32[]{:S(2)}) copy-start(s32[1,2,224,2]{3,2,1,0:T(8,128)} %copy-done.35) | copy-start | bytes 10756
  126.6 49.2 %copy-start.32 = (bf16[448,576]{1,0:T(8,128)(2,1)}, bf16[448,576]{1,0:T(8,128)(2,1)S(1)}, u32[]{:S(2)}) copy-start(bf16[448,576]{1,0:T(8,128)(2,1)S(1)} %get-tuple-element.93.refs_12_.refs_9_) | copy-start | bytes 1548292
  146.6 29.3 %copy-start.5 = (bf16[16,64,768]{2,1,0:T(8,128)(2,1)}, bf16[16,64,768]{2,1,0:T(8,128)(2,1)S(1)}, u32[]{:S(2)}) copy-start(bf16[16,64,768]{2,1,0:T(8,128)(2,1)S(1)} %get-tuple-element.78.refs_0_.refs_6_.refs_4_.refs_8_) | copy-start | bytes 4718596
  146.6 29.3 %copy-start.9 = (f32[448,768]{1,0:T(8,128)}, f32[448,768]{1,0:T(8,128)S(1)}, u32[]{:S(2)}) copy-start(f32[448,768]{1,0:T(8,128)S(1)} %get-tuple-element.79.refs_1_.refs_6_.refs_3_) | copy-start | bytes 4128772
  175.9 13.8 %copy-start.67 = (bf16[2,394,768]{2,0,1:T(2,128)(2,1)S(1)}, bf16[2,394,768]{2,0,1:T(2,128)(2,1)}, u32[]{:S(2)}) copy-start(bf16[2,394,768]{2,0,1:T(2,128)(2,1)} %param.12) | copy-start | bytes 3631108
  189.7 66.0 %copy-start.37 = (bf16[2,448,192]{2,1,0:T(8,128)(2,1)}, bf16[2,448,192]{2,1,0:T(8,128)(2,1)S(1)}, u32[]{:S(2)}) copy-start(bf16[2,448,192]{2,1,0:T(8,128)(2,1)S(1)} %get-tuple-element.87.refs_5_.refs_2_) | copy-start | bytes 1032196
  217.8 36.8 %copy-start.58 = (bf16[448,192]{1,0:T(8,128)(2,1)}, bf16[448,192]{1,0:T(8,128)(2,1)S(1)}, u32[]{:S(2)}) copy-start(bf16[448,192]{1,0:T(8,128)(2,1)S(1)} %get-tuple-element.104) | copy-start | bytes 516100
  217.8 36.8 %copy-start.19 = (bf16[16,64,768]{2,1,0:T(8,128)(2,1)S(1)}, bf16[16,64,768]{2,1,0:T(8,128)(2,1)}, u32[]{:S(2)}) copy-start(bf16[16,64,768]{2,1,0:T(8,128)(2,1)} %copy-done.18) | copy-start | bytes 4718596
  255.7 33.8 %copy-start.21 = (bf16[448,768]{1,0:T(8,128)(2,1)S(1)}, bf16[448,768]{1,0:T(8,128)(2,1)}, u32[]{:S(2)}) copy-start(bf16[448,768]{1,0:T(8,128)(2,1)} %copy-done.20) | copy-start | bytes 2064388
  255.7 33.8 %copy-start.33 = (bf16[448,576]{1,0:T(8,128)(2,1)S(1)}, bf16[448,576]{1,0:T(8,128)(2,1)}, u32[]{:S(2)}) copy-start(bf16[448,576]{1,0:T(8,128)(2,1)} %copy-done.32) | copy-start | bytes 1548292
  255.7 33.8 %copy-start.48 = (bf16[448,192]{1,0:T(8,128)(2,1)S(1)}, bf16[448,192]{1,0:T(8,128)(2,1)}, u32[]{:S(2)}) copy-start(bf16[448,192]{1,0:T(8,128)(2,1)} %copy-done.47) | copy-start | bytes 516100
  289.5 29.7 %copy-start.12 = (bf16[1,2,224,768]{3,2,1,0:T(8,128)(2,1)S(1)}, bf16[1,2,224,768]{3,2,1,0:T(8,128)(2,1)}, u32[]{:S(2)}) copy-start(bf16[1,2,224,768]{3,2,1,0:T(8,128)(2,1)} %copy-done.10) | copy-start | bytes 2064388
  341.8 33.1 %copy-start.55 = (bf16[2,448,192]{2,1,0:T(8,128)(2,1)S(1)}, bf16[2,448,192]{2,1,0:T(8,128)(2,1)}, u32[]{:S(2)}) copy-start(bf16[2,448,192]{2,1,0:T(8,128)(2,1)} %copy-done.54) | copy-start | bytes 1032196
  418.1 53.1 %copy-start.13 = (bf16[4,112,768]{2,1,0:T(8,128)(2,1)}, bf16[4,112,768]{2,1,0:T(8,128)(2,1)S(1)}, u32[]{:S(2)}) copy-start(bf16[4,112,768]{2,1,0:T(8,128)(2,1)S(1)} %get-tuple-element.105) | copy-start | bytes 2064388
  418.2 21.8 %copy-start.6 = (bf16[16,64,768]{2,1,0:T(8,128)(2,1)S(1)}, bf16[16,64,768]{2,1,0:T(8,128)(2,1)}, u32[]{:S(2)}) copy-start(bf16[16,64,768]{2,1,0:T(8,128)(2,1)} %copy-done.5) | copy-start | bytes 4718596
  440.0 31.3 %copy-start.38 = (bf16[2,448,192]{2,1,0:T(8,128)(2,1)S(1)}, bf16[2,448,192]{2,1,0:T(8,128)(2,1)}, u32[]{:S(2)}) copy-start(bf16[2,448,192]{2,1,0:T(8,128)(2,1)} %copy-done.37) | copy-start | bytes 1032196
  471.2 65.4 %copy-start.44 = (bf16[16,64,768]{2,1,0:T(8,128)(2,1)}, bf16[16,64,768]{2,1,0:T(8,128)(2,1)S(1)}, u32[]{:S(2)}) copy-start(bf16[16,64,768]{2,1,0:T(8,128)(2,1)S(1)} %get-tuple-element.127.refs_5_) | copy-start | bytes 4718596
  471.2 12.6 %copy-start.61 = (bf16[224,384]{1,0:T(8,128)(2,1)S(1)}, bf16[224,384]{1,0:T(8,128)(2,1)}, u32[]{:S(2)}) copy-start(bf16[224,384]{1,0:T(8,128)(2,1)} %copy-done.60) | copy-start | bytes 516100
  471.2 12.6 %copy-start.63 = (bf16[224,384]{1,0:T(8,128)(2,1)S(1)}, bf16[224,384]{1,0:T(8,128)(2,1)}, u32[]{:S(2)}) copy-start(bf16[224,384]{1,0:T(8,128)(2,1)} %copy-done.62) | copy-start | bytes 516100
  483.8 52.8 %copy-start.14 = (bf16[4,112,768]{2,1,0:T(8,128)(2,1)S(1)}, bf16[4,112,768]{2,1,0:T(8,128)(2,1)}, u32[]{:S(2)}) copy-start(bf16[4,112,768]{2,1,0:T(8,128)(2,1)} %copy-done.13) | copy-start | bytes 2064388
  483.8 52.8 %copy-start.29 = (bf16[4,224,384]{2,1,0:T(8,128)(2,1)S(1)}, bf16[4,224,384]{2,1,0:T(8,128)(2,1)}, u32[]{:S(2)}) copy-start(bf16[4,224,384]{2,1,0:T(8,128)(2,1)} %copy-done.27) | copy-start | bytes 2064388
  483.9 52.8 %copy-start.31 = (bf16[4,224,384]{2,1,0:T(8,128)(2,1)S(1)}, bf16[4,224,384]{2,1,0:T(8,128)(2,1)}, u32[]{:S(2)}) copy-start(bf16[4,224,384]{2,1,0:T(8,128)(2,1)} %copy-done.30) | copy-start | bytes 2064388
  (38 other events, 86.9 us)

commit v3 on v2

v3 whole, which is shorter than its diff:
```python
from types import SimpleNamespace

import jax
import jax.numpy as jnp
from jax import lax
from jax.experimental import pallas as pl
from jax.experimental.pallas import tpu as pltpu
from jax.sharding import PartitionSpec as P

TENSOR, PIPE, DP = "tensor", "pipe", "dp"
BF = jnp.bfloat16
F32 = jnp.float32
MESH = pl.DeviceIdType.MESH
D = 768
HD = 64
NH = 3
GW = NH * HD
IMG_LEN = 197
R = 224
NR = 2 * R
CH = NR // 4
EXPERTS = 32
SL = 32
NT = 4
NDP = 16
Q = D // NT
EPSILON = 1e-06
VMEM_BYTES = 58 * 1024 * 1024
GP = 896


def dot(a, b, ca=1, cb=0):
    return lax.dot_general(a, b, (((ca,), (cb,)), ((), ())), preferred_element_type=F32)


def params(**more):
    return pltpu.CompilerParams(vmem_limit_bytes=VMEM_BYTES, **more)


def norm_parts(values):
    mean = jnp.mean(values, axis=-1, keepdims=True)
    centred = values - mean
    inverse = lax.rsqrt(jnp.mean(centred * centred, axis=-1, keepdims=True) + EPSILON)
    return centred * inverse, inverse


def norm_back(delta, gain, normal, inverse):
    scaled = delta * gain
    return inverse * (
        scaled
        - jnp.mean(scaled, axis=-1, keepdims=True)
        - normal * jnp.mean(scaled * normal, axis=-1, keepdims=True)
    )


def pick(index, options):
    result = options[0]
    for number in range(1, len(options)):
        result = jnp.where(index == number, options[number], result)
    return result


def column_quarter(values, member):
    return pick(member, [values[:, Q * q : Q * (q + 1)] for q in range(NT)])


def unpack(packed):
    images = [
        jnp.concatenate([packed[q][:, Q * i : Q * (i + 1)] for q in range(NT)], axis=1)
        for i in range(2)
    ]
    return jnp.concatenate(images, axis=0)


def head_parts(projected, image, head):
    rows = slice(image * R, (image + 1) * R)
    return [
        projected[rows, part * GW + head * HD : part * GW + (head + 1) * HD] for part in range(3)
    ]


def probabilities(queries, keys):
    scores = dot(queries, keys, 1, 1) * (HD**-0.5)
    held = lax.broadcasted_iota(jnp.int32, scores.shape, 1) < IMG_LEN
    scores = jnp.where(held, scores, -1e30)
    exponent = jnp.exp(scores - jnp.max(scores, axis=-1, keepdims=True))
    return exponent / jnp.sum(exponent, axis=-1, keepdims=True)


VMEM = pl.BlockSpec(memory_space=pltpu.VMEM)
SMEM = pl.BlockSpec(memory_space=pltpu.SMEM)
ANYWHERE = pl.BlockSpec(memory_space=pl.ANY)


def drive(*running):
    running = list(running)
    while running:
        for steps in list(running):
            if next(steps, StopIteration) is StopIteration:
                running.remove(steps)


OUT, SEM, SOURCE = "out ", "sem ", ("/0", "/1")


def prefixed(prefix, items):
    return {prefix + name: item for name, item in items.items()}


class Frame:
    def __init__(self, barrier, count):
        self.barrier = barrier
        self.count = count
        self.met = False
        self.loading = {}
        self.storing = []
        self.refs = {}

    def meet(self):
        if not self.met:
            pl.semaphore_wait(self.barrier, self.count)
            self.met = True

    def __getattr__(self, name):
        if name in self.loading:
            self.loading.pop(name).wait()
        return self.refs[name]

    def group(self, prefix):
        size = len(prefix)
        return SimpleNamespace(
            **{name[size:]: ref for name, ref in self.refs.items() if name[:size] == prefix}
        )

    def flush(self, *refs):
        for ref in refs:
            name = next(name for name, known in self.refs.items() if known is ref)
            copy = pltpu.make_async_copy(ref, self.refs[OUT + name], self.refs[SEM + name])
            copy.start()
            self.storing.append(copy)


def greet(axes):
    barrier = pltpu.get_barrier_semaphore()
    count = 0
    for axis in axes:
        size = lax.axis_size(axis)
        me = lax.axis_index(axis)
        for step in range(1, size):
            pl.semaphore_signal(
                barrier, inc=1, device_id={axis: (me + step) % size}, device_id_type=MESH
            )
        count += size - 1
    return barrier, count


def launch(name, number, axes, plain, lazy, outs, scratch, program):
    arrays, specs, places = [], [], []
    for key, (array, spec) in plain.items():
        arrays.append(array)
        specs.append(spec)
        places.append(key)
    for key, item in lazy.items():
        for position, array in enumerate(item if isinstance(item, tuple) else (item,)):
            arrays.append(array)
            specs.append(ANYWHERE)
            places.append(key + SOURCE[position])
    held = dict(scratch)
    for key, item in lazy.items():
        array = item[0] if isinstance(item, tuple) else item
        held[key] = pltpu.VMEM(array.shape, array.dtype)
        held[SEM + key] = pltpu.SemaphoreType.DMA
    for key, (shape, dtype) in outs.items():
        held[key] = pltpu.VMEM(shape, dtype)
        held[SEM + key] = pltpu.SemaphoreType.DMA

    def kernel(*refs):
        frame = Frame(*greet(axes))
        names = places + [OUT + key for key in outs] + list(held)
        frame.refs = dict(zip(names, refs))
        stage = lax.axis_index(PIPE)
        for key, item in lazy.items():
            target, sem = frame.refs[key], frame.refs[SEM + key]
            copy = pltpu.make_async_copy(frame.refs[key + SOURCE[0]], target, sem)
            if isinstance(item, tuple):
                other = pltpu.make_async_copy(frame.refs[key + SOURCE[1]], target, sem)
                pl.when(stage == 0)(copy.start)
                pl.when(stage != 0)(other.start)
            else:
                copy.start()
            frame.loading[key] = copy
        program(frame)
        for copy in list(frame.loading.values()) + frame.storing:
            copy.wait()

    results = pl.pallas_call(
        kernel,
        in_specs=specs,
        out_specs=[ANYWHERE] * len(outs),
        out_shape=[jax.ShapeDtypeStruct(*out) for out in outs.values()],
        scratch_shapes=list(held.values()),
        compiler_params=params(collective_id=number, has_side_effects=True),
        name=name,
    )(*arrays)
    return SimpleNamespace(**dict(zip(outs, results)))


def send(source, target, send_sem, recv_sem, axis, peer):
    copy = pltpu.make_async_remote_copy(
        src_ref=source,
        dst_ref=target,
        send_sem=send_sem,
        recv_sem=recv_sem,
        device_id={axis: peer},
        device_id_type=MESH,
    )
    copy.start()
    return copy


def sems(*shape):
    return pltpu.SemaphoreType.DMA(shape)


def spread_over_tensor(source, target_of, pairs, row):
    me = lax.axis_index(TENSOR)
    return [
        send(
            source, target_of(me), pairs.at[row, step], pairs.at[row + 1, step], TENSOR,
            (me + step) % NT,
        )
        for step in range(1, NT)
    ]


def padded(values):
    kind = values.dtype
    values = values if kind == jnp.int32 else values.astype(F32)
    blank = jnp.zeros((R - IMG_LEN, values.shape[1]), values.dtype)
    return jnp.concatenate(
        [values[:IMG_LEN], blank, values[IMG_LEN:], blank], axis=0
    ).astype(kind)


def forward_scratch():
    return dict(
        a_part=pltpu.VMEM((NT, CH, D), BF),
        a_held=pltpu.VMEM((NT, CH, D), BF),
        a_mine=pltpu.VMEM((CH, D), BF),
        a_pairs=sems(4, NT),
        d_hot=pltpu.VMEM((NR, EXPERTS * SL), BF),
        d_match=pltpu.VMEM((2, NR, EXPERTS), F32),
    )


FORWARD_OUTS = dict(
    state=((NR, D), BF),
    qkv=((NR, 3 * GW), BF),
    ctx=((NR, GW), BF),
    summed=((NT, CH, D), BF),
    meta=((NR, 128), F32),
    arrived=((NDP, 2 * SL, D), BF),
)


def attention_steps(f, state):
    part, held, mine, pairs = (f.a_part, f.a_held, f.a_mine, f.a_pairs)
    qkv, ctx, summed = f.qkv, f.ctx, f.summed
    f.state[...] = state
    normal, _ = norm_parts(state.astype(F32))
    normed = (normal * f.gain_one[...]).astype(BF)
    projected = dot(normed, f.project[...], 1, 1).astype(BF)
    qkv[...] = projected
    for image in range(2):
        for head in range(NH):
            queries, keys, values = head_parts(projected, image, head)
            weights = probabilities(queries, keys).astype(BF)
            ctx[image * R : (image + 1) * R, head * HD : (head + 1) * HD] = dot(
                weights, values
            ).astype(BF)
    part[...] = dot(ctx[...], f.output[...]).astype(BF).reshape(NT, CH, D)
    f.meet()
    me = lax.axis_index(TENSOR)
    copies = [
        send(
            part.at[(me + step) % NT], held.at[me], pairs.at[0, step], pairs.at[1, step],
            TENSOR, (me + step) % NT,
        )
        for step in range(1, NT)
    ]
    f.flush(f.state, f.qkv, f.ctx)
    yield
    for copy in copies:
        copy.wait()
    total = part[me].astype(F32)
    for step in range(1, NT):
        total = total + held[(me + step) % NT].astype(F32)
    mine[...] = total.astype(BF)
    copies = spread_over_tensor(mine, lambda me: summed.at[me], pairs, 2)
    summed[me] = mine[...]
    yield
    for copy in copies:
        copy.wait()
    f.flush(f.summed)


RELATIVE = [(dy, dx, dc) for dy in (2, 1, 3, 0) for dx in (1, 0) for dc in (0, 1)]
RELATIVE.remove((0, 0, 0))


def peer_at(relative, sign):
    dy, dx, dc = relative
    me = lax.axis_index(DP)
    row = (me // 4 + sign * dy + 4) % 4
    return row * 4 + ((me // 2 + dx) % 2) * 2 + (me + dc) % 2


def quartered(relative):
    return relative[0] != 0 and relative[1] == 1


SHORT = [relative for relative in RELATIVE if quartered(relative)]


def to_experts(outbox, arrived, pairs, relayed, hybrid):
    me = lax.axis_index(DP)
    member = lax.axis_index(TENSOR)
    rows = pl.ds(pl.multiple_of(member * 16, 16), 16)
    direct, relays, order = [], [], []
    for number, relative in enumerate(RELATIVE):
        peer = peer_at(relative, 1)
        short = hybrid and quartered(relative)
        copy = send(
            outbox.at[peer, rows] if short else outbox.at[peer],
            arrived.at[me, rows] if short else arrived.at[me],
            pairs.at[0, number],
            pairs.at[1, number],
            DP,
            peer,
        )
        if short:
            order.append((number, relative, copy))
        else:
            direct.append(copy)
    arrived[me] = outbox[me]
    yield
    order.sort(key=lambda item: item[1][0] == 2)
    for _, relative, copy in order:
        number = SHORT.index(relative)
        copy.wait_recv()
        source = peer_at(relative, -1)
        for step in range(1, NT):
            relays.append(
                send(
                    arrived.at[source, rows],
                    arrived.at[source, rows],
                    relayed.at[0, number, step],
                    relayed.at[1, number, step],
                    TENSOR,
                    (member + step) % NT,
                )
            )
    for _ in range(6):
        yield
    for copy in direct:
        copy.wait()
    for _, _, copy in order:
        copy.wait_send()
    for copy in relays:
        copy.wait()


def to_experts_scratch(hybrid):
    return dict(
        outbox=pltpu.VMEM((NDP, 2 * SL, D), BF),
        pairs=sems(2, NDP),
        relayed=sems(2, len(SHORT), NT) if hybrid else sems(2, 1, 1),
    )


def live_rows(count):
    row = lax.broadcasted_iota(jnp.int32, (NR, 1), 0)
    image = (row >= R).astype(jnp.int32)
    return (image < count) & (row - image * R < IMG_LEN)


def places_steps(f, count, routes):
    meta = f.meta
    live = live_rows(count)
    experts = lax.broadcasted_iota(jnp.int32, (NR, EXPERTS), 1)
    route = [routes[:, k : k + 1] for k in range(2)]
    match = [jnp.where(live & (route[k] == experts), 1.0, 0.0) for k in range(2)]
    above = lax.broadcasted_iota(jnp.int32, (NR, NR), 1) < lax.broadcasted_iota(
        jnp.int32, (NR, NR), 0
    )
    before = dot(jnp.where(above, 1.0, 0.0).astype(BF), (match[0] + match[1]).astype(BF))
    hot = None
    slots = lax.broadcasted_iota(jnp.int32, (NR, EXPERTS * SL), 1)
    for k in range(2):
        slot = jnp.sum(match[k] * before, axis=1, keepdims=True).astype(jnp.int32)
        position = jnp.where(live, route[k] * SL + slot, -1)
        meta[:, 34 + k : 35 + k] = position.astype(F32)
        meta[:, 36 + k : 37 + k] = route[k].astype(F32)
        f.d_match[k] = match[k]
        same = slots == position
        hot = same if hot is None else hot | same
    meta[:, 38:39] = jnp.where(live, 1.0, 0.0)
    f.d_hot[...] = jnp.where(hot, 1.0, 0.0).astype(BF)
    yield


def dispatch_steps(f, hybrid):
    state, summed, meta = f.state, f.summed, f.meta
    outbox, arrived = f.d_outbox, f.arrived
    values = state[...].astype(F32) + summed[...].reshape(NR, D).astype(F32)
    normal, _ = norm_parts(values)
    normed = (normal * f.gain_two[...]).astype(BF)
    outbox[...] = dot(f.d_hot[...], normed, 0, 0).astype(BF).reshape(NDP, 2 * SL, D)
    f.meet()
    sending = to_experts(outbox, arrived, f.d_pairs, f.d_relayed, hybrid)
    next(sending)
    logits = dot(normed, f.router[...], 1, 1)
    exponent = jnp.exp(logits - jnp.max(logits, axis=-1, keepdims=True))
    gate = exponent / jnp.sum(exponent, axis=-1, keepdims=True)
    meta[:, 0:EXPERTS] = gate
    for k in range(2):
        meta[:, 32 + k : 33 + k] = jnp.sum(f.d_match[k] * gate, axis=1, keepdims=True)
    f.flush(f.meta)
    yield
    yield from sending
    f.flush(f.arrived)


def spread_steps(f, hybrid, delta, meta):
    outbox, arrived = f.s_outbox, f.delta_arrived
    values = delta[...].astype(F32) * meta[:, 38:39]
    slots = lax.broadcasted_iota(jnp.int32, (NR, EXPERTS * SL), 1)
    total = None
    for k in range(2):
        position = meta[:, 34 + k : 35 + k].astype(jnp.int32)
        hot = jnp.where(slots == position, 1.0, 0.0).astype(BF)
        scaled = (values * meta[:, 32 + k : 33 + k]).astype(BF)
        term = dot(hot, scaled, 0, 0)
        total = term if total is None else total + term
    outbox[...] = total.astype(BF).reshape(NDP, 2 * SL, D)
    f.meet()
    yield from to_experts(outbox, arrived, f.s_pairs, f.s_relayed, hybrid)
    f.flush(f.delta_arrived)


CUBE = 0.044715
ROOT = 0.7978845608028654


def gelu_parts(pre):
    squared = pre * pre
    inner = jnp.tanh(ROOT * (pre + CUBE * pre * squared))
    return 0.5 * pre * (1.0 + inner), inner, squared


def store_quarters(target, expert, values):
    values = values.astype(BF).reshape(NDP, 2, 16, D)
    for q in range(NT):
        for half in range(2):
            target[q, expert, :, :, half * Q : (half + 1) * Q] = values[
                :, half, :, q * Q : (q + 1) * Q
            ]


def expert_steps(f, key, compute):
    part, held, mine, sums, pairs = (key.part, key.held, key.mine, key.sums, key.pairs)
    store_quarters(part, 0, compute(0))
    f.meet()
    me = lax.axis_index(TENSOR)
    home = lax.axis_index(DP)
    whole = [
        send(
            part.at[(me + step) % NT, 0], held.at[me, 0], sums.at[0, 4, step], sums.at[1, 4, step],
            TENSOR, (me + step) % NT,
        )
        for step in range(1, NT)
    ]
    yield
    store_quarters(part, 1, compute(1))
    group = home // 4
    scattered = []
    for turn in range(4):
        block = ((group + turn + 1) % 4) * 4
        for step in range(1, NT):
            peer = (me + step) % NT
            scattered.append(
                send(
                    part.at[peer, 1, pl.ds(block, 4)],
                    held.at[me, 1, pl.ds(block, 4)],
                    sums.at[0, turn, step],
                    sums.at[1, turn, step],
                    TENSOR,
                    peer,
                )
            )
    yield
    for copy in whole:
        copy.wait()
    total = part[me, 0].astype(F32)
    for step in range(1, NT):
        total = total + held[(me + step) % NT, 0].astype(F32)
    mine[:, 0] = total.astype(BF)
    returned = []
    for turn in range(4):
        block = ((group + turn + 1) % 4) * 4
        for step in range(1, NT):
            scattered[turn * 3 + step - 1].wait_recv()
        total = part[me, 1, pl.ds(block, 4)].astype(F32)
        for step in range(1, NT):
            total = total + held[(me + step) % NT, 1, pl.ds(block, 4)].astype(F32)
        mine[pl.ds(block, 4), 1] = total.astype(BF)
        for number in range(4):
            if turn == 3 and number == 0:
                key.returned[home] = mine[home]
                continue
            offset = (turn + 1) % 4 * 4 + number
            peer = block + (home + number) % 4
            returned.append(
                send(
                    mine.at[peer], key.returned.at[home], pairs.at[0, offset], pairs.at[1, offset], DP,
                    peer,
                )
            )
        yield
    for copy in returned:
        copy.wait()
    for copy in scattered:
        copy.wait_send()


def expert_scratch():
    return dict(
        part=pltpu.VMEM((NT, 2, NDP, 16, 2 * Q), BF),
        held=pltpu.VMEM((NT, 2, NDP, 16, 2 * Q), BF),
        mine=pltpu.VMEM((NDP, 2, 16, 2 * Q), BF),
        sums=sems(2, 5, NT),
        pairs=sems(2, NDP),
        returned=pltpu.VMEM((NDP, 2, 16, 2 * Q), BF),
    )


def expert_rows(ref, expert):
    return ref[:, expert * SL : (expert + 1) * SL].reshape(NDP * SL, D)


def experts_forward_steps(f, arrived):
    def compute(expert):
        hidden = gelu_parts(dot(expert_rows(arrived, expert), f.first[expert]))[0].astype(BF)
        return dot(hidden, f.second[expert])

    yield from expert_steps(f, f.group("f_"), compute)


def experts_backward_steps(f, arrived):
    delta, hidden_out, dpre_out = f.delta_arrived, f.hidden, f.dpre

    def compute(expert):
        place = slice(expert * SL, (expert + 1) * SL)
        pre = dot(expert_rows(arrived, expert), f.first[expert])
        hidden, inner, squared = gelu_parts(pre)
        hidden_out[:, place] = hidden.astype(BF).reshape(NDP, SL, D)
        slope = 0.5 * (1.0 + inner) + (0.5 * ROOT) * pre * (1.0 - inner * inner) * (
            1.0 + 3.0 * CUBE * squared
        )
        dhidden = dot(expert_rows(delta, expert), f.second[expert], 1, 1)
        dpre = (dhidden.astype(BF).astype(F32) * slope).astype(BF)
        dpre_out[:, place] = dpre.reshape(NDP, SL, D)
        result = dot(dpre, f.first[expert], 1, 1)
        if expert == 1:
            f.flush(f.hidden, f.dpre)
        return result

    yield from expert_steps(f, f.group("b_"), compute)


def expert_grads_kernel(stage, *refs):
    grad_first, grad_second = refs[12:]

    def flat(ref):
        return ref[...].reshape(NDP * SL, D)

    def pairs(a, b):
        grad_first[0] = dot(flat(a[0]), flat(a[1]), 0, 0) + dot(flat(b[0]), flat(b[1]), 0, 0)
        grad_second[0] = dot(flat(a[2]), flat(a[3]), 0, 0) + dot(flat(b[2]), flat(b[3]), 0, 0)

    @pl.when(stage[0] == 0)
    def _():
        pairs(refs[0:4], refs[4:8])

    @pl.when(stage[0] != 0)
    def _():
        pairs(refs[0:4], refs[8:12])


def expert_grads(stage, both, first_only, last_only):
    shape = (NDP, SL, D)
    weights = pl.BlockSpec((1, D, D), lambda p, s: (p, 0, 0))
    return pl.pallas_call(
        expert_grads_kernel,
        grid_spec=pltpu.PrefetchScalarGridSpec(
            num_scalar_prefetch=1,
            grid=(2,),
            in_specs=[pl.BlockSpec(shape, lambda p, s: (0, p, 0))] * 4
            + [pl.BlockSpec(shape, lambda p, s: (0, p * (1 - s[0]), 0))] * 4
            + [pl.BlockSpec(shape, lambda p, s: (0, p * s[0], 0))] * 4,
            out_specs=[weights, weights],
        ),
        out_shape=[jax.ShapeDtypeStruct((2, D, D), F32)] * 2,
        compiler_params=params(),
        name="expert_grads",
    )(stage, *both, *first_only, *last_only)


def hot_steps(meta, hots):
    yield
    for k in range(2):
        position = meta[:, 34 + k : 35 + k].astype(jnp.int32)
        place = jnp.where(position >= 0, (position // SL) * 16 + position % 16, -1)
        hot = lax.broadcasted_iota(jnp.int32, (NR, NDP * SL), 1) == place
        hots[k] = jnp.where(hot, 1.0, 0.0).astype(BF)


def gathered(returned, meta, k, hots):
    position = meta[:, 34 + k : 35 + k].astype(jnp.int32)
    odd = (position // 16) % 2 == 1
    both = dot(hots[k], returned)
    return jnp.where(odd, both[:, Q:], both[:, :Q])


HOTS = pltpu.VMEM((2, NR, NDP * SL), BF)
HALVES = (slice(0, CH), slice(CH, R))


def combine_steps(f, onward, meta, hots):
    packed, pieces, returned = f.packed, f.pieces, f.f_returned
    member = lax.axis_index(TENSOR)
    live = meta[:, 38:39]
    total = column_quarter(f.state[...], member).astype(F32) + column_quarter(
        f.summed[...].reshape(NR, D), member
    ).astype(F32)
    rows = returned[...].reshape(NDP * SL, 2 * Q)
    for k in range(2):
        piece = gathered(rows, meta, k, hots)
        pieces[k] = piece.astype(BF)
        total = total + meta[:, 32 + k : 33 + k] * piece
    total = (total * live).astype(BF)
    packed[:, :Q] = total[:R]
    packed[:, Q:] = total[R:]
    f.flush(f.packed)
    if not onward:
        return
    f.flush(f.pieces)
    result = f.onward
    near, chosen, across_sems, pairs = (f.c_near, f.c_chosen, f.c_across, f.c_pairs)
    stage = lax.axis_index(PIPE)
    across = [
        send(
            packed.at[half], near.at[half], across_sems.at[0, i], across_sems.at[1, i], PIPE,
            1 - stage,
        )
        for i, half in enumerate(HALVES)
    ]
    copies = []
    for i, half in enumerate(HALVES):
        across[i].wait_recv()
        chosen[half] = jnp.where(stage == 0, packed[half], near[half])
        copies += spread_over_tensor(
            chosen.at[half], lambda me: result.at[me, half], pairs, 2 * i
        )
    result[member] = chosen[...]
    yield
    for copy in copies:
        copy.wait()
    for copy in across:
        copy.wait_send()
    f.flush(f.onward)


def combine_scratch():
    return dict(
        c_near=pltpu.VMEM((R, 2 * Q), BF),
        c_chosen=pltpu.VMEM((R, 2 * Q), BF),
        c_across=sems(2, 2),
        c_pairs=sems(4, NT),
        h_hot=HOTS,
    )


def collect_steps(f, meta, pieces, delta):
    returned, result, dpicks_all = f.b_returned, f.g_result, f.g_dpicks_all
    packed, dpicks, pairs = f.g_packed, f.g_dpicks, f.g_pairs
    member = lax.axis_index(TENSOR)
    total = None
    rows = returned[...].reshape(NDP * SL, 2 * Q)
    lanes = lax.broadcasted_iota(jnp.int32, (NR, 128), 1)
    columns = jnp.zeros((NR, 128), F32)
    part = column_quarter(delta[...], member).astype(F32) * meta[:, 38:39]
    for k in range(2):
        piece = gathered(rows, meta, k, f.h_hot)
        total = piece if total is None else total + piece
        dots = jnp.sum(pieces(k).astype(F32) * part, axis=1, keepdims=True)
        columns = jnp.where(lanes == k, dots, columns)
    total = total.astype(BF)
    packed[:, :Q] = total[:R]
    packed[:, Q:] = total[R:]
    dpicks[:, :NR] = jnp.transpose(columns)[:8]
    dpicks[:, NR:] = jnp.zeros((8, 512 - NR), F32)
    copies = spread_over_tensor(packed, lambda me: result.at[me], pairs, 0)
    copies += spread_over_tensor(dpicks, lambda me: dpicks_all.at[me], pairs, 2)
    result[member] = packed[...]
    dpicks_all[member] = dpicks[...]
    yield
    for copy in copies:
        copy.wait()


def collect_scratch():
    return dict(
        g_packed=pltpu.VMEM((R, 2 * Q), BF),
        g_dpicks=pltpu.VMEM((8, 512), F32),
        g_pairs=sems(4, NT),
        g_result=pltpu.VMEM((NT, R, 2 * Q), BF),
        g_dpicks_all=pltpu.VMEM((NT, 8, 512), F32),
    )


def halves(values):
    high = values.astype(BF)
    return high, (values - high.astype(F32)).astype(BF)


RS_ROWS = ((0, 64), (64, 48))
GR = D // NDP


def sum_dp(pack, result, near, half, held, mine, tile, tiles, core_sems, chip_sems, tile_sems):
    home = lax.axis_index(DP)
    core = home % 2
    chip = home // 2
    partner = home + 1 - 2 * core
    copy = send(pack.at[1 - core], near, core_sems.at[0, 0], core_sems.at[1, 0], DP, partner)
    yield
    copy.wait()
    half[...] = (pack[core].astype(F32) + near[...].astype(F32)).astype(BF)
    chips = [(dy, dx) for dy in (2, 1, 3, 0) for dx in (1, 0) if (dy, dx) != (0, 0)]

    def chip_at(dy, dx):
        return ((chip // 2 + dy) % 4) * 2 + (chip + dx) % 2

    copies = []
    for number, (dy, dx) in enumerate(chips):
        other = chip_at(dy, dx)
        copies.append(
            send(
                half.at[other], held.at[chip], chip_sems.at[0, number], chip_sems.at[1, number],
                DP, other * 2 + core,
            )
        )
    yield
    for copy in copies:
        copy.wait()
    total = half[chip].astype(F32)
    for step in range(1, 8):
        total = total + held[(chip + step) % 8].astype(F32)
    mine[...] = total[:, :768].astype(BF)
    tile[...] = total[:, 768:]
    small = spread_over_tensor(tile, lambda me: tiles.at[me], tile_sems, 0)
    copies = []
    for number, (dy, dx) in enumerate(chips):
        other = chip_at(dy, dx)
        copies.append(
            send(
                mine, result.at[core, chip, :, pl.ds(0, 768)], chip_sems.at[2, number],
                chip_sems.at[3, number], DP, other * 2 + core,
            )
        )
    result[core, chip, :, 0:768] = mine[...]
    yield
    for copy in small:
        copy.wait()
    me = lax.axis_index(TENSOR)
    others = tile[...]
    for step in range(1, NT):
        others = others + tiles[(me + step) % NT]
    lanes = lax.broadcasted_iota(jnp.int32, (GR, 128), 1)
    result[core, chip, :, 768:] = jnp.where(lanes == 33, others, tile[...]).astype(BF)
    for number, (dy, dx) in enumerate(chips):
        other = chip_at(dy, dx)
        place = result.at[core, chip, :, pl.ds(768, 128)]
        copies.append(
            send(
                place, place, chip_sems.at[4, number], chip_sems.at[5, number], DP,
                other * 2 + core,
            )
        )
    yield
    for copy in copies:
        copy.wait()
    copy = send(
        result.at[core], result.at[core], core_sems.at[0, 1], core_sems.at[1, 1], DP, partner
    )
    yield
    copy.wait()


SUM_SCRATCH = dict(
    t_near=pltpu.VMEM((8, GR, GP), BF),
    t_half=pltpu.VMEM((8, GR, GP), BF),
    t_held=pltpu.VMEM((8, GR, GP), BF),
    t_mine=pltpu.VMEM((GR, D), BF),
    t_tile=pltpu.VMEM((GR, 128), F32),
    t_tiles=pltpu.VMEM((NT, GR, 128), F32),
    t_core=sems(2, 2),
    t_chip=sems(6, 8),
    t_tile_sems=sems(2, NT),
    t_pack=pltpu.VMEM((2, 8, GR, GP), BF),
    t_gathers=sems(6, NT),
)


def gathers(sources, targets, pairs, begin):
    def handle(chosen):
        me = lax.axis_index(TENSOR)
        for number in chosen:
            for step in range(1, NT):
                copy = pltpu.make_async_remote_copy(
                    src_ref=sources[number],
                    dst_ref=targets[number].at[me],
                    send_sem=pairs.at[2 * number, step],
                    recv_sem=pairs.at[2 * number + 1, step],
                    device_id={TENSOR: (me + step) % NT},
                    device_id_type=MESH,
                )
                if begin:
                    copy.start()
                else:
                    copy.wait()

    @pl.when(lax.axis_index(PIPE) == 0)
    def _():
        handle((0,))

    @pl.when(lax.axis_index(PIPE) == 1)
    def _():
        handle((1, 2))


def weights_steps(f):
    yield
    projected = f.qkv_in[...]
    for image in range(2):
        for head in range(NH):
            queries, keys, _ = head_parts(projected, image, head)
            f.l_weights[image * NH + head] = probabilities(queries, keys)


def layer_steps(f, last, meta, delta):
    packed, dpicks, state = f.g_result, f.g_dpicks_all, f.state_in
    dqkv, part, dx1_kept, held, near, chosen, pairs, across_sems = (
        f.l_dqkv, f.l_part, f.l_dx1, f.l_held, f.l_near, f.l_chosen, f.l_pairs, f.l_across
    )
    x1 = state[...].astype(F32) + f.summed_in[...].reshape(NR, D).astype(F32)
    live = meta[:, 38:39]
    gate = meta[:, 0:EXPERTS]
    dx2 = delta[...].astype(F32) * live
    total = dpicks[0] + dpicks[1] + dpicks[2] + dpicks[3]
    total = jnp.concatenate([total, jnp.zeros((120, 512), F32)], axis=0)
    columns = jnp.transpose(total)[:NR]
    experts = lax.broadcasted_iota(jnp.int32, (NR, EXPERTS), 1)
    dgate = jnp.zeros((NR, EXPERTS), F32)
    for k in range(2):
        route = meta[:, 36 + k : 37 + k].astype(jnp.int32)
        dgate = dgate + jnp.where(route == experts, columns[:, k : k + 1] * live, 0.0)
    dlogits = gate * (dgate - jnp.sum(gate * dgate, axis=-1, keepdims=True))
    normal, inverse = norm_parts(x1)
    high, low = halves(dlogits)
    dz2 = (
        unpack(packed).astype(F32) + dot(high, f.router[...]) + dot(low, f.router[...])
    )
    dx1 = dx2 + norm_back(dz2, f.gain_two[...], normal, inverse)
    dx1_kept[...] = dx1.reshape(NT, CH, D)
    dattn = dx1.astype(BF)
    if last:
        sources = [f.own_in, f.wide_one_in, f.wide_two_in]
        targets = [f.own, f.wide_one, f.wide_two]
        gathers(sources, targets, f.t_gathers, True)
        for source, target in zip(sources, targets):
            target[lax.axis_index(TENSOR)] = source[...]
    dctx = dot(dattn, f.output[...], 1, 1).astype(BF)
    scale = HD**-0.5
    projected = f.qkv_in[...]
    for image in range(2):
        rows = slice(image * R, (image + 1) * R)
        for head in range(NH):
            queries, keys, values = head_parts(projected, image, head)
            dc = dctx[rows, head * HD : (head + 1) * HD]
            weights = f.l_weights[image * NH + head]
            dweights = dot(dc, values, 1, 1)
            dvalues = dot(weights.astype(BF), dc, 0, 0)
            dscores = weights * (dweights - jnp.sum(weights * dweights, axis=-1, keepdims=True))
            dscores = dscores.astype(BF)
            dqueries = dot(dscores, keys) * scale
            dkeys = dot(dscores, queries, 0, 0) * scale
            for number, value in enumerate((dqueries, dkeys, dvalues)):
                start = number * GW + head * HD
                dqkv[rows, start : start + HD] = value.astype(BF)
    own_part = dot(dqkv[...], f.project[...]).astype(BF)
    part[...] = own_part.reshape(NT, CH, D)
    me = lax.axis_index(TENSOR)
    stage = lax.axis_index(PIPE)
    scattered = [
        [
            send(
                part.at[(me + step) % NT, pl.ds(start, size)],
                held.at[me, pl.ds(start, size)],
                pairs.at[2 * i, step],
                pairs.at[2 * i + 1, step],
                TENSOR,
                (me + step) % NT,
            )
            for step in range(1, NT)
        ]
        for i, (start, size) in enumerate(RS_ROWS)
    ]
    normal_one, _ = norm_parts(state[...].astype(F32))
    normed_one = (normal_one * f.gain_one[...]).astype(BF)
    normed = (normal * f.gain_two[...]).astype(BF)
    gain_rows = [
        jnp.sum(dz2 * normal, axis=0, keepdims=True),
        jnp.sum(own_part.astype(F32) * normal_one, axis=0, keepdims=True),
    ]
    places = lax.broadcasted_iota(jnp.int32, (128, D), 0)
    tall = jnp.where(places == 32, gain_rows[0], 0.0)
    tall = jnp.where(places == 33, gain_rows[1], tall)
    terms = [
        (0, 576, dot(normed_one, dqkv[...], 0, 0)),
        (576, 768, dot(dattn, f.ctx_in[...], 0, 0)),
    ]
    side = jnp.transpose(tall)
    router_term = dot(normed, high, 0, 0) + dot(normed, low, 0, 0)
    side = side + jnp.concatenate([router_term, jnp.zeros((D, 96), F32)], axis=1)
    terms.append((768, GP, side))
    if last:
        one, first, pack = f.grads_one, f.grads_first, f.t_pack
        for low_end, high_end, term in terms:
            term = jnp.where(stage == 0, term, first[:, low_end:high_end])
            term = term + one[:, low_end:high_end]
            pack[:, :, :, low_end:high_end] = term.astype(BF).reshape(
                2, 8, GR, high_end - low_end
            )
        summing = sum_dp(
            pack,
            f.whole,
            f.t_near, f.t_half, f.t_held, f.t_mine, f.t_tile, f.t_tiles, f.t_core, f.t_chip,
            f.t_tile_sems,
        )
        next(summing)
        next(summing)
    else:
        for low_end, high_end, term in terms:
            f.grads[:, low_end:high_end] = term
        f.flush(f.grads)
        summing = iter(())
    waiting = []
    result = f.result
    chunk = chosen if last else f.chunk
    across = []
    for i, (start, size) in enumerate(RS_ROWS):
        rows = pl.ds(start, size)
        for copy in scattered[i]:
            copy.wait_recv()
        dz1 = part[me, rows].astype(F32)
        for step in range(1, NT):
            dz1 = dz1 + held[(me + step) % NT, rows].astype(F32)
        here = pl.ds(pl.multiple_of(me * CH + start, 16), size)
        normal_here, inverse_here = norm_parts(state[here].astype(F32))
        delta_here = norm_back(dz1, f.gain_one[...], normal_here, inverse_here)
        chunk[rows] = (dx1_kept[me, rows] + delta_here).astype(BF)
        if not last:
            across.append(
                send(
                    chunk.at[rows], near.at[rows], across_sems.at[0, i], across_sems.at[1, i],
                    PIPE, 1 - stage,
                )
            )
    for i, (start, size) in enumerate(RS_ROWS):
        rows = pl.ds(start, size)
        if not last:
            across[i].wait_recv()
            chosen[rows] = jnp.where(stage == 1, chunk[rows], near[rows])
        waiting += spread_over_tensor(
            chosen.at[rows], lambda me: result.at[me, rows], pairs, 4 + 2 * i
        )
    result[me] = chosen[...]
    yield
    for _ in summing:
        yield
    if last:
        gathers(sources, targets, f.t_gathers, False)
        f.flush(f.own, f.wide_one, f.wide_two, f.whole)
    for copy in waiting:
        copy.wait()
    for group in scattered:
        for copy in group:
            copy.wait_send()
    for copy in across:
        copy.wait_send()
    f.flush(f.result)
    if not last:
        f.flush(f.chunk)


LAYER_SCRATCH = dict(
    l_dqkv=pltpu.VMEM((NR, 3 * GW), BF),
    l_part=pltpu.VMEM((NT, CH, D), BF),
    l_dx1=pltpu.VMEM((NT, CH, D), F32),
    l_held=pltpu.VMEM((NT, CH, D), BF),
    l_near=pltpu.VMEM((CH, D), BF),
    l_chosen=pltpu.VMEM((CH, D), BF),
    l_pairs=sems(8, NT),
    l_across=sems(2, 2),
    l_weights=pltpu.VMEM((2 * NH, R, R), F32),
    h_hot=HOTS,
)
ROWS_OUT = ((NDP, 2 * SL, D), BF)
BACKWARD_OUTS = dict(
    delta_arrived=ROWS_OUT,
    hidden=ROWS_OUT,
    dpre=ROWS_OUT,
    result=((NT, CH, D), BF),
)
LINEAR_OUTS = dict(chunk=((CH, D), BF), grads=((D, GP), F32))


def finish_kernel(stage, *refs):
    states, grads, whole = refs[:4], refs[4:8], refs[8]
    section_out, input_grad, project_grad, output_grad, router_grad, gains = refs[9:]

    def rows(values):
        values = values.astype(F32)
        return jnp.concatenate([values[:IMG_LEN], values[R : R + IMG_LEN]], axis=0).astype(BF)

    def place(base):
        for micro in range(2):
            section_out[micro] = rows(unpack(states[base + micro]))
            input_grad[micro] = rows(grads[base + micro][...])

    @pl.when(stage[0, 0] == 0)
    def _():
        place(0)

    @pl.when(stage[0, 0] != 0)
    def _():
        place(2)

    project_grad[...] = jnp.transpose(whole[:, :576].astype(F32))
    output_grad[...] = jnp.transpose(whole[:, 576:768].astype(F32))
    side = whole[:, 768:].astype(F32)
    side = jnp.transpose(side)
    router_grad[...] = side[:EXPERTS]
    gains[...] = side[EXPERTS : EXPERTS + 8]


def finish(stage, states, grads, whole):
    return pl.pallas_call(
        finish_kernel,
        in_specs=[SMEM] + [VMEM] * 9,
        out_shape=[
            jax.ShapeDtypeStruct((2, 2 * IMG_LEN, D), BF),
            jax.ShapeDtypeStruct((2, 2 * IMG_LEN, D), BF),
            jax.ShapeDtypeStruct((3 * GW, D), F32),
            jax.ShapeDtypeStruct((GW, D), F32),
            jax.ShapeDtypeStruct((EXPERTS, D), F32),
            jax.ShapeDtypeStruct((8, D), F32),
        ],
        compiler_params=params(),
        name="finish",
    )(stage, *states, *grads, whole)


def body(
    tokens,
    cotangent,
    image_counts,
    routes,
    attn_norm_gain,
    query_key_value,
    attn_output,
    moe_norm_gain,
    router_weight,
    expert_in,
    expert_down,
):
    project = query_key_value[0].transpose(1, 2, 0).reshape(3 * GW, D)
    stage = lax.axis_index(PIPE)
    all_axes = (TENSOR, DP, PIPE)
    gains = dict(gain_one=(attn_norm_gain, VMEM), gain_two=(moe_norm_gain, VMEM))
    small = dict(project=project, output=attn_output[0], router=router_weight[0].T)
    heavy = dict(first=expert_in[0], second=expert_down[0])
    placing = dict(counts=(image_counts, SMEM), routes=(routes, VMEM))

    def place_of(f, moment):
        home = lax.axis_index(DP)
        one, other = min(moment, 1), max(moment - 1, 0)
        early = lax.axis_index(PIPE) == 0
        count = jnp.where(early, f.counts[one, home], f.counts[other, home])
        path = jnp.where(early, f.routes[one], f.routes[other])
        return count, padded(path)

    def forward(moment, arriving):
        def program(f):
            if moment == 0:
                state = padded(f.tokens[0])
            else:
                early = lax.axis_index(PIPE) == 0
                state = jnp.where(early, padded(f.tokens[1]), unpack(f.arriving))
            drive(attention_steps(f, state), places_steps(f, *place_of(f, moment)))
            drive(dispatch_steps(f, True))
            drive(experts_forward_steps(f, f.arrived), hot_steps(f.meta, f.h_hot))
            drive(combine_steps(f, True, f.meta, f.h_hot))

        outs = dict(FORWARD_OUTS)
        outs["packed"] = ((R, 2 * Q), BF)
        outs["pieces"] = ((2, NR, Q), BF)
        outs["onward"] = ((NT, R, 2 * Q), BF)
        plain = dict(**gains, **placing, tokens=(tokens, VMEM))
        if moment > 0:
            plain["arriving"] = (arriving, VMEM)
        return launch(
            "forward_%d" % moment, 1 + moment, all_axes, plain, dict(**small, **heavy), outs,
            dict(
                **forward_scratch(), **prefixed("d_", to_experts_scratch(True)), **prefixed("f_", expert_scratch()),
                **combine_scratch(),
            ),
            program,
        )

    def kept(saved):
        return dict(
            state_in=saved.state,
            summed_in=saved.summed,
            qkv_in=saved.qkv,
            ctx_in=saved.ctx,
            meta_in=saved.meta,
            arrived_in=saved.arrived,
        )

    def either(one, other):
        return {key: (one[key], other[key]) for key in one}

    backward_scratch = dict(**prefixed("b_", expert_scratch()), **collect_scratch(), **LAYER_SCRATCH)
    zero = forward(0, None)
    one = forward(1, zero.onward)

    def turning(f):
        state = unpack(f.arriving)
        delta = padded(f.delta[0])
        f.delta_kept[...] = delta
        drive(
            spread_steps(f, False, delta, f.meta_in),
            attention_steps(f, state),
            places_steps(f, *place_of(f, 2)),
        )
        drive(
            experts_backward_steps(f, f.arrived_in),
            dispatch_steps(f, False),
            hot_steps(f.meta_in, f.h_hot),
            weights_steps(f),
        )
        drive(
            collect_steps(f, f.meta_in, lambda k: f.pieces_in[k], f.delta_kept)
        )
        drive(layer_steps(f, False, f.meta_in, f.delta_kept))

    two = launch(
        "turning", 3, all_axes,
        dict(**gains, **placing, delta=(cotangent, VMEM), arriving=(one.onward, VMEM)),
        dict(**small, **kept(one), pieces_in=one.pieces, **heavy),
        dict(**FORWARD_OUTS, **BACKWARD_OUTS, **LINEAR_OUTS),
        dict(
            **forward_scratch(), **prefixed("d_", to_experts_scratch(False)),
            **prefixed("s_", to_experts_scratch(False)), **backward_scratch,
            delta_kept=pltpu.VMEM((NR, D), BF),
        ),
        turning,
    )

    def middle(f):
        early = lax.axis_index(PIPE) == 0
        delta = jnp.where(early, f.arriving[...].reshape(NR, D), padded(f.delta[1]))
        f.delta_kept[...] = delta
        drive(
            spread_steps(f, False, delta, f.meta_in),
            experts_forward_steps(f, f.late_arrived),
            hot_steps(f.late_meta, f.k_hot),
        )

        def combining():
            yield
            yield from combine_steps(f, False, f.late_meta, f.k_hot)

        drive(
            experts_backward_steps(f, f.arrived_in),
            combining(),
            hot_steps(f.meta_in, f.h_hot),
            weights_steps(f),
        )
        drive(
            collect_steps(
                f,
                f.meta_in,
                lambda k: jnp.where(early, f.pieces_in[k], f.pieces[k]),
                f.delta_kept,
            )
        )
        drive(layer_steps(f, False, f.meta_in, f.delta_kept))

    three = launch(
        "middle", 4, all_axes,
        dict(**gains, delta=(cotangent, VMEM), arriving=(two.result, VMEM)),
        dict(
            **either(kept(zero), kept(two)), **heavy, late_arrived=two.arrived,
            late_meta=two.meta, state=two.state, summed=two.summed,
            pieces_in=zero.pieces, **small,
        ),
        dict(**BACKWARD_OUTS, **LINEAR_OUTS, packed=((R, 2 * Q), BF)),
        dict(
            **prefixed("s_", to_experts_scratch(False)), **prefixed("f_", expert_scratch()), **backward_scratch,
            pieces=pltpu.VMEM((2, NR, Q), BF), k_hot=HOTS, delta_kept=pltpu.VMEM((NR, D), BF),
        ),
        middle,
    )

    def ending(f):
        delta = f.arriving[...].reshape(NR, D)
        f.delta_kept[...] = delta
        drive(spread_steps(f, True, delta, f.meta_in))
        drive(
            experts_backward_steps(f, f.arrived_in),
            hot_steps(f.meta_in, f.h_hot),
            weights_steps(f),
        )
        drive(
            collect_steps(f, f.meta_in, lambda k: f.pieces_in[k], f.delta_kept)
        )
        drive(layer_steps(f, True, f.meta_in, f.delta_kept))

    wide = ((NT, R, 2 * Q), BF)
    four = launch(
        "ending", 5, (TENSOR, DP),
        dict(**gains, arriving=(three.result, VMEM)),
        dict(
            **kept(one), **heavy, pieces_in=one.pieces, **small,
            own_in=three.chunk, wide_one_in=one.packed,
            wide_two_in=three.packed, grads_one=three.grads,
            grads_first=two.grads,
        ),
        dict(
            **BACKWARD_OUTS, whole=((2, 8, GR, GP), BF), own=((NT, CH, D), BF),
            wide_one=wide, wide_two=wide,
        ),
        dict(
            **prefixed("s_", to_experts_scratch(True)), **backward_scratch, **SUM_SCRATCH,
            delta_kept=pltpu.VMEM((NR, D), BF),
        ),
        ending,
    )

    def outer(saved, results):
        return (saved.arrived, results.dpre, results.hidden, results.delta_arrived)

    early = stage == 0
    middle_arrived = jnp.where(early, zero.arrived, two.arrived)
    grad_first, grad_second = expert_grads(
        stage.reshape(1).astype(jnp.int32),
        outer(SimpleNamespace(arrived=middle_arrived), three),
        outer(one, four),
        outer(one, two),
    )
    section_out, input_grad, project_grad, output_grad, router_grad, gain_grads = finish(
        stage.reshape(1, 1).astype(jnp.int32),
        [zero.onward, one.onward, four.wide_one, four.wide_two],
        [
            array.reshape(NR, D)
            for array in (four.own, four.result, two.result, three.result)
        ],
        four.whole.reshape(D, GP),
    )
    return (
        section_out[None],
        input_grad[None],
        gain_grads[1:2],
        project_grad.reshape(1, 3, GW, D).transpose(0, 3, 1, 2),
        output_grad[None],
        gain_grads[0:1],
        router_grad.T[None],
        grad_first[None],
        grad_second[None],
    )


def solution(mesh):
    placed = (
        P(None, DP, None),
        P(None, DP, None),
        P(),
        P(None, DP, None),
        P(PIPE, None),
        P(PIPE, None, None, TENSOR),
        P(PIPE, TENSOR, None),
        P(PIPE, None),
        P(PIPE, None, None),
        P(PIPE, DP, None, TENSOR),
        P(PIPE, DP, TENSOR, None),
    )
    return jax.shard_map(
        body,
        mesh=mesh,
        in_specs=placed,
        out_specs=(
            P(PIPE, None, DP, None),
            P(PIPE, None, DP, None),
            P(PIPE, None),
            P(PIPE, None, None, TENSOR),
            P(PIPE, TENSOR, None),
            P(PIPE, None),
            P(PIPE, None, None),
            P(PIPE, DP, None, TENSOR),
            P(PIPE, DP, TENSOR, None),
        ),
        check_vma=False,
    )
```

time: 569 us -> 518 us (0.910)
  local copies, waits for them, and re-layouts: 41.3 us -> 12 us
  Pallas kernels: 517 us -> 492 us
    pallas_call x20 -> x5, Pallas kernels: 502 us -> 475 us  [launch(): pl.pallas_call(kernel, in_specs=specs, out_specs=[ANYWHERE] * len(outs),...]
    unnamed x144 -> x11, local copies, waits for them, and re-layouts: 30.4 us -> 10.6 us
where the time goes in v3:
time: 518 us; the launch traced here: 508 us
  Pallas kernels  492 us (95%)
  local copies, waits for them, and re-layouts  12 us (2%)
    pallas_call x5, Pallas kernels, launch(): pl.pallas_call(kernel, in_specs=specs, out_specs=[ANYWHERE] * len(outs),...  475 us
    pallas_call x1, Pallas kernels, expert_grads(): pl.pallas_call(expert_grads_kernel, grid_spec=pltpu.PrefetchScalarGridSpe...  11.6 us
    unnamed x11, local copies, waits for them, and re-layouts  10.6 us

profile of v3, /device:TPU:7, one launch (start us, length us, event | category | flops | bytes accessed | tf_op | source)
XLA Modules:
  0.0 507.8 jit_solution(2621018300934384071)
XLA Ops:
  0.6 0.0 copy-start.2
  0.7 1.7 copy.20.refs_3_
  2.4 2.4 copy.21.refs_4_
  4.8 0.0 copy-done.2
  4.8 1.2 copy.26.refs_4_.refs_2_
  6.0 85.2 %forward_0.1 = (bf16[448,768]{1,0:T(8,128)(2,1)}, bf16[448,576]{1,0:T(8,128)(2,1)}, bf16[448,192]{1,0:T(8,128)(2,1)}, bf16[4,112,768]{2,1,0:T(8,128)(2,1)}, f32[...) custom-call(f32[1,768]{1,0:T(1,128)} %refs_0_.9, ...), custom_call_target="tpu_custom_call" | custom-call | tf_op jit(solution)/shard_map/forward_0/pallas_call | solution.py:196
  91.2 82.2 %forward_1.1 = (bf16[448,768]{1,0:T(8,128)(2,1)}, bf16[448,576]{1,0:T(8,128)(2,1)}, bf16[448,192]{1,0:T(8,128)(2,1)}, bf16[4,112,768]{2,1,0:T(8,128)(2,1)}, f32[...) custom-call(f32[1,768]{1,0:T(1,128)} %refs_0_.9, ...), custom_call_target="tpu_custom_call" | custom-call | tf_op jit(solution)/shard_map/forward_1/pallas_call | solution.py:196
  173.5 0.0 copy-start
  173.5 99.7 %turning.1 = (bf16[448,768]{1,0:T(8,128)(2,1)}, bf16[448,576]{1,0:T(8,128)(2,1)}, bf16[448,192]{1,0:T(8,128)(2,1)}, bf16[4,112,768]{2,1,0:T(8,128)(2,1)}, f32[44...) custom-call(f32[1,768]{1,0:T(1,128)} %refs_0_.9, ...), custom_call_target="tpu_custom_call" | custom-call | tf_op jit(solution)/shard_map/turning/pallas_call | solution.py:196
  273.2 0.0 copy-done
  273.2 2.7 broadcast_select_fusion.refs_0_
  275.9 99.1 %middle.1 = (bf16[16,64,768]{2,1,0:T(8,128)(2,1)}, bf16[16,64,768]{2,1,0:T(8,128)(2,1)}, bf16[16,64,768]{2,1,0:T(8,128)(2,1)}, bf16[4,112,768]{2,1,0:T(8,128)(2,...) custom-call(f32[1,768]{1,0:T(1,128)} %refs_0_.9, f32[1,768]{1,0:T(1,128)} %refs_1_.9, ...), custom_call_target="tpu_custom_call" | custom-call | tf_op jit(solution)/shard_map/middle/pallas_call | solution.py:196
  375.1 108.5 %ending.1 = (bf16[16,64,768]{2,1,0:T(8,128)(2,1)}, bf16[16,64,768]{2,1,0:T(8,128)(2,1)}, bf16[16,64,768]{2,1,0:T(8,128)(2,1)}, bf16[4,112,768]{2,1,0:T(8,128)(2,...) custom-call(f32[1,768]{1,0:T(1,128)} %refs_0_.9, ...), custom_call_target="tpu_custom_call" | custom-call | tf_op jit(solution)/shard_map/ending/pallas_call | solution.py:196
  483.6 11.6 %expert_grads.1 = (f32[2,768,768]{2,1,0:T(8,128)}, f32[2,768,768]{2,1,0:T(8,128)}) custom-call(s32[1]{0:T(128)} %bitcast.24.stage, bf16[16,64,768]{2,1,0:T(8,128)(2,1)} %broadcast_select_fusion.refs_0_, bf16[16,64,768]{2,1,0:T(8,128)(2,1)} %get-tuple-element.100.refs_1_, bf16[16,64,768]{2,1,0:T(8,128)(2,1)} %get-tuple-element.101.refs_2_, ...), custom_call_target="tpu_custom_call" | custom-call | tf_op jit(solution)/shard_map/expert_grads/pallas_call | solution.py:603
  495.1 5.7 %finish.1 = (bf16[2,394,768]{2,1,0:T(8,128)(2,1)}, bf16[2,394,768]{2,1,0:T(8,128)(2,1)}, f32[576,768]{1,0:T(8,128)}, f32[192,768]{1,0:T(8,128)}, f32[32,768]{1,0:T(8,128)}, /*index=5*/f32[8,768]{1,0:T(8,128)}) custom-call(s32[1,1]{1,0:T(1,128)} %bitcast.stage, bf16[4,224,384]{2,1,0:T(8,128)(2,1)} %get-tuple-element.60.refs_5_.refs_0_, ...), custom_call_target="tpu_custom_call" | custom-call | tf_op jit(solution)/shard_map/finish/pallas_call | solution.py:1070
  500.9 0.0 copy-start.1
  500.9 3.3 copy.27
  504.2 0.0 copy-done.1
  504.2 2.0 copy.28
  506.2 1.4 fusion
Async XLA Ops:
  0.6 4.2 copy-start.2
  173.5 99.7 %copy-start = (bf16[16,64,768]{2,1,0:T(8,128)(2,1)S(1)}, bf16[16,64,768]{2,1,0:T(8,128)(2,1)}, u32[]{:S(2)}) copy-start(bf16[16,64,768]{2,1,0:T(8,128)(2,1)} %get-tuple-element.80.refs_14_) | copy-start | bytes 4718596
  500.9 3.3 copy-start.1

commit v4 on v3

--- a/solution.py
+++ b/solution.py
@@ -107,6 +107,11 @@
     return {prefix + name: item for name, item in items.items()}
 
 
+def chain(*makers):
+    for maker in makers:
+        yield from maker()
+
+
 class Frame:
     def __init__(self, barrier, count):
         self.barrier = barrier
@@ -247,7 +252,7 @@
         a_part=pltpu.VMEM((NT, CH, D), BF),
         a_held=pltpu.VMEM((NT, CH, D), BF),
         a_mine=pltpu.VMEM((CH, D), BF),
-        a_pairs=sems(4, NT),
+        a_pairs=sems(8, NT),
         d_hot=pltpu.VMEM((NR, EXPERTS * SL), BF),
         d_match=pltpu.VMEM((2, NR, EXPERTS), F32),
     )
@@ -281,22 +286,30 @@
     part[...] = dot(ctx[...], f.output[...]).astype(BF).reshape(NT, CH, D)
     f.meet()
     me = lax.axis_index(TENSOR)
-    copies = [
-        send(
-            part.at[(me + step) % NT], held.at[me], pairs.at[0, step], pairs.at[1, step],
-            TENSOR, (me + step) % NT,
-        )
-        for step in range(1, NT)
+    scattered = [
+        [
+            send(
+                part.at[(me + step) % NT, pl.ds(start, size)], held.at[me, pl.ds(start, size)],
+                pairs.at[4 * i, step], pairs.at[4 * i + 1, step], TENSOR, (me + step) % NT,
+            )
+            for step in range(1, NT)
+        ]
+        for i, (start, size) in enumerate(RS_ROWS)
     ]
     f.flush(f.state, f.qkv, f.ctx)
     yield
-    for copy in copies:
-        copy.wait()
-    total = part[me].astype(F32)
-    for step in range(1, NT):
-        total = total + held[(me + step) % NT].astype(F32)
-    mine[...] = total.astype(BF)
-    copies = spread_over_tensor(mine, lambda me: summed.at[me], pairs, 2)
+    copies = []
+    for i, (start, size) in enumerate(RS_ROWS):
+        rows = pl.ds(start, size)
+        for copy in scattered[i]:
+            copy.wait()
+        total = part[me, rows].astype(F32)
+        for step in range(1, NT):
+            total = total + held[(me + step) % NT, rows].astype(F32)
+        mine[rows] = total.astype(BF)
+        copies += spread_over_tensor(
+            mine.at[rows], lambda me: summed.at[me, rows], pairs, 4 * i + 2
+        )
     summed[me] = mine[...]
     yield
     for copy in copies:
@@ -468,52 +481,75 @@
 
 
 def expert_steps(f, key, compute):
-    part, held, mine, sums, pairs = (key.part, key.held, key.mine, key.sums, key.pairs)
+    part, held, mine, passing, pairs = (key.part, key.held, key.mine, key.passing, key.pairs)
+    me = lax.axis_index(TENSOR)
+    home = lax.axis_index(DP)
+    group = home // 4
+    near = ((me + 1) % NT, (me + 3) % NT)
+    far = (me + 2) % NT
+    half = (pl.ds(0, 8), pl.ds(8, 8))
+
+    def begin(expert):
+        return [
+            send(
+                part.at[far, expert, half[way]], passing.at[way, expert],
+                key.pass_sems.at[0, way, expert], key.pass_sems.at[1, way, expert],
+                TENSOR, near[way],
+            )
+            for way in range(2)
+        ]
+
+    def add_passing(expert, copies):
+        for way in range(2):
+            copies[way].wait()
+            rows = (near[way], expert, half[way])
+            part[rows] = (part[rows].astype(F32) + passing[way, expert].astype(F32)).astype(BF)
+
     store_quarters(part, 0, compute(0))
     f.meet()
-    me = lax.axis_index(TENSOR)
-    home = lax.axis_index(DP)
+    one = begin(0)
+    yield
+    store_quarters(part, 1, compute(1))
+    two = begin(1)
+    add_passing(0, one)
     whole = [
         send(
-            part.at[(me + step) % NT, 0], held.at[me, 0], sums.at[0, 4, step], sums.at[1, 4, step],
-            TENSOR, (me + step) % NT,
-        )
-        for step in range(1, NT)
+            part.at[near[way], 0], held.at[way, 0], key.sums.at[0, 4, way],
+            key.sums.at[1, 4, way], TENSOR, near[way],
+        )
+        for way in range(2)
     ]
     yield
-    store_quarters(part, 1, compute(1))
-    group = home // 4
+    add_passing(1, two)
     scattered = []
     for turn in range(4):
         block = ((group + turn + 1) % 4) * 4
-        for step in range(1, NT):
-            peer = (me + step) % NT
+        for way in range(2):
             scattered.append(
                 send(
-                    part.at[peer, 1, pl.ds(block, 4)],
-                    held.at[me, 1, pl.ds(block, 4)],
-                    sums.at[0, turn, step],
-                    sums.at[1, turn, step],
+                    part.at[near[way], 1, pl.ds(block, 4)],
+                    held.at[way, 1, pl.ds(block, 4)],
+                    key.sums.at[0, turn, way],
+                    key.sums.at[1, turn, way],
                     TENSOR,
-                    peer,
+                    near[way],
                 )
             )
     yield
     for copy in whole:
         copy.wait()
-    total = part[me, 0].astype(F32)
-    for step in range(1, NT):
-        total = total + held[(me + step) % NT, 0].astype(F32)
+    total = part[me, 0].astype(F32) + held[0, 0].astype(F32) + held[1, 0].astype(F32)
     mine[:, 0] = total.astype(BF)
     returned = []
     for turn in range(4):
         block = ((group + turn + 1) % 4) * 4
-        for step in range(1, NT):
-            scattered[turn * 3 + step - 1].wait_recv()
-        total = part[me, 1, pl.ds(block, 4)].astype(F32)
-        for step in range(1, NT):
-            total = total + held[(me + step) % NT, 1, pl.ds(block, 4)].astype(F32)
-        mine[pl.ds(block, 4), 1] = total.astype(BF)
+        for way in range(2):
+            scattered[turn * 2 + way].wait_recv()
+        rows = pl.ds(block, 4)
+        total = part[me, 1, rows].astype(F32)
+        for way in range(2):
+            total = total + held[way, 1, rows].astype(F32)
+        mine[rows, 1] = total.astype(BF)
         for number in range(4):
             if turn == 3 and number == 0:
                 key.returned[home] = mine[home]
@@ -522,8 +558,8 @@
             peer = block + (home + number) % 4
             returned.append(
                 send(
-                    mine.at[peer], key.returned.at[home], pairs.at[0, offset], pairs.at[1, offset], DP,
-                    peer,
+                    mine.at[peer], key.returned.at[home], pairs.at[0, offset],
+                    pairs.at[1, offset], DP, peer,
                 )
             )
         yield
@@ -536,9 +572,11 @@
 def expert_scratch():
     return dict(
         part=pltpu.VMEM((NT, 2, NDP, 16, 2 * Q), BF),
-        held=pltpu.VMEM((NT, 2, NDP, 16, 2 * Q), BF),
+        held=pltpu.VMEM((2, 2, NDP, 16, 2 * Q), BF),
+        passing=pltpu.VMEM((2, 2, 8, 16, 2 * Q), BF),
+        pass_sems=sems(2, 2, 2),
         mine=pltpu.VMEM((NDP, 2, 16, 2 * Q), BF),
-        sums=sems(2, 5, NT),
+        sums=sems(2, 5, 2),
         pairs=sems(2, NDP),
         returned=pltpu.VMEM((NDP, 2, 16, 2 * Q), BF),
     )
@@ -1162,20 +1200,17 @@
         delta = padded(f.delta[0])
         f.delta_kept[...] = delta
         drive(
-            spread_steps(f, False, delta, f.meta_in),
-            attention_steps(f, state),
+            chain(
+                lambda: spread_steps(f, False, delta, f.meta_in),
+                lambda: experts_backward_steps(f, f.arrived_in),
+                lambda: collect_steps(f, f.meta_in, lambda k: f.pieces_in[k], f.delta_kept),
+                lambda: layer_steps(f, False, f.meta_in, f.delta_kept),
+            ),
+            chain(lambda: attention_steps(f, state), lambda: dispatch_steps(f, False)),
             places_steps(f, *place_of(f, 2)),
-        )
-        drive(
-            experts_backward_steps(f, f.arrived_in),
-            dispatch_steps(f, False),
             hot_steps(f.meta_in, f.h_hot),
             weights_steps(f),
         )
-        drive(
-            collect_steps(f, f.meta_in, lambda k: f.pieces_in[k], f.delta_kept)
-        )
-        drive(layer_steps(f, False, f.meta_in, f.delta_kept))
 
     two = launch(
         "turning", 3, all_axes,
@@ -1195,30 +1230,24 @@
         delta = jnp.where(early, f.arriving[...].reshape(NR, D), padded(f.delta[1]))
         f.delta_kept[...] = delta
         drive(
-            spread_steps(f, False, delta, f.meta_in),
-            experts_forward_steps(f, f.late_arrived),
-            hot_steps(f.late_meta, f.k_hot),
-        )
-
-        def combining():
-            yield
-            yield from combine_steps(f, False, f.late_meta, f.k_hot)
-
-        drive(
-            experts_backward_steps(f, f.arrived_in),
-            combining(),
-            hot_steps(f.meta_in, f.h_hot),
+            chain(
+                lambda: spread_steps(f, False, delta, f.meta_in),
+                lambda: experts_backward_steps(f, f.arrived_in),
+                lambda: collect_steps(
+                    f,
+                    f.meta_in,
+                    lambda k: jnp.where(early, f.pieces_in[k], f.pieces[k]),
+                    f.delta_kept,
+                ),
+                lambda: layer_steps(f, False, f.meta_in, f.delta_kept),
+            ),
+            chain(
+                lambda: experts_forward_steps(f, f.late_arrived),
+                lambda: combine_steps(f, False, f.late_meta, f.k_hot),
+            ),
+            chain(lambda: hot_steps(f.late_meta, f.k_hot), lambda: hot_steps(f.meta_in, f.h_hot)),
             weights_steps(f),
         )
-        drive(
-            collect_steps(
-                f,
-                f.meta_in,
-                lambda k: jnp.where(early, f.pieces_in[k], f.pieces[k]),
-                f.delta_kept,
-            )
-        )
-        drive(layer_steps(f, False, f.meta_in, f.delta_kept))
 
     three = launch(
         "middle", 4, all_axes,

time: 518 us -> 491 us (0.948)
  Pallas kernels: 492 us -> 466 us
    pallas_call x5, Pallas kernels: 475 us -> 449 us  [launch(): pl.pallas_call(kernel, in_specs=specs, out_specs=[ANYWHERE] * len(outs),...]
where the time goes in v4:
time: 491 us; the launch traced here: 482 us
  Pallas kernels  466 us (95%)
  local copies, waits for them, and re-layouts  12 us (2%)
    pallas_call x5, Pallas kernels, launch(): pl.pallas_call(kernel, in_specs=specs, out_specs=[ANYWHERE] * len(outs),...  449 us
    pallas_call x1, Pallas kernels, expert_grads(): pl.pallas_call(expert_grads_kernel, grid_spec=pltpu.PrefetchScalarGridSpe...  11.6 us
    unnamed x11, local copies, waits for them, and re-layouts  10.6 us

profile of v4, /device:TPU:7, one launch (start us, length us, event | category | flops | bytes accessed | tf_op | source)
XLA Modules:
  0.0 482.1 jit_solution(17227196385815421018)
XLA Ops:
  0.6 0.0 copy-start.2
  0.7 1.7 copy.20.refs_3_
  2.4 2.4 copy.21.refs_4_
  4.8 0.0 copy-done.2
  4.8 1.2 copy.26.refs_4_.refs_2_
  6.0 79.4 %forward_0.1 = (bf16[448,768]{1,0:T(8,128)(2,1)}, bf16[448,576]{1,0:T(8,128)(2,1)}, bf16[448,192]{1,0:T(8,128)(2,1)}, bf16[4,112,768]{2,1,0:T(8,128)(2,1)}, f32[...) custom-call(f32[1,768]{1,0:T(1,128)} %refs_0_.9, ...), custom_call_target="tpu_custom_call" | custom-call | tf_op jit(solution)/shard_map/forward_0/pallas_call | solution.py:201
  85.4 77.0 %forward_1.1 = (bf16[448,768]{1,0:T(8,128)(2,1)}, bf16[448,576]{1,0:T(8,128)(2,1)}, bf16[448,192]{1,0:T(8,128)(2,1)}, bf16[4,112,768]{2,1,0:T(8,128)(2,1)}, f32[...) custom-call(f32[1,768]{1,0:T(1,128)} %refs_0_.9, ...), custom_call_target="tpu_custom_call" | custom-call | tf_op jit(solution)/shard_map/forward_1/pallas_call | solution.py:201
  162.4 0.0 copy-start
  162.5 93.6 %turning.1 = (bf16[448,768]{1,0:T(8,128)(2,1)}, bf16[448,576]{1,0:T(8,128)(2,1)}, bf16[448,192]{1,0:T(8,128)(2,1)}, bf16[4,112,768]{2,1,0:T(8,128)(2,1)}, f32[44...) custom-call(f32[1,768]{1,0:T(1,128)} %refs_0_.9, ...), custom_call_target="tpu_custom_call" | custom-call | tf_op jit(solution)/shard_map/turning/pallas_call | solution.py:201
  256.1 0.0 copy-done
  256.1 2.7 broadcast_select_fusion.refs_0_
  258.8 91.2 %middle.1 = (bf16[16,64,768]{2,1,0:T(8,128)(2,1)}, bf16[16,64,768]{2,1,0:T(8,128)(2,1)}, bf16[16,64,768]{2,1,0:T(8,128)(2,1)}, bf16[4,112,768]{2,1,0:T(8,128)(2,...) custom-call(f32[1,768]{1,0:T(1,128)} %refs_0_.9, f32[1,768]{1,0:T(1,128)} %refs_1_.9, ...), custom_call_target="tpu_custom_call" | custom-call | tf_op jit(solution)/shard_map/middle/pallas_call | solution.py:201
  350.0 107.9 %ending.1 = (bf16[16,64,768]{2,1,0:T(8,128)(2,1)}, bf16[16,64,768]{2,1,0:T(8,128)(2,1)}, bf16[16,64,768]{2,1,0:T(8,128)(2,1)}, bf16[4,112,768]{2,1,0:T(8,128)(2,...) custom-call(f32[1,768]{1,0:T(1,128)} %refs_0_.9, ...), custom_call_target="tpu_custom_call" | custom-call | tf_op jit(solution)/shard_map/ending/pallas_call | solution.py:201
  457.9 11.6 %expert_grads.1 = (f32[2,768,768]{2,1,0:T(8,128)}, f32[2,768,768]{2,1,0:T(8,128)}) custom-call(s32[1]{0:T(128)} %bitcast.24.stage, bf16[16,64,768]{2,1,0:T(8,128)(2,1)} %broadcast_select_fusion.refs_0_, bf16[16,64,768]{2,1,0:T(8,128)(2,1)} %get-tuple-element.100.refs_1_, bf16[16,64,768]{2,1,0:T(8,128)(2,1)} %get-tuple-element.101.refs_2_, ...), custom_call_target="tpu_custom_call" | custom-call | tf_op jit(solution)/shard_map/expert_grads/pallas_call | solution.py:641
  469.5 5.7 %finish.1 = (bf16[2,394,768]{2,1,0:T(8,128)(2,1)}, bf16[2,394,768]{2,1,0:T(8,128)(2,1)}, f32[576,768]{1,0:T(8,128)}, f32[192,768]{1,0:T(8,128)}, f32[32,768]{1,0:T(8,128)}, /*index=5*/f32[8,768]{1,0:T(8,128)}) custom-call(s32[1,1]{1,0:T(1,128)} %bitcast.stage, bf16[4,224,384]{2,1,0:T(8,128)(2,1)} %get-tuple-element.60.refs_5_.refs_0_, ...), custom_call_target="tpu_custom_call" | custom-call | tf_op jit(solution)/shard_map/finish/pallas_call | solution.py:1108
  475.2 0.0 copy-start.1
  475.2 3.3 copy.27
  478.6 0.0 copy-done.1
  478.6 2.0 copy.28
  480.5 1.4 fusion
Async XLA Ops:
  0.6 4.2 copy-start.2
  162.4 93.6 %copy-start = (bf16[16,64,768]{2,1,0:T(8,128)(2,1)S(1)}, bf16[16,64,768]{2,1,0:T(8,128)(2,1)}, u32[]{:S(2)}) copy-start(bf16[16,64,768]{2,1,0:T(8,128)(2,1)} %get-tuple-element.80.refs_14_) | copy-start | bytes 4718596
  475.2 3.3 copy-start.1

commit v5 on v4

--- a/solution.py
+++ b/solution.py
@@ -1158,8 +1158,8 @@
                 early = lax.axis_index(PIPE) == 0
                 state = jnp.where(early, padded(f.tokens[1]), unpack(f.arriving))
             drive(attention_steps(f, state), places_steps(f, *place_of(f, moment)))
-            drive(dispatch_steps(f, True))
-            drive(experts_forward_steps(f, f.arrived), hot_steps(f.meta, f.h_hot))
+            drive(dispatch_steps(f, True), hot_steps(f.meta, f.h_hot))
+            drive(experts_forward_steps(f, f.arrived))
             drive(combine_steps(f, True, f.meta, f.h_hot))
 
         outs = dict(FORWARD_OUTS)
@@ -1268,16 +1268,16 @@
     def ending(f):
         delta = f.arriving[...].reshape(NR, D)
         f.delta_kept[...] = delta
-        drive(spread_steps(f, True, delta, f.meta_in))
         drive(
-            experts_backward_steps(f, f.arrived_in),
+            chain(
+                lambda: spread_steps(f, True, delta, f.meta_in),
+                lambda: experts_backward_steps(f, f.arrived_in),
+                lambda: collect_steps(f, f.meta_in, lambda k: f.pieces_in[k], f.delta_kept),
+                lambda: layer_steps(f, True, f.meta_in, f.delta_kept),
+            ),
             hot_steps(f.meta_in, f.h_hot),
             weights_steps(f),
         )
-        drive(
-            collect_steps(f, f.meta_in, lambda k: f.pieces_in[k], f.delta_kept)
-        )
-        drive(layer_steps(f, True, f.meta_in, f.delta_kept))
 
     wide = ((NT, R, 2 * Q), BF)
     four = launch(

time: 491 us -> 491 us (level)
  no operation moved by 1% of the time
where the time goes in v5:
time: 491 us; the launch traced here: 482 us
  Pallas kernels  466 us (95%)
  local copies, waits for them, and re-layouts  12 us (2%)
    pallas_call x5, Pallas kernels, launch(): pl.pallas_call(kernel, in_specs=specs, out_specs=[ANYWHERE] * len(outs),...  449 us
    pallas_call x1, Pallas kernels, expert_grads(): pl.pallas_call(expert_grads_kernel, grid_spec=pltpu.PrefetchScalarGridSpe...  11.6 us
    unnamed x11, local copies, waits for them, and re-layouts  10.6 us

profile of v5, /device:TPU:7, one launch (start us, length us, event | category | flops | bytes accessed | tf_op | source)
XLA Modules:
  0.0 481.8 jit_solution(5076234556200120030)
XLA Ops:
  0.6 0.0 copy-start.2
  0.7 1.7 copy.20.refs_3_
  2.4 2.4 copy.21.refs_4_
  4.8 0.0 copy-done.2
  4.8 1.2 copy.26.refs_4_.refs_2_
  6.0 79.4 %forward_0.1 = (bf16[448,768]{1,0:T(8,128)(2,1)}, bf16[448,576]{1,0:T(8,128)(2,1)}, bf16[448,192]{1,0:T(8,128)(2,1)}, bf16[4,112,768]{2,1,0:T(8,128)(2,1)}, f32[...) custom-call(f32[1,768]{1,0:T(1,128)} %refs_0_.9, ...), custom_call_target="tpu_custom_call" | custom-call | tf_op jit(solution)/shard_map/forward_0/pallas_call | solution.py:201
  85.4 76.7 %forward_1.1 = (bf16[448,768]{1,0:T(8,128)(2,1)}, bf16[448,576]{1,0:T(8,128)(2,1)}, bf16[448,192]{1,0:T(8,128)(2,1)}, bf16[4,112,768]{2,1,0:T(8,128)(2,1)}, f32[...) custom-call(f32[1,768]{1,0:T(1,128)} %refs_0_.9, ...), custom_call_target="tpu_custom_call" | custom-call | tf_op jit(solution)/shard_map/forward_1/pallas_call | solution.py:201
  162.1 0.0 copy-start
  162.1 96.4 %turning.1 = (bf16[448,768]{1,0:T(8,128)(2,1)}, bf16[448,576]{1,0:T(8,128)(2,1)}, bf16[448,192]{1,0:T(8,128)(2,1)}, bf16[4,112,768]{2,1,0:T(8,128)(2,1)}, f32[44...) custom-call(f32[1,768]{1,0:T(1,128)} %refs_0_.9, ...), custom_call_target="tpu_custom_call" | custom-call | tf_op jit(solution)/shard_map/turning/pallas_call | solution.py:201
  258.6 0.0 copy-done
  258.6 2.7 broadcast_select_fusion.refs_0_
  261.3 88.3 %middle.1 = (bf16[16,64,768]{2,1,0:T(8,128)(2,1)}, bf16[16,64,768]{2,1,0:T(8,128)(2,1)}, bf16[16,64,768]{2,1,0:T(8,128)(2,1)}, bf16[4,112,768]{2,1,0:T(8,128)(2,...) custom-call(f32[1,768]{1,0:T(1,128)} %refs_0_.9, f32[1,768]{1,0:T(1,128)} %refs_1_.9, ...), custom_call_target="tpu_custom_call" | custom-call | tf_op jit(solution)/shard_map/middle/pallas_call | solution.py:201
  349.7 107.9 %ending.1 = (bf16[16,64,768]{2,1,0:T(8,128)(2,1)}, bf16[16,64,768]{2,1,0:T(8,128)(2,1)}, bf16[16,64,768]{2,1,0:T(8,128)(2,1)}, bf16[4,112,768]{2,1,0:T(8,128)(2,...) custom-call(f32[1,768]{1,0:T(1,128)} %refs_0_.9, ...), custom_call_target="tpu_custom_call" | custom-call | tf_op jit(solution)/shard_map/ending/pallas_call | solution.py:201
  457.6 11.6 %expert_grads.1 = (f32[2,768,768]{2,1,0:T(8,128)}, f32[2,768,768]{2,1,0:T(8,128)}) custom-call(s32[1]{0:T(128)} %bitcast.24.stage, bf16[16,64,768]{2,1,0:T(8,128)(2,1)} %broadcast_select_fusion.refs_0_, bf16[16,64,768]{2,1,0:T(8,128)(2,1)} %get-tuple-element.100.refs_1_, bf16[16,64,768]{2,1,0:T(8,128)(2,1)} %get-tuple-element.101.refs_2_, ...), custom_call_target="tpu_custom_call" | custom-call | tf_op jit(solution)/shard_map/expert_grads/pallas_call | solution.py:641
  469.2 5.7 %finish.1 = (bf16[2,394,768]{2,1,0:T(8,128)(2,1)}, bf16[2,394,768]{2,1,0:T(8,128)(2,1)}, f32[576,768]{1,0:T(8,128)}, f32[192,768]{1,0:T(8,128)}, f32[32,768]{1,0:T(8,128)}, /*index=5*/f32[8,768]{1,0:T(8,128)}) custom-call(s32[1,1]{1,0:T(1,128)} %bitcast.stage, bf16[4,224,384]{2,1,0:T(8,128)(2,1)} %get-tuple-element.60.refs_5_.refs_0_, ...), custom_call_target="tpu_custom_call" | custom-call | tf_op jit(solution)/shard_map/finish/pallas_call | solution.py:1108
  474.9 0.0 copy-start.1
  474.9 3.3 copy.27
  478.2 0.0 copy-done.1
  478.2 2.0 copy.28
  480.2 1.4 fusion
Async XLA Ops:
  0.6 4.2 copy-start.2
  162.1 96.5 %copy-start = (bf16[16,64,768]{2,1,0:T(8,128)(2,1)S(1)}, bf16[16,64,768]{2,1,0:T(8,128)(2,1)}, u32[]{:S(2)}) copy-start(bf16[16,64,768]{2,1,0:T(8,128)(2,1)} %get-tuple-element.80.refs_14_) | copy-start | bytes 4718596
  474.9 3.3 copy-start.1
